TPU v7x, 32 devices: a whole 2x2x4 slice. The times are simulated.
32 devices in a mesh: groups: 2 (over y), row: 8 (over z, x), col: 2 (over core).
Axes of the slice: x: 2, y: 2, z: 4, core: 2. Of those that a mesh axis runs over, the one named last changes fastest.
Arguments:
- effects: float32 [16384, 512], P(('groups', 'row', 'col')), parts along dimension 0, may hold values from -6 to 6
- zscores: float32 [16384, 512], P(('groups', 'row', 'col')), parts along dimension 0, may hold values from -6 to 6
- ridge: float32 [1024], P('groups'), parts along dimension 0, may hold values from 0.1 to 1
- band_tiles: bfloat16 [128, 9, 128, 128], P(('groups', 'row', 'col')), parts along dimension 0, may hold values from -0.1875 to 0.1875
- lr_tiles: bfloat16 [256, 128, 128], P(('groups', 'row', 'col')), parts along dimension 0, may hold values from -0.0625 to 0.0625
- lr_local: int32 [256], P(('groups', 'row', 'col')), parts along dimension 0, may hold values from 0 to 3
- lr_hub: int32 [256], P(('groups', 'row', 'col')), parts along dimension 0, may hold values from 0 to 3
- hub_blocks: int32 [8], P('groups'), parts along dimension 0, may hold values from 0 to 63, as said below
Outputs:
- fitted: float32 [16384, 512], P(('groups', 'row', 'col')), parts along dimension 0
There are 2 independent parts, one for each index of `groups`. A program takes and returns all parts, laid end to end along the dimension named above; each array names one. Nothing has to cross between parts.
Inputs may be any that keep to these rules, and one draw needn't show every extreme that they name: `hub_blocks`: the 4 entries are distinct block numbers.
All inputs are finite; a program needn't handle non-finite values.
Results may differ from a plain program's by a relative error of at most 0.0017.
Values may be sent and summed in bfloat16 or wider, within the bound.
No kernel may reach another device: no remote copies, remote signals or barrier semaphores. Data moves between devices by JAX's collectives and lax.ppermute only.
A program may use at most 64 MiB of HBM per device.

v0:
```python
import jax
import jax.numpy as jnp
from jax import lax
from jax.sharding import PartitionSpec as P

ITERS = 2


step_size = 0.5


def spread(block, axis, owner):
    block = jnp.where(lax.axis_index(axis) == owner, block, jnp.zeros_like(block))
    return lax.psum(block, axis)


def extended(x, sides, width):
    for axis, dim in sides:
        size, length = (lax.axis_size(axis), x.shape[dim])
        up = [(i, (i + 1) % size) for i in range(size - 1)]
        down = [(j, i) for i, j in up]
        last = lax.slice_in_dim(x, length - width, length, axis=dim)
        leading = lax.slice_in_dim(x, 0, width, axis=dim)
        before = lax.ppermute(last, axis, up)
        after = lax.ppermute(leading, axis, down)
        x = jnp.concatenate([before, x, after], axis=dim)
    return x


def fetch_rows(values_flat, hub_blocks, blk_dev, tile_rows):
    pieces = []
    for hub_index in range(hub_blocks.shape[0]):
        block_id = hub_blocks[hub_index]
        local_rows = lax.dynamic_slice_in_dim(
            values_flat, block_id % blk_dev * tile_rows, tile_rows, 0
        )
        pieces.append(
            spread(local_rows.astype(jnp.bfloat16), ("row", "col"), block_id // blk_dev).astype(
                local_rows.dtype
            )
        )
    return jnp.stack(pieces)


def local_gradient(
    current,
    zscores,
    ridge,
    band_tiles,
    lr_tiles,
    panels_flat,
    hub_panel,
    row_pick,
    hub_pick,
    blk_dev,
    tile_rows,
    width,
):
    traits = current.shape[1]
    padded = extended(panels_flat, ((("row", "col"), 0),), width * tile_rows)
    padded = padded.reshape(blk_dev + 2 * width, tile_rows, traits)
    gradient = jnp.zeros((blk_dev, tile_rows, traits), jnp.float32)
    for offset in range(2 * width + 1):
        gradient = gradient + jnp.einsum(
            "bij,bjt->bit",
            band_tiles[:, offset],
            padded[offset : offset + blk_dev],
            preferred_element_type=jnp.float32,
        )
    far_panels = jnp.einsum(
        "sh,hjt->sjt", hub_pick.astype(jnp.bfloat16), hub_panel, preferred_element_type=jnp.float32
    ).astype(jnp.bfloat16)
    far_terms = jnp.einsum("sij,sjt->sit", lr_tiles, far_panels, preferred_element_type=jnp.float32)
    gradient = gradient + jnp.einsum(
        "sk,sit->kit", row_pick.astype(jnp.float32), far_terms, precision=lax.Precision.HIGHEST
    )
    own_blocks = panels_flat.reshape(blk_dev, tile_rows, traits)
    near_panels = jnp.einsum(
        "sk,kjt->sjt", row_pick.astype(jnp.bfloat16), own_blocks, preferred_element_type=jnp.float32
    ).astype(jnp.bfloat16)
    back_terms = jnp.einsum(
        "sji,sjt->sit", lr_tiles, near_panels, preferred_element_type=jnp.float32
    )
    hub_terms = jnp.einsum(
        "sh,sit->hit", hub_pick.astype(jnp.float32), back_terms, precision=lax.Precision.HIGHEST
    )
    penalty = ridge[None, :] * current - zscores
    gradient = gradient + penalty.reshape(blk_dev, tile_rows, traits)
    return (gradient, hub_terms)


def shards(effects, zscores, ridge, band_tiles, lr_tiles, lr_local, lr_hub, hub_blocks):
    tile_rows = band_tiles.shape[2]
    width = (band_tiles.shape[1] - 1) // 2
    blk_dev = effects.shape[0] // tile_rows
    traits = effects.shape[1]
    hub_count = hub_blocks.shape[0]
    my_index = lax.axis_index(("row", "col"))
    row_pick = lr_local[:, None] == jnp.arange(blk_dev, dtype=jnp.int32)[None, :]
    hub_pick = lr_hub[:, None] == jnp.arange(hub_count, dtype=jnp.int32)[None, :]
    owned = hub_blocks // blk_dev == my_index
    owned_pick = (
        owned[:, None]
        & ((hub_blocks % blk_dev)[:, None] == jnp.arange(blk_dev, dtype=jnp.int32)[None, :])
    ).astype(jnp.float32)
    current = effects
    hub_state = fetch_rows(effects, hub_blocks, blk_dev, tile_rows)
    for sweep in range(ITERS):
        panels_flat = current.astype(jnp.bfloat16)
        hub_panel = hub_state.astype(jnp.bfloat16)
        gradient, hub_terms = local_gradient(
            current,
            zscores,
            ridge,
            band_tiles,
            lr_tiles,
            panels_flat,
            hub_panel,
            row_pick,
            hub_pick,
            blk_dev,
            tile_rows,
            width,
        )
        own_rows = jnp.einsum("hk,kit->hit", owned_pick, gradient, precision=lax.Precision.HIGHEST)
        summed, own_sum = lax.psum((hub_terms, own_rows), ("row", "col"))
        hub_state = hub_state - step_size * (own_sum + summed)
        gradient = gradient + jnp.einsum(
            "hk,hit->kit", owned_pick, summed, precision=lax.Precision.HIGHEST
        )
        current = current - step_size * gradient.reshape(blk_dev * tile_rows, traits)
    return current


def solution(mesh):
    placed = (
        P(("groups", "row", "col"), None),
        P(("groups", "row", "col"), None),
        P("groups"),
        P(("groups", "row", "col"), None, None, None),
        P(("groups", "row", "col"), None, None),
        P(("groups", "row", "col")),
        P(("groups", "row", "col")),
        P("groups"),
    )
    return jax.shard_map(
        shards,
        mesh=mesh,
        in_specs=placed,
        out_specs=P(("groups", "row", "col"), None),
        check_vma=False,
    )
```

profile of v0, /device:TPU:0, one launch (start us, length us, event | category | flops | bytes accessed | tf_op | source)
XLA Modules:
  0.0 364.0 jit_solution(1271820320804093802)
XLA Ops:
  6.5 3.2 fusion.116
  9.8 3.3 collective-permute-start
  13.1 1.3 collective-permute-start.1
  14.4 0.7 fusion.117
  25.3 0.9 fusion.54
  26.2 0.0 all-reduce.6.cloned.1.call-start
  26.2 0.6 fusion.43
  26.8 2.0 fusion.24
  28.8 3.1 copy.29
  31.9 2.7 fusion.2
  34.6 1.3 copy.19
  36.0 0.2 all-reduce.8.cloned.1.call-start
  36.2 1.2 fusion.67
  37.5 83.3 %all-reduce.10.cloned.1.call-done = (bf16[1,128,512]{2,1,0:T(8,128)(2,1)}, bf16[1,128,512]{2,1,0:T(8,128)(2,1)}, bf16[1,128,512]{2,1,0:T(8,128)(2,1)}, bf16[1,128,512]{2,1,0:T(8,128)(2,1)}) async-done(((bf16[1,128,512]{2,1,0:T(8,128)(2,1)}, bf16[1,128,512]{2,1,0:T(8,128)(2,1)}, bf16[1,128,512]{2,1,0:T(8,128)(2,1)}, bf16[1,128,512]{2,1,0:T(8,128)(2,1)}), (bf16[1,128,512]{2,1,0:T(8,128)(2,1)}, ...) | async-done | bytes 524304 | tf_op jit(solution)/shard_map/psum | solution.py:14
  120.8 0.9 constant_dynamic-update-slice_fusion.3
  121.7 0.9 constant_dynamic-update-slice_fusion.2
  122.6 0.9 constant_dynamic-update-slice_fusion.1
  123.5 0.9 constant_dynamic-update-slice_fusion
  124.4 0.6 fusion.45
  125.0 2.0 fusion.23
  127.0 3.1 copy.26
  130.2 3.7 %fusion.4 = f32[4,128,512]{2,0,1:T(4,128)} fusion(f32[8,512,128]{1,0,2:T(8,128)} %copy.26, s32[8]{0:T(128)S(1)} %copy-done.18), kind=kOutput, calls=%fused_computation.4 | convolution fusion | flops 25165856 | bytes 3145760 | tf_op jit(solution)/shard_map/sk,sit->kit/dot_general | solution.py:74
  133.9 2.5 pad_maximum_fusion.2
  136.4 0.3 convolution_bitcast_fusion.4
  136.7 0.3 convolution_bitcast_fusion.5
  136.9 0.3 convolution_bitcast_fusion.6
  137.2 0.9 copy-done.9
  138.2 1.4 fusion.22
  139.6 0.3 fusion.19
  139.8 2.3 fusion.57
  142.2 1.3 fusion.18
  143.4 74.4 %all-reduce.6.cloned.1.call-done = f32[4,128,512]{2,1,0:T(8,128)} async-done(((f32[4,128,512]{2,1,0:T(8,128)}), f32[4,128,512]{2,1,0:T(8,128)}) %all-reduce.6.cloned.1.call-update) | async-done | bytes 1048592 | tf_op jit(solution)/shard_map/psum | solution.py:126
  217.8 3.0 fusion.29
  220.9 3.7 %fusion.28 = (f32[4,128,512]{2,1,0:T(8,128)S(1)}, f32[4,128,512]{2,1,0:T(8,128)}) fusion(f32[4,128,512]{2,0,1:T(4,128)S(1)} %fusion.29, f32[4,128,512]{2,1,0:T(8,128)S(1)} %bitcast.197, f32[4,128,512]{2,0,1:T(4,128)S(1)} %copy-done.6, f32[4,128,512]{2,1,0:T(8,128)} %fusion.57, f32[4,128,512]{2,1,0:T(8,128)} %fusion.18, ...), kind=kOutput, calls=%fused_computation.64 | convolution fusion | flops 68681728 | bytes 7995392 | tf_op jit(solution)/shard_map/bij,bjt->bit/dot_general | solution.py:64
  224.6 1.4 fusion.115
  226.0 2.1 collective-permute-start.2
  228.2 1.3 collective-permute-start.3
  229.4 0.6 fusion.39
  230.0 2.0 convolution_bitcast_fusion
  232.0 3.1 copy.37
  235.2 3.1 fusion.26
  238.3 1.3 copy.31
  239.6 0.6 copy-done.2
  240.2 2.0 fusion.102
  242.3 1.2 fusion.65
  243.5 2.6 pad_maximum_fusion
  246.1 0.3 fusion.72
  246.4 0.3 fusion.75
  246.7 1.3 fusion.13
  248.0 2.3 fusion.55
  250.3 0.3 fusion.12
  250.6 0.3 convolution_add_fusion.2
  250.9 1.4 convolution_add_fusion.1
  252.2 90.4 %all-reduce.8.cloned.1.call-done = (f32[4,128,512]{2,0,1:T(4,128)}, f32[4,128,512]{2,1,0:T(8,128)}) async-done(((f32[4,128,512]{2,0,1:T(4,128)}, f32[4,128,512]{2,1,0:T(8,128)}), (f32[4,128,512]{2,0,1:T(4,128)}, f32[4,128,512]{2,1,0:T(8,128)})) %all-reduce.8.cloned.1.call-update) | async-done | bytes 2097168 | tf_op jit(solution)/shard_map/psum | solution.py:126
  342.6 1.8 subtract_convert_fusion
  344.4 0.6 fusion.41
  345.0 2.0 fusion.25
  347.0 3.1 copy.34
  350.1 2.8 fusion
  353.0 1.1 fusion.111
  354.1 0.1 copy-done.8
  354.1 0.3 copy-done.10
  354.5 1.7 fusion.11
  356.2 1.3 bitcast_subtract_fusion
  (44 shorter events, 0.2 us)
Async XLA Ops:
  6.5 20.3 %copy-start = (bf16[8,128,128]{2,1,0:T(8,128)(2,1)S(1)}, bf16[8,128,128]{2,1,0:T(8,128)(2,1)}, u32[]{:S(2)}) copy-start(bf16[8,128,128]{2,1,0:T(8,128)(2,1)} %param.12) | copy-start | bytes 786436
  6.5 18.7 %copy-start.1 = (f32[512,512]{1,0:T(8,128)S(1)}, f32[512,512]{1,0:T(8,128)}, u32[]{:S(2)}) copy-start(f32[512,512]{1,0:T(8,128)} %param.8) | copy-start | bytes 3145732
  6.5 7.9 %copy-start.16 = (s32[4]{0:T(128)S(1)}, s32[4]{0:T(128)}, u32[]{:S(2)}) copy-start(s32[4]{0:T(128)} %param.15) | copy-start | bytes 52
  6.5 114.2 %all-reduce.10.cloned.1.call-start = ((), (), s32[]{:S(2)}) async-start(), calls=%async_computation.2 | async-start | bytes 1048576 | tf_op jit(solution)/shard_map/psum | solution.py:14
  9.8 16.4 %copy-start.18 = (s32[8]{0:T(128)S(1)}, s32[8]{0:T(128)}, u32[]{:S(2)}) copy-start(s32[8]{0:T(128)} %param.13) | copy-start | bytes 100
  9.8 124.1 %collective-permute-start = (bf16[512,512]{1,0:T(8,128)(2,1)S(1)}, bf16[512,512]{1,0:T(8,128)(2,1)}, u32[]{:S(2)}, u32[]{:S(2)}) collective-permute-start(bf16[512,512]{1,0:T(8,128)(2,1)S(1)} %get-tuple-element.29), channel_id=1, source_target_pairs={{0,1},{1,2},{2,3},{3,4},{4,5},{5,6},{6,7},{7,8},{8,9},{9,10},{10,1... | collective-permute-start | bytes 1572872 | tf_op jit(solution)/shard_map/ppermute | solution.py:24
  13.1 120.7 %collective-permute-start.1 = (bf16[512,512]{1,0:T(8,128)(2,1)S(1)}, bf16[512,512]{1,0:T(8,128)(2,1)}, u32[]{:S(2)}, u32[]{:S(2)}) collective-permute-start(bf16[512,512]{1,0:T(8,128)(2,1)S(1)} %get-tuple-element.29), channel_id=1, source_target_pairs={{1,0},{2,1},{3,2},{4,3},{5,4},{6,5},{7,6},{8,7},{9,8},{10,9},{11,1... | collective-permute-start | bytes 1572872 | tf_op jit(solution)/shard_map/ppermute | solution.py:25
  26.2 191.7 %all-reduce.6.cloned.1.call-start = ((), (), s32[]{:S(2)}) async-start(), calls=%async_computation | async-start | bytes 2097152 | tf_op jit(solution)/shard_map/psum | solution.py:126
  28.8 3.1 copy-start.17
  34.6 1.6 copy-start.3
  36.0 306.6 %all-reduce.8.cloned.1.call-start = ((), (), s32[]{:S(2)}) async-start(), calls=%async_computation.1 | async-start | bytes 4194304 | tf_op jit(solution)/shard_map/psum | solution.py:126
  136.9 1.2 copy-start.9
  142.2 78.7 %copy-start.13 = (bf16[512,512]{1,0:T(8,128)(2,1)S(1)}, bf16[512,512]{1,0:T(8,128)(2,1)}, u32[]{:S(2)}) copy-start(bf16[512,512]{1,0:T(8,128)(2,1)} %get-tuple-element.23) | copy-start | bytes 1572868
  217.8 3.1 copy-start.5
  217.8 3.1 copy-start.6
  220.9 3.7 %copy-start.7 = (f32[512,512]{1,0:T(8,128)S(1)}, f32[512,512]{1,0:T(8,128)}, u32[]{:S(2)}) copy-start(f32[512,512]{1,0:T(8,128)} %param.9) | copy-start | bytes 3145732
  220.9 3.7 %copy-start.15 = (f32[512]{0:T(512)S(1)}, f32[512]{0:T(512)}, u32[]{:S(2)}) copy-start(f32[512]{0:T(512)} %param.10) | copy-start | bytes 6148
  226.0 17.5 %collective-permute-start.2 = (bf16[512,512]{1,0:T(8,128)(2,1)S(1)}, bf16[512,512]{1,0:T(8,128)(2,1)}, u32[]{:S(2)}, u32[]{:S(2)}) collective-permute-start(bf16[512,512]{1,0:T(8,128)(2,1)S(1)} %get-tuple-element.11), channel_id=1, source_target_pairs={{0,1},{1,2},{2,3},{3,4},{4,5},{5,6},{6,7},{7,8},{8,9},{9,10},{10,1... | collective-permute-start | bytes 1572872 | tf_op jit(solution)/shard_map/ppermute | solution.py:24
  228.2 15.3 %collective-permute-start.3 = (bf16[512,512]{1,0:T(8,128)(2,1)S(1)}, bf16[512,512]{1,0:T(8,128)(2,1)}, u32[]{:S(2)}, u32[]{:S(2)}) collective-permute-start(bf16[512,512]{1,0:T(8,128)(2,1)S(1)} %get-tuple-element.11), channel_id=1, source_target_pairs={{1,0},{2,1},{3,2},{4,3},{5,4},{6,5},{7,6},{8,7},{9,8},{10,9},{11,1... | collective-permute-start | bytes 1572872 | tf_op jit(solution)/shard_map/ppermute | solution.py:25
  238.2 2.0 copy-start.2
  243.5 2.6 copy-start.4
  350.1 2.9 copy-start.14
  350.1 4.0 %copy-start.11 = (f32[512,512]{1,0:T(8,128)S(1)}, f32[512,512]{1,0:T(8,128)}, u32[]{:S(2)}) copy-start(f32[512,512]{1,0:T(8,128)} %get-tuple-element.12) | copy-start | bytes 3145732
  350.1 4.0 %copy-start.12 = (bf16[512,512]{1,0:T(8,128)(2,1)S(1)}, bf16[512,512]{1,0:T(8,128)(2,1)}, u32[]{:S(2)}) copy-start(bf16[512,512]{1,0:T(8,128)(2,1)} %get-tuple-element.13) | copy-start | bytes 1572868
  352.9 1.2 copy-start.8
  352.9 1.5 copy-start.10
Sparse Core Ops, SparseCore 0:
  26.3 94.4 all-reduce.9
  124.2 93.5 all-reduce.5
  242.4 100.1 all-reduce.7
where the time goes:
time: 365 us; the launch traced here: 364 us
  waiting for transfers between devices  248 us (68%)
  matrix products  48.7 us (13%)
  between operations  23.6 us (6%)
  local copies, waits for them, and re-layouts  21.5 us (6%)
  other arithmetic  13.8 us (4%)
  starting transfers between devices  8.3 us (2%)
    psum x2, waiting for transfers between devices, shards(): summed, own_sum = lax.psum((hub_terms, own_rows), ('row', 'col'))  165 us
    psum x1, waiting for transfers between devices, spread(): return lax.psum(block, axis)  83.3 us
    dot_general x18, matrix products, local_gradient(): jnp.einsum('bij,bjt->bit', band_tiles[:, offset], padded[offset:offset +...  20 us
  transfers between devices with their start and end apart: 7, of which 3 were waited for; matrix products, arithmetic and copies ran while one was open for 15% of the time, Pallas kernels for 0%

commit v1 on v0

v1 whole, which is shorter than its diff:
```python
import functools

import jax
import jax.numpy as jnp
from jax import lax
from jax.experimental import pallas as pl
from jax.experimental.pallas import tpu as pltpu
from jax.sharding import PartitionSpec as P

ITERS = 2
STEP = 0.5
F32 = jnp.float32
BF16 = jnp.bfloat16
VMEM = pl.BlockSpec(memory_space=pltpu.VMEM)
SMEM = pl.BlockSpec(memory_space=pltpu.SMEM)


def dot(a, b):
    return jnp.dot(a, b, preferred_element_type=F32)


def dot_t(a, b):
    return lax.dot_general(a, b, (((0,), (0,)), ((), ())), preferred_element_type=F32)


class Place:
    def __init__(self, block, blocks, cores):
        self.chip = block // (blocks * cores)
        self.core = (block // blocks) % cores
        self.blk = block % blocks


def back_terms(local_ref, hub_ref, lr_ref, panel_ref, acc_ref, out_ref):
    tile = lr_ref.shape[1]
    acc_ref[...] = jnp.zeros_like(acc_ref)
    for s in range(lr_ref.shape[0]):
        rows = pl.ds(pl.multiple_of(local_ref[s] * tile, tile), tile)
        hub = pl.ds(pl.multiple_of(hub_ref[s] * tile, tile), tile)
        acc_ref[hub, :] += dot_t(lr_ref[s], panel_ref[rows, :])
    out_ref[...] = acc_ref[...].astype(BF16)


def first_kernel(local_ref, hub_ref, effects_ref, lr_ref, panel_ref, back_ref, acc_ref):
    panel_ref[...] = effects_ref[...].astype(BF16)
    back_terms(local_ref, hub_ref, lr_ref, panel_ref, acc_ref, back_ref)


def pick_kernel(cores, tile, blocks_ref, mine_ref, other_ref, back_ref, back_other_ref, out_ref):
    me, core = lax.axis_index("row"), lax.axis_index("col")
    blocks = mine_ref.shape[0] // tile
    count = out_ref.shape[0] // tile
    for j in range(count):
        hub = core * count + j
        place = Place(blocks_ref[hub], blocks, cores)
        out = pl.ds(j * tile, tile)
        src = pl.ds(pl.multiple_of(place.blk * tile, tile), tile)
        row = pl.ds(pl.multiple_of(hub * tile, tile), tile)
        here = place.chip == me

        @pl.when(here & (place.core == core))
        def _():
            out_ref[out, :] = mine_ref[src, :]

        @pl.when(here & (place.core != core))
        def _():
            out_ref[out, :] = other_ref[src, :]

        @pl.when(jnp.logical_not(here))
        def _():
            both = back_ref[row, :].astype(F32) + back_other_ref[row, :].astype(F32)
            out_ref[out, :] = both.astype(BF16)


def merge_kernel(cores, tile, per_chip, blocks_ref, in_ref, out_ref):
    me, core = lax.axis_index("row"), lax.axis_index("col")
    chips, rows, _ = in_ref.shape
    hub = (core * (chips * rows) + me * rows) // tile
    owner = blocks_ref[hub] // per_chip

    def add(p, total):
        return total + jnp.where(p == owner, 0.0, in_ref[p].astype(F32))

    def put(p, carry):
        out_ref[p] = jnp.where(p == owner, total, state)
        return carry

    zero = jnp.zeros(in_ref.shape[1:], F32)
    total = lax.fori_loop(0, chips, add, zero, unroll=chips <= 16).astype(BF16)
    state = in_ref[owner]
    lax.fori_loop(0, chips, put, 0, unroll=chips <= 16)


def step_kernel(
    cores,
    last,
    blocks_ref,
    local_ref,
    hub_ref,
    current_ref,
    zscores_ref,
    ridge_ref,
    band_ref,
    lr_ref,
    mine_ref,
    other_ref,
    outer_ref,
    half_ref,
    half_other_ref,
    back_ref,
    back_other_ref,
    *rest,
):
    if last:
        next_ref, window_ref, state_ref, grad_ref = rest
    else:
        next_ref, panel_ref, back_out_ref, window_ref, state_ref, grad_ref, acc_ref = rest
    me, core = lax.axis_index("row"), lax.axis_index("col")
    blocks, width, tile, _ = band_ref.shape
    rows = blocks * tile
    hubs = blocks_ref.shape[0]
    per_half = hubs // cores
    reach = (width - 1) // 2 * tile

    window_ref[reach : reach + rows, :] = mine_ref[...]

    @pl.when(core == 0)
    def _():
        window_ref[:reach, :] = outer_ref[rows - reach :, :]
        window_ref[reach + rows :, :] = other_ref[:reach, :]

    @pl.when(core != 0)
    def _():
        window_ref[:reach, :] = other_ref[rows - reach :, :]
        window_ref[reach + rows :, :] = outer_ref[:reach, :]

    for b in range(blocks):
        tiles = jnp.concatenate([band_ref[b, o] for o in range(width)], axis=1)
        grad_ref[b * tile : (b + 1) * tile, :] = dot(
            tiles, window_ref[b * tile : (b + width) * tile, :]
        )

    for hub in range(hubs):
        place = Place(blocks_ref[hub], blocks, cores)
        here = place.chip == me
        near = core == hub // per_half
        src = pl.ds(hub % per_half * tile, tile)
        dst = pl.ds(hub * tile, tile)
        own = pl.ds(pl.multiple_of(place.blk * tile, tile), tile)

        @pl.when(jnp.logical_not(here))
        def _():
            state_ref[dst, :] = jnp.where(near, half_ref[src, :], half_other_ref[src, :])

        @pl.when(here & (place.core != core))
        def _():
            state_ref[dst, :] = other_ref[own, :]

        @pl.when(here & (place.core == core))
        def _():
            state_ref[dst, :] = mine_ref[own, :]
            far = jnp.where(near, half_ref[src, :], half_other_ref[src, :])
            grad_ref[own, :] += (
                far.astype(F32) + back_ref[dst, :].astype(F32) + back_other_ref[dst, :].astype(F32)
            )

    for s in range(lr_ref.shape[0]):
        row = pl.ds(pl.multiple_of(local_ref[s] * tile, tile), tile)
        col = pl.ds(pl.multiple_of(hub_ref[s] * tile, tile), tile)
        grad_ref[row, :] += dot(lr_ref[s], state_ref[col, :])

    current = current_ref[...]
    gradient = grad_ref[...] + (ridge_ref[...] * current - zscores_ref[...])
    following = current - STEP * gradient
    next_ref[...] = following
    if not last:
        panel_ref[...] = following.astype(BF16)
        back_terms(local_ref, hub_ref, lr_ref, panel_ref, acc_ref, back_out_ref)


def shards(rows_dev, cores, effects, zscores, ridge, band, lr, lr_local, lr_hub, hub_blocks):
    blocks, _, tile, _ = band.shape
    rows, traits = effects.shape
    hubs = hub_blocks.shape[0]
    hub_rows = hubs * tile
    half = hub_rows // cores
    total = rows_dev * cores
    params = pltpu.CompilerParams(vmem_limit_bytes=48 * 1024 * 1024)
    panel_type = jax.ShapeDtypeStruct((rows, traits), BF16)
    back_type = jax.ShapeDtypeStruct((hub_rows, traits), BF16)
    ridge = ridge[None, :]

    odd = [(i, i + 1) for i in range(cores - 1, total - 1, cores)]
    odd = odd + [(j, i) for i, j in odd]
    swap = [(0, 1), (1, 0)]

    def other_core(x):
        return lax.ppermute(x, "col", swap)

    def exchange(x):
        x = x.reshape(rows_dev, half // rows_dev, traits)
        return lax.all_to_all(x, "row", 0, 0)

    panels, back = pl.pallas_call(
        first_kernel,
        out_shape=(panel_type, back_type),
        in_specs=[SMEM, SMEM, VMEM, VMEM],
        out_specs=(VMEM, VMEM),
        scratch_shapes=[pltpu.VMEM((hub_rows, traits), F32)],
        compiler_params=params,
        name="first",
    )(lr_local, lr_hub, effects, lr)

    current = effects
    for sweep in range(ITERS):
        last = sweep == ITERS - 1
        other = other_core(panels)
        back_other = other_core(back)
        outer = lax.ppermute(panels, ("row", "col"), odd)
        chosen = pl.pallas_call(
            functools.partial(pick_kernel, cores, tile),
            out_shape=jax.ShapeDtypeStruct((half, traits), BF16),
            in_specs=[SMEM, VMEM, VMEM, VMEM, VMEM],
            out_specs=VMEM,
            compiler_params=params,
            name="pick",
        )(hub_blocks, panels, other, back, back_other)
        gathered = exchange(chosen)
        merged = pl.pallas_call(
            functools.partial(merge_kernel, cores, tile, blocks * cores),
            out_shape=jax.ShapeDtypeStruct(gathered.shape, BF16),
            in_specs=[SMEM, VMEM],
            out_specs=VMEM,
            compiler_params=params,
            name="merge",
        )(hub_blocks, gathered)
        mine = exchange(merged).reshape(half, traits)
        theirs = other_core(mine)
        out_shape = [jax.ShapeDtypeStruct((rows, traits), F32)]
        scratch = [
            pltpu.VMEM((rows + 2 * ((band.shape[1] - 1) // 2) * tile, traits), BF16),
            pltpu.VMEM((hub_rows, traits), BF16),
            pltpu.VMEM((rows, traits), F32),
        ]
        if not last:
            out_shape += [panel_type, back_type]
            scratch += [pltpu.VMEM((hub_rows, traits), F32)]
        result = pl.pallas_call(
            functools.partial(step_kernel, cores, last),
            out_shape=tuple(out_shape),
            in_specs=[SMEM] * 3 + [VMEM] * 12,
            out_specs=(VMEM,) * len(out_shape),
            scratch_shapes=scratch,
            compiler_params=params,
            name="step",
        )(
            hub_blocks,
            lr_local,
            lr_hub,
            current,
            zscores,
            ridge,
            band,
            lr,
            panels,
            other,
            outer,
            mine,
            theirs,
            back,
            back_other,
        )
        if last:
            return result[0]
        current, panels, back = result


def solution(mesh):
    every = ("groups", "row", "col")
    placed = (
        P(every, None),
        P(every, None),
        P("groups"),
        P(every, None, None, None),
        P(every, None, None),
        P(every),
        P(every),
        P("groups"),
    )
    return jax.shard_map(
        functools.partial(shards, mesh.shape["row"], mesh.shape["col"]),
        mesh=mesh,
        in_specs=placed,
        out_specs=P(every, None),
        check_vma=False,
    )
```

time: 365 us -> 98.8 us (0.27)
  the two profiles are of different devices: /device:TPU:0 before, /device:TPU:13 now
where the time goes in v1:
time: 98.8 us; the launch traced here: 98.1 us
  starting transfers between devices  30.3 us (31%)
  waiting for transfers between devices  22.3 us (23%)
  blocking collectives  22.3 us (23%)
  Pallas kernels  13.1 us (13%)
  local copies, waits for them, and re-layouts  9.9 us (10%)
    all_to_all x2, blocking collectives, exchange(): return lax.all_to_all(x, 'row', 0, 0)  22.3 us
    ppermute x2, waiting for transfers between devices, shards(): outer = lax.ppermute(panels, ('row', 'col'), odd)  16.3 us
    all_to_all x2, starting transfers between devices, exchange(): return lax.all_to_all(x, 'row', 0, 0)  11.3 us
    unnamed x34, local copies, waits for them, and re-layouts  9.9 us
    ppermute x6, starting transfers between devices, other_core(): return lax.ppermute(x, 'col', swap)  9.54 us
    ppermute x2, starting transfers between devices, shards(): outer = lax.ppermute(panels, ('row', 'col'), odd)  9.45 us
    pallas_call x2, Pallas kernels, shards(): pl.pallas_call(functools.partial(step_kernel, cores, last), out_shape=tup...  8.66 us
    ppermute x6, waiting for transfers between devices, other_core(): return lax.ppermute(x, 'col', swap)  4.36 us
  transfers between devices with their start and end apart: 10, of which 8 were waited for; matrix products, arithmetic and copies ran while one was open for 0% of the time, Pallas kernels for 0%

profile of v1, /device:TPU:13, one launch (start us, length us, event | category | flops | bytes accessed | tf_op | source)
XLA Modules:
  0.0 98.1 jit_solution(14531641424756309009)
XLA Ops:
  0.0 0.0 copy-start.1
  0.0 1.2 %copy-done.1 = f32[512,512]{1,0:T(8,128)S(1)} copy-done((f32[512,512]{1,0:T(8,128)S(1)}, f32[512,512]{1,0:T(8,128)}, u32[]{:S(2)}) %copy-start.1) | copy-done | bytes 1048600
  1.2 0.0 copy-start.2
  1.2 0.9 copy-done.2
  2.2 0.0 copy-start.13
  2.2 0.7 copy-done.13
  2.8 0.0 copy-start.15
  2.8 0.7 copy-done.15
  3.5 0.0 copy-start.11
  3.5 1.1 %first.1 = (bf16[512,512]{1,0:T(8,128)(2,1)S(1)}, bf16[512,512]{1,0:T(8,128)(2,1)S(1)}) custom-call(s32[8]{0:T(128)S(1)} %copy-done.13, s32[8]{0:T(128)S(1)} %copy-done.15, f32[512,512]{1,0:T(8,128)S(1)} %copy-done.1, bf16[8,128,128]{2,1,0:T(8,128)(2,1)S(1)} %copy-done.2), custom_call_target="tpu_custom_call" | custom-call | tf_op jit(solution)/shard_map/first/pallas_call | solution.py:203
  4.6 0.7 collective-permute-start.2
  5.3 0.1 collective-permute-start
  5.4 1.5 %collective-permute-done.2.back_other_ref = bf16[512,512]{1,0:T(8,128)(2,1)S(1)} collective-permute-done((bf16[512,512]{1,0:T(8,128)(2,1)S(1)}, bf16[512,512]{1,0:T(8,128)(2,1)S(1)}, u32[]{:S(2)}, u32[]{:S(2)}) %collective-permute-start.2) | collective-permute-done | bytes 524320 | tf_op jit(solution)/shard_map/ppermute | solution.py:197
  6.9 0.7 collective-permute-done.other_ref
  7.6 0.0 copy-done.11
  7.6 0.7 pick.2
  8.3 0.0 copy-start.3
  8.3 0.0 copy-start.12
  8.3 0.0 copy-start.14
  8.3 0.0 copy-start.16
  8.3 12.1 %all_to_all.20.in_ref = bf16[8,32,512]{2,1,0:T(8,128)(2,1)S(1)} all-to-all(bf16[8,32,512]{2,1,0:T(8,128)(2,1)S(1)} %bitcast.7), channel_id=1, replica_groups=mesh['groups'=2,'row'=8,'col'=2] {'row'}, dimensions={0} | all-to-all | bytes 524288 | tf_op jit(solution)/shard_map/all_to_all | solution.py:201
  20.5 1.3 %merge.2 = bf16[8,32,512]{2,1,0:T(8,128)(2,1)} custom-call(s32[4]{0:T(128)S(1)} %copy-done.11, bf16[8,32,512]{2,1,0:T(8,128)(2,1)S(1)} %all_to_all.20.in_ref), custom_call_target="tpu_custom_call" | custom-call | tf_op jit(solution)/shard_map/merge/pallas_call | solution.py:228
  21.8 5.7 %all-to-all-start.1 = ((bf16[8,32,512]{2,1,0:T(8,128)(2,1)}), bf16[8,32,512]{2,1,0:T(8,128)(2,1)S(1)}, u32[]{:S(2)}, u32[]{:S(2)}) async-start(bf16[8,32,512]{2,1,0:T(8,128)(2,1)} %merge.2), calls=%async_computation.1 | async-start | bytes 524288 | tf_op jit(solution)/shard_map/all_to_all | solution.py:201
  27.5 4.5 %collective-permute-start.1 = (bf16[512,512]{1,0:T(8,128)(2,1)S(1)}, bf16[512,512]{1,0:T(8,128)(2,1)S(1)}, u32[]{:S(2)}, u32[]{:S(2)}) collective-permute-start(bf16[512,512]{1,0:T(8,128)(2,1)S(1)} %get-tuple-element.10.mine_ref), channel_id=1, source_target_pairs={{1,2},{3,4},{5,6},{7,8},{9,10},{11,12},{13,14},{2,1},{4,3},{6,5},{... | collective-permute-start | bytes 1572872 | tf_op jit(solution)/shard_map/ppermute | solution.py:218
  32.0 1.1 %all-to-all-done.1 = bf16[8,32,512]{2,1,0:T(8,128)(2,1)S(1)} async-done(((bf16[8,32,512]{2,1,0:T(8,128)(2,1)}), bf16[8,32,512]{2,1,0:T(8,128)(2,1)S(1)}, u32[]{:S(2)}, u32[]{:S(2)}) %all-to-all-start.1) | async-done | bytes 262176 | tf_op jit(solution)/shard_map/all_to_all | solution.py:201
  33.1 4.0 %collective-permute-start.3 = (bf16[256,512]{1,0:T(8,128)(2,1)S(1)}, bf16[256,512]{1,0:T(8,128)(2,1)S(1)}, u32[]{:S(2)}, u32[]{:S(2)}) collective-permute-start(bf16[256,512]{1,0:T(8,128)(2,1)S(1)} %bitcast.5), channel_id=1, source_target_pairs={{0,1},{1,0},{2,3},{3,2},{4,5},{5,4},{6,7},{7,6},{8,9},{9,8},{10,11... | collective-permute-start | bytes 786440 | tf_op jit(solution)/shard_map/ppermute | solution.py:197
  37.1 0.0 copy-start.6
  37.1 0.7 copy-done.6
  37.8 7.8 %collective-permute-done.1.outer_ref = bf16[512,512]{1,0:T(8,128)(2,1)S(1)} collective-permute-done((bf16[512,512]{1,0:T(8,128)(2,1)S(1)}, bf16[512,512]{1,0:T(8,128)(2,1)S(1)}, u32[]{:S(2)}, u32[]{:S(2)}) %collective-permute-start.1) | collective-permute-done | bytes 524320 | tf_op jit(solution)/shard_map/ppermute | solution.py:218
  45.5 0.0 copy-start.9
  45.5 0.8 copy-done.9
  46.3 0.0 collective-permute-done.3.half_other_ref
  46.3 0.0 copy-done.3
  46.3 0.0 copy-done.12
  46.3 0.0 copy-done.14
  46.3 0.0 copy-done.16
  46.4 0.0 copy-start.7
  46.4 0.9 copy-done.7
  47.3 0.0 copy-start.10
  47.3 1.0 %copy-done.10 = bf16[512,512]{1,0:T(8,128)(2,1)S(1)} copy-done((bf16[512,512]{1,0:T(8,128)(2,1)S(1)}, bf16[512,512]{1,0:T(8,128)(2,1)}, u32[]{:S(2)}) %copy-start.10) | copy-done | bytes 524312
  48.4 4.3 %step.2 = (f32[512,512]{1,0:T(8,128)S(1)}, bf16[512,512]{1,0:T(8,128)(2,1)S(1)}, bf16[512,512]{1,0:T(8,128)(2,1)S(1)}) custom-call(s32[4]{0:T(128)S(1)} %copy-done.11, s32[8]{0:T(128)S(1)} %copy-done.14, s32[8]{0:T(128)S(1)} %copy-done.16, f32[512,512]{1,0:T(8,128)} %current_ref.1, f32[512,512]{1,0:T(8,128)} %zscores_ref.3, f32[1,512]{1,0:T(1,128)S(1)} %bitcast.9, ...), custom_call_target="tpu_custom_call" | custom-call | tf_op jit(solution)/shard_map/step/pallas_call | solution.py:247
  52.7 0.0 copy-start.4
  52.7 1.0 copy-done.4
  53.7 0.0 collective-permute-start.6
  53.7 0.5 collective-permute-start.4
  54.2 1.4 %collective-permute-done.6.back_other_ref = bf16[512,512]{1,0:T(8,128)(2,1)S(1)} collective-permute-done((bf16[512,512]{1,0:T(8,128)(2,1)S(1)}, bf16[512,512]{1,0:T(8,128)(2,1)S(1)}, u32[]{:S(2)}, u32[]{:S(2)}) %collective-permute-start.6) | collective-permute-done | bytes 524320 | tf_op jit(solution)/shard_map/ppermute | solution.py:197
  55.6 0.7 collective-permute-done.4.other_ref
  56.3 0.7 pick.3
  57.0 0.0 copy-start
  57.0 10.2 %all_to_all.21.in_ref = bf16[8,32,512]{2,1,0:T(8,128)(2,1)S(1)} all-to-all(bf16[8,32,512]{2,1,0:T(8,128)(2,1)S(1)} %bitcast.8), channel_id=1, replica_groups=mesh['groups'=2,'row'=8,'col'=2] {'row'}, dimensions={0} | all-to-all | bytes 524288 | tf_op jit(solution)/shard_map/all_to_all | solution.py:201
  67.2 0.6 merge.3
  67.9 0.0 copy-start.8
  67.9 0.7 copy-done.8
  68.6 5.7 %all-to-all-start.3 = ((bf16[8,32,512]{2,1,0:T(8,128)(2,1)}), bf16[8,32,512]{2,1,0:T(8,128)(2,1)}, u32[]{:S(2)}, u32[]{:S(2)}) async-start(bf16[8,32,512]{2,1,0:T(8,128)(2,1)} %copy-done.8), calls=%async_computation.3 | async-start | bytes 524288 | tf_op jit(solution)/shard_map/all_to_all | solution.py:201
  74.3 4.9 %collective-permute-start.5 = (bf16[512,512]{1,0:T(8,128)(2,1)S(1)}, bf16[512,512]{1,0:T(8,128)(2,1)}, u32[]{:S(2)}, u32[]{:S(2)}) collective-permute-start(bf16[512,512]{1,0:T(8,128)(2,1)S(1)} %get-tuple-element.13.mine_ref), channel_id=1, source_target_pairs={{1,2},{3,4},{5,6},{7,8},{9,10},{11,12},{13,14},{2,1},{4,3},{6,5},{... | collective-permute-start | bytes 1572872 | tf_op jit(solution)/shard_map/ppermute | solution.py:218
  79.2 0.5 all-to-all-done.3
  79.7 4.2 %collective-permute-start.7 = (bf16[256,512]{1,0:T(8,128)(2,1)}, bf16[256,512]{1,0:T(8,128)(2,1)S(1)}, u32[]{:S(2)}, u32[]{:S(2)}) collective-permute-start(bf16[256,512]{1,0:T(8,128)(2,1)} %bitcast.4.half_ref), channel_id=1, source_target_pairs={{0,1},{1,0},{2,3},{3,2},{4,5},{5,4},{6,7},{7,6},{8,9},{9,8},{10,11... | collective-permute-start | bytes 786440 | tf_op jit(solution)/shard_map/ppermute | solution.py:197
  84.0 8.5 %collective-permute-done.5.outer_ref = bf16[512,512]{1,0:T(8,128)(2,1)} collective-permute-done((bf16[512,512]{1,0:T(8,128)(2,1)S(1)}, bf16[512,512]{1,0:T(8,128)(2,1)}, u32[]{:S(2)}, u32[]{:S(2)}) %collective-permute-start.5) | collective-permute-done | bytes 524320 | tf_op jit(solution)/shard_map/ppermute | solution.py:218
  92.5 0.0 collective-permute-done.7.half_other_ref
  92.5 0.0 copy-done
  92.5 0.0 copy-start.5
  92.5 1.2 %copy-done.5 = f32[512,512]{1,0:T(8,128)S(1)} copy-done((f32[512,512]{1,0:T(8,128)S(1)}, f32[512,512]{1,0:T(8,128)}, u32[]{:S(2)}) %copy-start.5) | copy-done | bytes 1048600
  93.7 4.3 %step.3 = f32[512,512]{1,0:T(8,128)} custom-call(s32[4]{0:T(128)S(1)} %copy-done.11, s32[8]{0:T(128)S(1)} %copy-done.14, s32[8]{0:T(128)S(1)} %copy-done.16, f32[512,512]{1,0:T(8,128)S(1)} %copy-done.5, f32[512,512]{1,0:T(8,128)S(1)} %copy-done, f32[1,512]{1,0:T(1,128)S(1)} %bitcast.10, bf16[4,9,128,128]{3,2,1,0:T(8,128)(2,1)} %band_ref.3, ...), custom_call_target="tpu_custom_call" | custom-call | tf_op jit(solution)/shard_map/step/pallas_call | solution.py:247
Async XLA Ops:
  0.0 1.2 %copy-start.1 = (f32[512,512]{1,0:T(8,128)S(1)}, f32[512,512]{1,0:T(8,128)}, u32[]{:S(2)}) copy-start(f32[512,512]{1,0:T(8,128)} %current_ref.1) | copy-start | bytes 3145732
  1.2 0.9 copy-start.2
  2.2 0.7 copy-start.13
  2.8 0.7 copy-start.15
  3.5 4.1 %copy-start.11 = (s32[4]{0:T(128)S(1)}, s32[4]{0:T(128)}, u32[]{:S(2)}) copy-start(s32[4]{0:T(128)} %blocks_ref.11) | copy-start | bytes 52
  4.6 2.3 %collective-permute-start.2 = (bf16[512,512]{1,0:T(8,128)(2,1)S(1)}, bf16[512,512]{1,0:T(8,128)(2,1)S(1)}, u32[]{:S(2)}, u32[]{:S(2)}) collective-permute-start(bf16[512,512]{1,0:T(8,128)(2,1)S(1)} %get-tuple-element.11.back_ref), channel_id=1, source_target_pairs={{0,1},{1,0},{2,3},{3,2},{4,5},{5,4},{6,7},{7,6},{8,9},{9,8},{10,11... | collective-permute-start | bytes 1572872 | tf_op jit(solution)/shard_map/ppermute | solution.py:197
  5.3 2.3 %collective-permute-start = (bf16[512,512]{1,0:T(8,128)(2,1)S(1)}, bf16[512,512]{1,0:T(8,128)(2,1)S(1)}, u32[]{:S(2)}, u32[]{:S(2)}) collective-permute-start(bf16[512,512]{1,0:T(8,128)(2,1)S(1)} %get-tuple-element.10.mine_ref), channel_id=1, source_target_pairs={{0,1},{1,0},{2,3},{3,2},{4,5},{5,4},{6,7},{7,6},{8,9},{9,8},{10,11... | collective-permute-start | bytes 1572872 | tf_op jit(solution)/shard_map/ppermute | solution.py:197
  8.3 38.0 %copy-start.3 = (bf16[8,128,128]{2,1,0:T(8,128)(2,1)S(1)}, bf16[8,128,128]{2,1,0:T(8,128)(2,1)}, u32[]{:S(2)}) copy-start(bf16[8,128,128]{2,1,0:T(8,128)(2,1)} %lr_ref.5) | copy-start | bytes 786436
  8.3 38.0 %copy-start.12 = (f32[512]{0:T(512)S(1)}, f32[512]{0:T(512)}, u32[]{:S(2)}) copy-start(f32[512]{0:T(512)} %param.10) | copy-start | bytes 6148
  8.3 38.0 %copy-start.14 = (s32[8]{0:T(128)S(1)}, s32[8]{0:T(128)}, u32[]{:S(2)}) copy-start(s32[8]{0:T(128)} %local_ref.5) | copy-start | bytes 100
  8.3 38.0 %copy-start.16 = (s32[8]{0:T(128)S(1)}, s32[8]{0:T(128)}, u32[]{:S(2)}) copy-start(s32[8]{0:T(128)} %hub_ref.5) | copy-start | bytes 100
  21.8 11.3 %all-to-all-start.1 = ((bf16[8,32,512]{2,1,0:T(8,128)(2,1)}), bf16[8,32,512]{2,1,0:T(8,128)(2,1)S(1)}, u32[]{:S(2)}, u32[]{:S(2)}) async-start(bf16[8,32,512]{2,1,0:T(8,128)(2,1)} %merge.2), calls=%async_computation.1 | async-start | bytes 524288 | tf_op jit(solution)/shard_map/all_to_all | solution.py:201
  27.5 18.1 %collective-permute-start.1 = (bf16[512,512]{1,0:T(8,128)(2,1)S(1)}, bf16[512,512]{1,0:T(8,128)(2,1)S(1)}, u32[]{:S(2)}, u32[]{:S(2)}) collective-permute-start(bf16[512,512]{1,0:T(8,128)(2,1)S(1)} %get-tuple-element.10.mine_ref), channel_id=1, source_target_pairs={{1,2},{3,4},{5,6},{7,8},{9,10},{11,12},{13,14},{2,1},{4,3},{6,5},{... | collective-permute-start | bytes 1572872 | tf_op jit(solution)/shard_map/ppermute | solution.py:218
  33.1 13.3 %collective-permute-start.3 = (bf16[256,512]{1,0:T(8,128)(2,1)S(1)}, bf16[256,512]{1,0:T(8,128)(2,1)S(1)}, u32[]{:S(2)}, u32[]{:S(2)}) collective-permute-start(bf16[256,512]{1,0:T(8,128)(2,1)S(1)} %bitcast.5), channel_id=1, source_target_pairs={{0,1},{1,0},{2,3},{3,2},{4,5},{5,4},{6,7},{7,6},{8,9},{9,8},{10,11... | collective-permute-start | bytes 786440 | tf_op jit(solution)/shard_map/ppermute | solution.py:197
  37.1 0.7 copy-start.6
  45.5 0.8 copy-start.9
  46.4 1.0 copy-start.7
  47.3 1.0 %copy-start.10 = (bf16[512,512]{1,0:T(8,128)(2,1)S(1)}, bf16[512,512]{1,0:T(8,128)(2,1)}, u32[]{:S(2)}) copy-start(bf16[512,512]{1,0:T(8,128)(2,1)} %copy-done.9) | copy-start | bytes 1572868
  52.7 1.0 copy-start.4
  53.7 1.9 %collective-permute-start.6 = (bf16[512,512]{1,0:T(8,128)(2,1)S(1)}, bf16[512,512]{1,0:T(8,128)(2,1)S(1)}, u32[]{:S(2)}, u32[]{:S(2)}) collective-permute-start(bf16[512,512]{1,0:T(8,128)(2,1)S(1)} %get-tuple-element.14.back_ref), channel_id=1, source_target_pairs={{0,1},{1,0},{2,3},{3,2},{4,5},{5,4},{6,7},{7,6},{8,9},{9,8},{10,11... | collective-permute-start | bytes 1572872 | tf_op jit(solution)/shard_map/ppermute | solution.py:197
  53.7 2.7 %collective-permute-start.4 = (bf16[512,512]{1,0:T(8,128)(2,1)S(1)}, bf16[512,512]{1,0:T(8,128)(2,1)S(1)}, u32[]{:S(2)}, u32[]{:S(2)}) collective-permute-start(bf16[512,512]{1,0:T(8,128)(2,1)S(1)} %get-tuple-element.13.mine_ref), channel_id=1, source_target_pairs={{0,1},{1,0},{2,3},{3,2},{4,5},{5,4},{6,7},{7,6},{8,9},{9,8},{10,11... | collective-permute-start | bytes 1572872 | tf_op jit(solution)/shard_map/ppermute | solution.py:197
  57.0 35.5 %copy-start = (f32[512,512]{1,0:T(8,128)S(1)}, f32[512,512]{1,0:T(8,128)}, u32[]{:S(2)}) copy-start(f32[512,512]{1,0:T(8,128)} %zscores_ref.3) | copy-start | bytes 3145732
  67.9 0.7 copy-start.8
  68.6 11.1 %all-to-all-start.3 = ((bf16[8,32,512]{2,1,0:T(8,128)(2,1)}), bf16[8,32,512]{2,1,0:T(8,128)(2,1)}, u32[]{:S(2)}, u32[]{:S(2)}) async-start(bf16[8,32,512]{2,1,0:T(8,128)(2,1)} %copy-done.8), calls=%async_computation.3 | async-start | bytes 524288 | tf_op jit(solution)/shard_map/all_to_all | solution.py:201
  74.3 18.2 %collective-permute-start.5 = (bf16[512,512]{1,0:T(8,128)(2,1)S(1)}, bf16[512,512]{1,0:T(8,128)(2,1)}, u32[]{:S(2)}, u32[]{:S(2)}) collective-permute-start(bf16[512,512]{1,0:T(8,128)(2,1)S(1)} %get-tuple-element.13.mine_ref), channel_id=1, source_target_pairs={{1,2},{3,4},{5,6},{7,8},{9,10},{11,12},{13,14},{2,1},{4,3},{6,5},{... | collective-permute-start | bytes 1572872 | tf_op jit(solution)/shard_map/ppermute | solution.py:218
  79.7 12.8 %collective-permute-start.7 = (bf16[256,512]{1,0:T(8,128)(2,1)}, bf16[256,512]{1,0:T(8,128)(2,1)S(1)}, u32[]{:S(2)}, u32[]{:S(2)}) collective-permute-start(bf16[256,512]{1,0:T(8,128)(2,1)} %bitcast.4.half_ref), channel_id=1, source_target_pairs={{0,1},{1,0},{2,3},{3,2},{4,5},{5,4},{6,7},{7,6},{8,9},{9,8},{10,11... | collective-permute-start | bytes 786440 | tf_op jit(solution)/shard_map/ppermute | solution.py:197
  92.5 1.2 %copy-start.5 = (f32[512,512]{1,0:T(8,128)S(1)}, f32[512,512]{1,0:T(8,128)}, u32[]{:S(2)}) copy-start(f32[512,512]{1,0:T(8,128)} %copy-done.4) | copy-start | bytes 3145732

commit v2 on v1

--- a/solution.py
+++ b/solution.py
@@ -11,7 +11,11 @@
 STEP = 0.5
 F32 = jnp.float32
 BF16 = jnp.bfloat16
+WIDE = pltpu.CompilerParams(vmem_limit_bytes=58 * 2**20)
+NARROW = pltpu.CompilerParams(vmem_limit_bytes=12 * 2**20)
 VMEM = pl.BlockSpec(memory_space=pltpu.VMEM)
+HBM = pl.BlockSpec(memory_space=pltpu.HBM)
+ANY = pl.BlockSpec(memory_space=pl.ANY)
 SMEM = pl.BlockSpec(memory_space=pltpu.SMEM)
 
 
@@ -40,7 +44,18 @@
     out_ref[...] = acc_ref[...].astype(BF16)
 
 
-def first_kernel(local_ref, hub_ref, effects_ref, lr_ref, panel_ref, back_ref, acc_ref):
+def fetch(pairs, sems):
+    copies = [pltpu.make_async_copy(a, b, sems.at[n]) for n, (a, b) in enumerate(pairs)]
+    for copy in copies:
+        copy.start()
+    return copies
+
+
+def first_kernel(*refs):
+    sources, (panel_ref, back_ref, acc_ref), held, sems = refs[:4], refs[4:7], refs[7:11], refs[11]
+    for copy in fetch(list(zip(sources, held)), sems):
+        copy.wait()
+    local_ref, hub_ref, effects_ref, lr_ref = held
     panel_ref[...] = effects_ref[...].astype(BF16)
     back_terms(local_ref, hub_ref, lr_ref, panel_ref, acc_ref, back_ref)
 
@@ -71,7 +86,8 @@
             out_ref[out, :] = both.astype(BF16)
 
 
-def merge_kernel(cores, tile, per_chip, blocks_ref, in_ref, out_ref):
+def merge_kernel(cores, tile, per_chip, blocks_ref, in_ref, outer_ref, out_ref):
+    del outer_ref
     me, core = lax.axis_index("row"), lax.axis_index("col")
     chips, rows, _ = in_ref.shape
     hub = (core * (chips * rows) + me * rows) // tile
@@ -88,6 +104,97 @@
     total = lax.fori_loop(0, chips, add, zero, unroll=chips <= 16).astype(BF16)
     state = in_ref[owner]
     lax.fori_loop(0, chips, put, 0, unroll=chips <= 16)
+
+
+def band_kernel(
+    cores,
+    blocks_ref,
+    current_hbm,
+    zscores_hbm,
+    ridge_hbm,
+    band_hbm,
+    mine_hbm,
+    other_hbm,
+    outer_hbm,
+    back_hbm,
+    back_other_hbm,
+    next_ref,
+    state_ref,
+    window_ref,
+    current_ref,
+    zscores_ref,
+    ridge_ref,
+    band_ref,
+    back_ref,
+    back_other_ref,
+    sems,
+):
+    me, core = lax.axis_index("row"), lax.axis_index("col")
+    blocks, width, tile, _ = band_ref.shape
+    rows = blocks * tile
+    reach = (width - 1) // 2 * tile
+    first, middle, last = pl.ds(0, reach), pl.ds(reach, rows), pl.ds(reach + rows, reach)
+    head, tail = pl.ds(0, reach), pl.ds(rows - reach, reach)
+
+    copies = fetch(
+        [
+            (mine_hbm, window_ref.at[middle]),
+            (band_hbm, band_ref),
+            (current_hbm, current_ref),
+            (zscores_hbm, zscores_ref),
+            (ridge_hbm, ridge_ref),
+            (back_hbm, back_ref),
+            (back_other_hbm, back_other_ref),
+        ],
+        sems,
+    )
+    before, after = sems.at[len(copies)], sems.at[len(copies) + 1]
+
+    @pl.when(core == 0)
+    def _():
+        pltpu.make_async_copy(outer_hbm.at[tail], window_ref.at[first], before).start()
+        pltpu.make_async_copy(other_hbm.at[head], window_ref.at[last], after).start()
+
+    @pl.when(core != 0)
+    def _():
+        pltpu.make_async_copy(other_hbm.at[tail], window_ref.at[first], before).start()
+        pltpu.make_async_copy(outer_hbm.at[head], window_ref.at[last], after).start()
+
+    for copy in copies:
+        copy.wait()
+    pltpu.make_async_copy(other_hbm.at[tail], window_ref.at[first], before).wait()
+    pltpu.make_async_copy(other_hbm.at[head], window_ref.at[last], after).wait()
+
+    for b in range(blocks):
+        out = slice(b * tile, (b + 1) * tile)
+        tiles = jnp.concatenate([band_ref[b, o] for o in range(width)], axis=1)
+        gradient = dot(tiles, window_ref[b * tile : (b + width) * tile, :])
+        current = current_ref[out, :]
+        gradient += ridge_ref[...] * current - zscores_ref[out, :]
+        next_ref[out, :] = current - STEP * gradient
+
+    for hub in range(blocks_ref.shape[0]):
+        place = Place(blocks_ref[hub], blocks, cores)
+        here = place.chip == me
+        row = pl.ds(hub * tile, tile)
+        own = pl.ds(pl.multiple_of(place.blk * tile, tile), tile)
+        middle = pl.ds(pl.multiple_of(reach + place.blk * tile, tile), tile)
+        shift = jnp.where(core == 0, rows, -rows)
+        beside = pl.ds(pl.multiple_of(reach + place.blk * tile + shift, tile), tile)
+
+        @pl.when(here & (place.core == core))
+        def _():
+            state_ref[row, :] = window_ref[middle, :]
+            both = back_ref[row, :].astype(F32) + back_other_ref[row, :].astype(F32)
+            next_ref[own, :] -= STEP * both
+
+        @pl.when(here & (place.core != core))
+        def _():
+            state_ref[row, :] = window_ref[beside, :]
+
+        @pl.when(jnp.logical_not(here))
+        def _():
+            state_ref[row, :] = jnp.zeros_like(state_ref[row, :])
 
 
 def step_kernel(
@@ -96,48 +203,23 @@
     blocks_ref,
     local_ref,
     hub_ref,
-    current_ref,
-    zscores_ref,
-    ridge_ref,
-    band_ref,
+    partial_ref,
     lr_ref,
-    mine_ref,
-    other_ref,
-    outer_ref,
+    own_state_ref,
     half_ref,
     half_other_ref,
-    back_ref,
-    back_other_ref,
     *rest,
 ):
     if last:
-        next_ref, window_ref, state_ref, grad_ref = rest
+        next_ref, state_ref, grad_ref = rest
     else:
-        next_ref, panel_ref, back_out_ref, window_ref, state_ref, grad_ref, acc_ref = rest
+        next_ref, panel_ref, back_out_ref, state_ref, grad_ref, acc_ref = rest
     me, core = lax.axis_index("row"), lax.axis_index("col")
-    blocks, width, tile, _ = band_ref.shape
-    rows = blocks * tile
+    tile = lr_ref.shape[1]
+    blocks = next_ref.shape[0] // tile
     hubs = blocks_ref.shape[0]
     per_half = hubs // cores
-    reach = (width - 1) // 2 * tile
-
-    window_ref[reach : reach + rows, :] = mine_ref[...]
-
-    @pl.when(core == 0)
-    def _():
-        window_ref[:reach, :] = outer_ref[rows - reach :, :]
-        window_ref[reach + rows :, :] = other_ref[:reach, :]
-
-    @pl.when(core != 0)
-    def _():
-        window_ref[:reach, :] = other_ref[rows - reach :, :]
-        window_ref[reach + rows :, :] = outer_ref[:reach, :]
-
-    for b in range(blocks):
-        tiles = jnp.concatenate([band_ref[b, o] for o in range(width)], axis=1)
-        grad_ref[b * tile : (b + 1) * tile, :] = dot(
-            tiles, window_ref[b * tile : (b + width) * tile, :]
-        )
+    grad_ref[...] = jnp.zeros_like(grad_ref)
 
     for hub in range(hubs):
         place = Place(blocks_ref[hub], blocks, cores)
@@ -146,31 +228,26 @@
         src = pl.ds(hub % per_half * tile, tile)
         dst = pl.ds(hub * tile, tile)
         own = pl.ds(pl.multiple_of(place.blk * tile, tile), tile)
+        came = jnp.where(near, half_ref[src, :], half_other_ref[src, :])
+
+        @pl.when(here)
+        def _():
+            state_ref[dst, :] = own_state_ref[dst, :]
+
+        @pl.when(here & (place.core == core))
+        def _():
+            grad_ref[own, :] = came.astype(F32)
 
         @pl.when(jnp.logical_not(here))
         def _():
-            state_ref[dst, :] = jnp.where(near, half_ref[src, :], half_other_ref[src, :])
-
-        @pl.when(here & (place.core != core))
-        def _():
-            state_ref[dst, :] = other_ref[own, :]
-
-        @pl.when(here & (place.core == core))
-        def _():
-            state_ref[dst, :] = mine_ref[own, :]
-            far = jnp.where(near, half_ref[src, :], half_other_ref[src, :])
-            grad_ref[own, :] += (
-                far.astype(F32) + back_ref[dst, :].astype(F32) + back_other_ref[dst, :].astype(F32)
-            )
+            state_ref[dst, :] = came
 
     for s in range(lr_ref.shape[0]):
         row = pl.ds(pl.multiple_of(local_ref[s] * tile, tile), tile)
         col = pl.ds(pl.multiple_of(hub_ref[s] * tile, tile), tile)
         grad_ref[row, :] += dot(lr_ref[s], state_ref[col, :])
 
-    current = current_ref[...]
-    gradient = grad_ref[...] + (ridge_ref[...] * current - zscores_ref[...])
-    following = current - STEP * gradient
+    following = partial_ref[...] - STEP * grad_ref[...]
     next_ref[...] = following
     if not last:
         panel_ref[...] = following.astype(BF16)
@@ -184,7 +261,6 @@
     hub_rows = hubs * tile
     half = hub_rows // cores
     total = rows_dev * cores
-    params = pltpu.CompilerParams(vmem_limit_bytes=48 * 1024 * 1024)
     panel_type = jax.ShapeDtypeStruct((rows, traits), BF16)
     back_type = jax.ShapeDtypeStruct((hub_rows, traits), BF16)
     ridge = ridge[None, :]
@@ -203,10 +279,17 @@
     panels, back = pl.pallas_call(
         first_kernel,
         out_shape=(panel_type, back_type),
-        in_specs=[SMEM, SMEM, VMEM, VMEM],
+        in_specs=[HBM] * 4,
         out_specs=(VMEM, VMEM),
-        scratch_shapes=[pltpu.VMEM((hub_rows, traits), F32)],
-        compiler_params=params,
+        scratch_shapes=[
+            pltpu.VMEM((hub_rows, traits), F32),
+            pltpu.SMEM(lr_local.shape, jnp.int32),
+            pltpu.SMEM(lr_hub.shape, jnp.int32),
+            pltpu.VMEM(effects.shape, F32),
+            pltpu.VMEM(lr.shape, BF16),
+            pltpu.SemaphoreType.DMA((4,)),
+        ],
+        compiler_params=WIDE,
         name="first",
     )(lr_local, lr_hub, effects, lr)
 
@@ -221,23 +304,44 @@
             out_shape=jax.ShapeDtypeStruct((half, traits), BF16),
             in_specs=[SMEM, VMEM, VMEM, VMEM, VMEM],
             out_specs=VMEM,
-            compiler_params=params,
+            compiler_params=NARROW,
             name="pick",
         )(hub_blocks, panels, other, back, back_other)
         gathered = exchange(chosen)
         merged = pl.pallas_call(
             functools.partial(merge_kernel, cores, tile, blocks * cores),
             out_shape=jax.ShapeDtypeStruct(gathered.shape, BF16),
-            in_specs=[SMEM, VMEM],
+            in_specs=[SMEM, VMEM, ANY],
             out_specs=VMEM,
-            compiler_params=params,
+            compiler_params=NARROW,
             name="merge",
-        )(hub_blocks, gathered)
+        )(hub_blocks, gathered, outer)
+        partial, own_state = pl.pallas_call(
+            functools.partial(band_kernel, cores),
+            out_shape=(jax.ShapeDtypeStruct((rows, traits), F32), back_type),
+            in_specs=[SMEM] + [HBM] * 9,
+            out_specs=(VMEM, VMEM),
+            scratch_shapes=[
+                pltpu.VMEM((rows + (band.shape[1] - 1) * tile, traits), BF16),
+                pltpu.VMEM(current.shape, F32),
+                pltpu.VMEM(zscores.shape, F32),
+                pltpu.VMEM(ridge.shape, F32),
+                pltpu.VMEM(band.shape, BF16),
+                pltpu.VMEM(back.shape, BF16),
+                pltpu.VMEM(back.shape, BF16),
+                pltpu.SemaphoreType.DMA((9,)),
+            ],
+            compiler_params=WIDE,
+            cost_estimate=pl.CostEstimate(
+                flops=2 * band.size * traits, bytes_accessed=8 * 2**20, transcendentals=0
+            ),
+            name="band",
+        )(hub_blocks, current, zscores, ridge, band, panels, other, outer, back, back_other)
         mine = exchange(merged).reshape(half, traits)
+        mine, partial, own_state = lax.optimization_barrier((mine, partial, own_state))
         theirs = other_core(mine)
         out_shape = [jax.ShapeDtypeStruct((rows, traits), F32)]
         scratch = [
-            pltpu.VMEM((rows + 2 * ((band.shape[1] - 1) // 2) * tile, traits), BF16),
             pltpu.VMEM((hub_rows, traits), BF16),
             pltpu.VMEM((rows, traits), F32),
         ]
@@ -247,27 +351,20 @@
         result = pl.pallas_call(
             functools.partial(step_kernel, cores, last),
             out_shape=tuple(out_shape),
-            in_specs=[SMEM] * 3 + [VMEM] * 12,
+            in_specs=[SMEM] * 3 + [VMEM] * 5,
             out_specs=(VMEM,) * len(out_shape),
             scratch_shapes=scratch,
-            compiler_params=params,
+            compiler_params=NARROW,
             name="step",
         )(
             hub_blocks,
             lr_local,
             lr_hub,
-            current,
-            zscores,
-            ridge,
-            band,
+            partial,
             lr,
-            panels,
-            other,
-            outer,
+            own_state,
             mine,
             theirs,
-            back,
-            back_other,
         )
         if last:
             return result[0]

time: 98.8 us -> 86.2 us (0.87)
  the two profiles are of different devices: /device:TPU:13 before, /device:TPU:0 now
where the time goes in v2:
time: 86.2 us; the launch traced here: 85.4 us
  waiting for transfers between devices  32.7 us (38%)
  Pallas kernels  23.8 us (28%)
  starting transfers between devices  21 us (24%)
  local copies, waits for them, and re-layouts  7.64 us (9%)
    all_to_all x4, waiting for transfers between devices, exchange(): return lax.all_to_all(x, 'row', 0, 0)  26.5 us
    all_to_all x4, starting transfers between devices, exchange(): return lax.all_to_all(x, 'row', 0, 0)  18.6 us
    pallas_call x2, Pallas kernels, shards(): pl.pallas_call(functools.partial(band_kernel, cores), out_shape=(jax.Shap...  11.4 us
    unnamed x42, local copies, waits for them, and re-layouts  7.64 us
    ppermute x6, waiting for transfers between devices, other_core(): return lax.ppermute(x, 'col', swap)  6.25 us
    pallas_call x2, Pallas kernels, shards(): pl.pallas_call(functools.partial(step_kernel, cores, last), out_shape=tup...  4.22 us
    pallas_call x2, Pallas kernels, shards(): pl.pallas_call(functools.partial(pick_kernel, cores, tile), out_shape=jax...  2.75 us
    pallas_call x2, Pallas kernels, shards(): pl.pallas_call(functools.partial(merge_kernel, cores, tile, blocks * core...  2.69 us
  transfers between devices with their start and end apart: 12, of which 10 were waited for; matrix products, arithmetic and copies ran while one was open for 0% of the time, Pallas kernels for 17%

profile of v2, /device:TPU:0, one launch (start us, length us, event | category | flops | bytes accessed | tf_op | source)
XLA Modules:
  0.0 85.4 jit_solution(14447738858656004612)
XLA Ops:
  0.0 0.0 copy-start.16
  0.0 2.7 %first.1 = (bf16[512,512]{1,0:T(8,128)(2,1)}, bf16[512,512]{1,0:T(8,128)(2,1)}) custom-call(s32[8]{0:T(128)} %local_ref.3, s32[8]{0:T(128)} %hub_ref.3, f32[512,512]{1,0:T(8,128)} %current_hbm.1, bf16[8,128,128]{2,1,0:T(8,128)(2,1)} %lr_ref.3), custom_call_target="tpu_custom_call" | custom-call | tf_op jit(solution)/shard_map/first/pallas_call | solution.py:279
  2.7 0.5 collective-permute-start
  3.2 0.1 collective-permute-start.1
  3.3 0.7 collective-permute-start.2
  4.0 1.0 %collective-permute-done.other_ref.other_hbm = bf16[512,512]{1,0:T(8,128)(2,1)S(1)} collective-permute-done((bf16[512,512]{1,0:T(8,128)(2,1)}, bf16[512,512]{1,0:T(8,128)(2,1)S(1)}, u32[]{:S(2)}, u32[]{:S(2)}) %collective-permute-start) | collective-permute-done | bytes 524320 | tf_op jit(solution)/shard_map/ppermute | solution.py:273
  4.9 0.7 collective-permute-done.1.back_other_ref.back_other_hbm
  5.7 0.0 copy-done.16
  5.7 1.0 %copy-done.3 = bf16[512,512]{1,0:T(8,128)(2,1)S(1)} copy-done((bf16[512,512]{1,0:T(8,128)(2,1)S(1)}, bf16[512,512]{1,0:T(8,128)(2,1)}, u32[]{:S(2)}) %copy-start.3) | copy-done | bytes 524312
  6.7 1.0 %copy-done.4 = bf16[512,512]{1,0:T(8,128)(2,1)S(1)} copy-done((bf16[512,512]{1,0:T(8,128)(2,1)S(1)}, bf16[512,512]{1,0:T(8,128)(2,1)}, u32[]{:S(2)}) %copy-start.4) | copy-done | bytes 524312
  7.8 1.4 %pick.2 = bf16[256,512]{1,0:T(8,128)(2,1)} custom-call(s32[4]{0:T(128)S(1)} %copy-done.16, bf16[512,512]{1,0:T(8,128)(2,1)S(1)} %copy-done.3, bf16[512,512]{1,0:T(8,128)(2,1)S(1)} %collective-permute-done.other_ref.other_hbm, bf16[512,512]{1,0:T(8,128)(2,1)S(1)} %copy-done.4, bf16[512,512]{1,0:T(8,128)(2,1)S(1)} %collective-permute-done.1.back_other_ref.back_other_hbm), custom_call_target="tpu_custom_call" | custom-call | tf_op jit(solution)/shard_map/pick/pallas_call | solution.py:302
  9.2 0.0 copy-done.6
  9.2 0.0 copy-done.8
  9.2 7.1 %all-to-all-start = ((bf16[8,32,512]{2,1,0:T(8,128)(2,1)}), bf16[8,32,512]{2,1,0:T(8,128)(2,1)S(1)}, u32[]{:S(2)}, u32[]{:S(2)}) async-start(bf16[8,32,512]{2,1,0:T(8,128)(2,1)} %bitcast), calls=%async_computation | async-start | bytes 524288 | tf_op jit(solution)/shard_map/all_to_all | solution.py:277
  16.3 0.0 collective-permute-done.2.outer_ref.outer_hbm
  16.3 0.0 copy-start.10
  16.3 9.5 %all-to-all-done.in_ref = bf16[8,32,512]{2,1,0:T(8,128)(2,1)S(1)} async-done(((bf16[8,32,512]{2,1,0:T(8,128)(2,1)}), bf16[8,32,512]{2,1,0:T(8,128)(2,1)S(1)}, u32[]{:S(2)}, u32[]{:S(2)}) %all-to-all-start) | async-done | bytes 262176 | tf_op jit(solution)/shard_map/all_to_all | solution.py:277
  25.9 1.3 %merge.2 = bf16[8,32,512]{2,1,0:T(8,128)(2,1)} custom-call(s32[4]{0:T(128)S(1)} %copy-done.16, bf16[8,32,512]{2,1,0:T(8,128)(2,1)S(1)} %all-to-all-done.in_ref, bf16[512,512]{1,0:T(8,128)(2,1)S(1)} %collective-permute-done.2.outer_ref.outer_hbm), custom_call_target="tpu_custom_call" | custom-call | tf_op jit(solution)/shard_map/merge/pallas_call | solution.py:311
  27.2 3.6 %all-to-all-start.1 = ((bf16[8,32,512]{2,1,0:T(8,128)(2,1)}), bf16[8,32,512]{2,1,0:T(8,128)(2,1)S(1)}, u32[]{:S(2)}, u32[]{:S(2)}) async-start(bf16[8,32,512]{2,1,0:T(8,128)(2,1)} %merge.2), calls=%async_computation.1 | async-start | bytes 524288 | tf_op jit(solution)/shard_map/all_to_all | solution.py:277
  30.8 0.0 copy-done.10
  30.8 0.0 copy-start
  30.8 0.0 copy-start.17
  30.8 0.0 copy-start.19
  30.8 0.0 copy-start.20
  30.8 5.7 %band.2 = (f32[512,512]{1,0:T(8,128)}, bf16[512,512]{1,0:T(8,128)(2,1)}) custom-call(s32[4]{0:T(128)} %blocks_ref.15, f32[512,512]{1,0:T(8,128)} %current_hbm.1, f32[512,512]{1,0:T(8,128)} %zscores_hbm.3, f32[1,512]{1,0:T(1,128)} %bitcast.9, bf16[4,9,128,128]{3,2,1,0:T(8,128)(2,1)} %band_hbm.3, bf16[512,512]{1,0:T(8,128)(2,1)} %get-tuple-element.20.mine_ref.mine_hbm, ...), custom_call_target="tpu_custom_call" | custom-call | flops 603979776 | bytes 8388608 | tf_op jit(solution)/shard_map/band/pallas_call | solution.py:319
  36.5 3.4 %all-to-all-done.1 = bf16[8,32,512]{2,1,0:T(8,128)(2,1)S(1)} async-done(((bf16[8,32,512]{2,1,0:T(8,128)(2,1)}), bf16[8,32,512]{2,1,0:T(8,128)(2,1)S(1)}, u32[]{:S(2)}, u32[]{:S(2)}) %all-to-all-start.1) | async-done | bytes 262176 | tf_op jit(solution)/shard_map/all_to_all | solution.py:277
  39.9 0.0 collective-permute-start.3
  39.9 1.5 %collective-permute-done.3.half_other_ref = bf16[256,512]{1,0:T(8,128)(2,1)S(1)} collective-permute-done((bf16[256,512]{1,0:T(8,128)(2,1)S(1)}, bf16[256,512]{1,0:T(8,128)(2,1)S(1)}, u32[]{:S(2)}, u32[]{:S(2)}) %collective-permute-start.3) | collective-permute-done | bytes 262176 | tf_op jit(solution)/shard_map/ppermute | solution.py:273
  41.4 0.0 copy-done
  41.4 0.0 copy-done.17
  41.4 0.0 copy-done.19
  41.4 0.0 copy-done.20
  41.4 0.0 copy-start.11
  41.5 1.2 %copy-done.11 = f32[512,512]{1,0:T(8,128)S(1)} copy-done((f32[512,512]{1,0:T(8,128)S(1)}, f32[512,512]{1,0:T(8,128)}, u32[]{:S(2)}) %copy-start.11) | copy-done | bytes 1048600
  42.7 1.0 %copy-done.14 = bf16[512,512]{1,0:T(8,128)(2,1)S(1)} copy-done((bf16[512,512]{1,0:T(8,128)(2,1)S(1)}, bf16[512,512]{1,0:T(8,128)(2,1)}, u32[]{:S(2)}) %copy-start.14) | copy-done | bytes 524312
  43.7 1.9 %step.2 = (f32[512,512]{1,0:T(8,128)S(1)}, bf16[512,512]{1,0:T(8,128)(2,1)S(1)}, bf16[512,512]{1,0:T(8,128)(2,1)S(1)}) custom-call(s32[4]{0:T(128)S(1)} %copy-done.17, s32[8]{0:T(128)S(1)} %copy-done.19, s32[8]{0:T(128)S(1)} %copy-done.20, f32[512,512]{1,0:T(8,128)S(1)} %copy-done.11, bf16[8,128,128]{2,1,0:T(8,128)(2,1)S(1)} %copy-done, ...), custom_call_target="tpu_custom_call" | custom-call | tf_op jit(solution)/shard_map/step/pallas_call | solution.py:351
  45.6 0.0 copy-start.12
  45.7 1.0 %copy-done.12 = f32[512,512]{1,0:T(8,128)} copy-done((f32[512,512]{1,0:T(8,128)}, f32[512,512]{1,0:T(8,128)S(1)}, u32[]{:S(2)}) %copy-start.12) | copy-done | bytes 1048600
  46.6 0.1 collective-permute-start.4
  46.7 0.4 collective-permute-start.5
  47.1 0.7 collective-permute-start.6
  47.8 0.7 collective-permute-done.4.other_ref.other_hbm
  48.5 0.7 collective-permute-done.5.back_other_ref.back_other_hbm
  49.3 1.4 %pick.3 = bf16[256,512]{1,0:T(8,128)(2,1)} custom-call(s32[4]{0:T(128)S(1)} %copy-done.17, bf16[512,512]{1,0:T(8,128)(2,1)S(1)} %get-tuple-element.27.mine_ref.mine_hbm, bf16[512,512]{1,0:T(8,128)(2,1)S(1)} %collective-permute-done.4.other_ref.other_hbm, bf16[512,512]{1,0:T(8,128)(2,1)S(1)} %get-tuple-element.28.back_ref.back_hbm, ...), custom_call_target="tpu_custom_call" | custom-call | tf_op jit(solution)/shard_map/pick/pallas_call | solution.py:302
  50.7 0.0 copy-done.1
  50.7 0.0 copy-done.2
  50.7 0.0 copy-done.5
  50.7 0.0 copy-done.7
  50.7 3.7 %all-to-all-start.2 = ((bf16[8,32,512]{2,1,0:T(8,128)(2,1)}), bf16[8,32,512]{2,1,0:T(8,128)(2,1)S(1)}, u32[]{:S(2)}, u32[]{:S(2)}) async-start(bf16[8,32,512]{2,1,0:T(8,128)(2,1)} %bitcast.3), calls=%async_computation.2 | async-start | bytes 524288 | tf_op jit(solution)/shard_map/all_to_all | solution.py:277
  54.4 0.0 collective-permute-done.6.outer_ref.outer_hbm
  54.4 0.0 copy-start.9
  54.4 10.2 %all-to-all-done.2.in_ref = bf16[8,32,512]{2,1,0:T(8,128)(2,1)S(1)} async-done(((bf16[8,32,512]{2,1,0:T(8,128)(2,1)}), bf16[8,32,512]{2,1,0:T(8,128)(2,1)S(1)}, u32[]{:S(2)}, u32[]{:S(2)}) %all-to-all-start.2) | async-done | bytes 262176 | tf_op jit(solution)/shard_map/all_to_all | solution.py:277
  64.6 1.4 %merge.3 = bf16[8,32,512]{2,1,0:T(8,128)(2,1)} custom-call(s32[4]{0:T(128)S(1)} %copy-done.17, bf16[8,32,512]{2,1,0:T(8,128)(2,1)S(1)} %all-to-all-done.2.in_ref, bf16[512,512]{1,0:T(8,128)(2,1)S(1)} %collective-permute-done.6.outer_ref.outer_hbm), custom_call_target="tpu_custom_call" | custom-call | tf_op jit(solution)/shard_map/merge/pallas_call | solution.py:311
  66.0 4.2 %all-to-all-start.3 = ((bf16[8,32,512]{2,1,0:T(8,128)(2,1)}), bf16[8,32,512]{2,1,0:T(8,128)(2,1)S(1)}, u32[]{:S(2)}, u32[]{:S(2)}) async-start(bf16[8,32,512]{2,1,0:T(8,128)(2,1)} %merge.3), calls=%async_computation.3 | async-start | bytes 524288 | tf_op jit(solution)/shard_map/all_to_all | solution.py:277
  70.1 0.0 copy-done.9
  70.1 0.0 copy-start.18
  70.1 5.7 %band.3 = (f32[512,512]{1,0:T(8,128)}, bf16[512,512]{1,0:T(8,128)(2,1)}) custom-call(s32[4]{0:T(128)} %blocks_ref.15, f32[512,512]{1,0:T(8,128)} %copy-done.12, f32[512,512]{1,0:T(8,128)} %zscores_hbm.3, f32[1,512]{1,0:T(1,128)} %bitcast.10, bf16[4,9,128,128]{3,2,1,0:T(8,128)(2,1)} %band_hbm.3, bf16[512,512]{1,0:T(8,128)(2,1)} %copy-done.1, ...), custom_call_target="tpu_custom_call" | custom-call | flops 603979776 | bytes 8388608 | tf_op jit(solution)/shard_map/band/pallas_call | solution.py:319
  75.9 3.4 %all-to-all-done.3 = bf16[8,32,512]{2,1,0:T(8,128)(2,1)S(1)} async-done(((bf16[8,32,512]{2,1,0:T(8,128)(2,1)}), bf16[8,32,512]{2,1,0:T(8,128)(2,1)S(1)}, u32[]{:S(2)}, u32[]{:S(2)}) %all-to-all-start.3) | async-done | bytes 262176 | tf_op jit(solution)/shard_map/all_to_all | solution.py:277
  79.3 0.0 collective-permute-start.7
  79.3 1.5 %collective-permute-done.7.half_other_ref = bf16[256,512]{1,0:T(8,128)(2,1)S(1)} collective-permute-done((bf16[256,512]{1,0:T(8,128)(2,1)S(1)}, bf16[256,512]{1,0:T(8,128)(2,1)S(1)}, u32[]{:S(2)}, u32[]{:S(2)}) %collective-permute-start.7) | collective-permute-done | bytes 262176 | tf_op jit(solution)/shard_map/ppermute | solution.py:273
  80.8 0.0 copy-done.18
  80.8 1.2 %copy-done.13 = f32[512,512]{1,0:T(8,128)S(1)} copy-done((f32[512,512]{1,0:T(8,128)S(1)}, f32[512,512]{1,0:T(8,128)}, u32[]{:S(2)}) %copy-start.13) | copy-done | bytes 1048600
  82.0 1.0 %copy-done.15 = bf16[512,512]{1,0:T(8,128)(2,1)S(1)} copy-done((bf16[512,512]{1,0:T(8,128)(2,1)S(1)}, bf16[512,512]{1,0:T(8,128)(2,1)}, u32[]{:S(2)}) %copy-start.15) | copy-done | bytes 524312
  83.1 2.3 %step.3 = f32[512,512]{1,0:T(8,128)} custom-call(s32[4]{0:T(128)S(1)} %copy-done.18, s32[8]{0:T(128)S(1)} %copy-done.19, s32[8]{0:T(128)S(1)} %copy-done.20, f32[512,512]{1,0:T(8,128)S(1)} %copy-done.13, bf16[8,128,128]{2,1,0:T(8,128)(2,1)S(1)} %copy-done, bf16[512,512]{1,0:T(8,128)(2,1)S(1)} %copy-done.15, bf16[256,512]{1,0:T(8,128)(2,1)S(1)} %bitcast.8, ...), custom_call_target="tpu_custom_call" | custom-call | tf_op jit(solution)/shard_map/step/pallas_call | solution.py:351
  (11 shorter events, 0.0 us)
Async XLA Ops:
  0.0 5.7 %copy-start.16 = (s32[4]{0:T(128)S(1)}, s32[4]{0:T(128)}, u32[]{:S(2)}) copy-start(s32[4]{0:T(128)} %blocks_ref.15) | copy-start | bytes 52
  2.7 2.3 %collective-permute-start = (bf16[512,512]{1,0:T(8,128)(2,1)}, bf16[512,512]{1,0:T(8,128)(2,1)S(1)}, u32[]{:S(2)}, u32[]{:S(2)}) collective-permute-start(bf16[512,512]{1,0:T(8,128)(2,1)} %get-tuple-element.20.mine_ref.mine_hbm), channel_id=1, source_target_pairs={{0,1},{1,0},{2,3},{3,2},{4,5},{5,4},{6,7},{7,6},{8,9},{9,8},{10,11... | collective-permute-start | bytes 1572872 | tf_op jit(solution)/shard_map/ppermute | solution.py:273
  3.2 2.5 %collective-permute-start.1 = (bf16[512,512]{1,0:T(8,128)(2,1)}, bf16[512,512]{1,0:T(8,128)(2,1)S(1)}, u32[]{:S(2)}, u32[]{:S(2)}) collective-permute-start(bf16[512,512]{1,0:T(8,128)(2,1)} %get-tuple-element.21.back_ref.back_hbm), channel_id=1, source_target_pairs={{0,1},{1,0},{2,3},{3,2},{4,5},{5,4},{6,7},{7,6},{8,9},{9,8},{10,11... | collective-permute-start | bytes 1572872 | tf_op jit(solution)/shard_map/ppermute | solution.py:273
  3.3 13.0 %collective-permute-start.2 = (bf16[512,512]{1,0:T(8,128)(2,1)}, bf16[512,512]{1,0:T(8,128)(2,1)S(1)}, u32[]{:S(2)}, u32[]{:S(2)}) collective-permute-start(bf16[512,512]{1,0:T(8,128)(2,1)} %get-tuple-element.20.mine_ref.mine_hbm), channel_id=1, source_target_pairs={{1,2},{3,4},{5,6},{7,8},{9,10},{11,12},{13,14},{2,1},{4,3},{6,5},{... | collective-permute-start | bytes 1572872 | tf_op jit(solution)/shard_map/ppermute | solution.py:301
  4.9 4.2 %copy-start.6 = (bf16[512,512]{1,0:T(8,128)(2,1)}, bf16[512,512]{1,0:T(8,128)(2,1)S(1)}, u32[]{:S(2)}) copy-start(bf16[512,512]{1,0:T(8,128)(2,1)S(1)} %collective-permute-done.other_ref.other_hbm) | copy-start | bytes 1572868
  5.7 1.0 %copy-start.3 = (bf16[512,512]{1,0:T(8,128)(2,1)S(1)}, bf16[512,512]{1,0:T(8,128)(2,1)}, u32[]{:S(2)}) copy-start(bf16[512,512]{1,0:T(8,128)(2,1)} %get-tuple-element.20.mine_ref.mine_hbm) | copy-start | bytes 1572868
  6.7 1.0 %copy-start.4 = (bf16[512,512]{1,0:T(8,128)(2,1)S(1)}, bf16[512,512]{1,0:T(8,128)(2,1)}, u32[]{:S(2)}) copy-start(bf16[512,512]{1,0:T(8,128)(2,1)} %get-tuple-element.21.back_ref.back_hbm) | copy-start | bytes 1572868
  7.8 1.4 %copy-start.8 = (bf16[512,512]{1,0:T(8,128)(2,1)}, bf16[512,512]{1,0:T(8,128)(2,1)S(1)}, u32[]{:S(2)}) copy-start(bf16[512,512]{1,0:T(8,128)(2,1)S(1)} %collective-permute-done.1.back_other_ref.back_other_hbm) | copy-start | bytes 1572868
  9.2 16.7 %all-to-all-start = ((bf16[8,32,512]{2,1,0:T(8,128)(2,1)}), bf16[8,32,512]{2,1,0:T(8,128)(2,1)S(1)}, u32[]{:S(2)}, u32[]{:S(2)}) async-start(bf16[8,32,512]{2,1,0:T(8,128)(2,1)} %bitcast), calls=%async_computation | async-start | bytes 524288 | tf_op jit(solution)/shard_map/all_to_all | solution.py:277
  16.3 14.5 %copy-start.10 = (bf16[512,512]{1,0:T(8,128)(2,1)}, bf16[512,512]{1,0:T(8,128)(2,1)S(1)}, u32[]{:S(2)}) copy-start(bf16[512,512]{1,0:T(8,128)(2,1)S(1)} %collective-permute-done.2.outer_ref.outer_hbm) | copy-start | bytes 1572868
  27.2 12.7 %all-to-all-start.1 = ((bf16[8,32,512]{2,1,0:T(8,128)(2,1)}), bf16[8,32,512]{2,1,0:T(8,128)(2,1)S(1)}, u32[]{:S(2)}, u32[]{:S(2)}) async-start(bf16[8,32,512]{2,1,0:T(8,128)(2,1)} %merge.2), calls=%async_computation.1 | async-start | bytes 524288 | tf_op jit(solution)/shard_map/all_to_all | solution.py:277
  30.8 10.6 %copy-start = (bf16[8,128,128]{2,1,0:T(8,128)(2,1)S(1)}, bf16[8,128,128]{2,1,0:T(8,128)(2,1)}, u32[]{:S(2)}) copy-start(bf16[8,128,128]{2,1,0:T(8,128)(2,1)} %lr_ref.3) | copy-start | bytes 786436
  30.8 10.6 %copy-start.17 = (s32[4]{0:T(128)S(1)}, s32[4]{0:T(128)}, u32[]{:S(2)}) copy-start(s32[4]{0:T(128)} %blocks_ref.15) | copy-start | bytes 52
  30.8 10.6 %copy-start.19 = (s32[8]{0:T(128)S(1)}, s32[8]{0:T(128)}, u32[]{:S(2)}) copy-start(s32[8]{0:T(128)} %local_ref.3) | copy-start | bytes 100
  30.8 10.6 %copy-start.20 = (s32[8]{0:T(128)S(1)}, s32[8]{0:T(128)}, u32[]{:S(2)}) copy-start(s32[8]{0:T(128)} %hub_ref.3) | copy-start | bytes 100
  39.9 1.5 %collective-permute-start.3 = (bf16[256,512]{1,0:T(8,128)(2,1)S(1)}, bf16[256,512]{1,0:T(8,128)(2,1)S(1)}, u32[]{:S(2)}, u32[]{:S(2)}) collective-permute-start(bf16[256,512]{1,0:T(8,128)(2,1)S(1)} %bitcast.5), channel_id=1, source_target_pairs={{0,1},{1,0},{2,3},{3,2},{4,5},{5,4},{6,7},{7,6},{8,9},{9,8},{10,11... | collective-permute-start | bytes 786440 | tf_op jit(solution)/shard_map/ppermute | solution.py:273
  41.4 1.2 %copy-start.11 = (f32[512,512]{1,0:T(8,128)S(1)}, f32[512,512]{1,0:T(8,128)}, u32[]{:S(2)}) copy-start(f32[512,512]{1,0:T(8,128)} %get-tuple-element.24.partial_ref) | copy-start | bytes 3145732
  42.7 1.0 %copy-start.14 = (bf16[512,512]{1,0:T(8,128)(2,1)S(1)}, bf16[512,512]{1,0:T(8,128)(2,1)}, u32[]{:S(2)}) copy-start(bf16[512,512]{1,0:T(8,128)(2,1)} %get-tuple-element.25.own_state_ref) | copy-start | bytes 1572868
  45.6 1.0 %copy-start.12 = (f32[512,512]{1,0:T(8,128)}, f32[512,512]{1,0:T(8,128)S(1)}, u32[]{:S(2)}) copy-start(f32[512,512]{1,0:T(8,128)S(1)} %get-tuple-element.29.current_hbm) | copy-start | bytes 3145732
  46.6 4.0 %copy-start.1 = (bf16[512,512]{1,0:T(8,128)(2,1)}, bf16[512,512]{1,0:T(8,128)(2,1)S(1)}, u32[]{:S(2)}) copy-start(bf16[512,512]{1,0:T(8,128)(2,1)S(1)} %get-tuple-element.27.mine_ref.mine_hbm) | copy-start | bytes 1572868
  46.6 4.0 %copy-start.2 = (bf16[512,512]{1,0:T(8,128)(2,1)}, bf16[512,512]{1,0:T(8,128)(2,1)S(1)}, u32[]{:S(2)}) copy-start(bf16[512,512]{1,0:T(8,128)(2,1)S(1)} %get-tuple-element.28.back_ref.back_hbm) | copy-start | bytes 1572868
  46.6 1.9 %collective-permute-start.4 = (bf16[512,512]{1,0:T(8,128)(2,1)S(1)}, bf16[512,512]{1,0:T(8,128)(2,1)S(1)}, u32[]{:S(2)}, u32[]{:S(2)}) collective-permute-start(bf16[512,512]{1,0:T(8,128)(2,1)S(1)} %get-tuple-element.27.mine_ref.mine_hbm), channel_id=1, source_target_pairs={{0,1},{1,0},{2,3},{3,2},{4,5},{5,4},{6,7},{7,6},{8,9},{9,8},{10,11... | collective-permute-start | bytes 1572872 | tf_op jit(solution)/shard_map/ppermute | solution.py:273
  46.7 2.5 %collective-permute-start.5 = (bf16[512,512]{1,0:T(8,128)(2,1)S(1)}, bf16[512,512]{1,0:T(8,128)(2,1)S(1)}, u32[]{:S(2)}, u32[]{:S(2)}) collective-permute-start(bf16[512,512]{1,0:T(8,128)(2,1)S(1)} %get-tuple-element.28.back_ref.back_hbm), channel_id=1, source_target_pairs={{0,1},{1,0},{2,3},{3,2},{4,5},{5,4},{6,7},{7,6},{8,9},{9,8},{10,11... | collective-permute-start | bytes 1572872 | tf_op jit(solution)/shard_map/ppermute | solution.py:273
  47.1 7.2 %collective-permute-start.6 = (bf16[512,512]{1,0:T(8,128)(2,1)S(1)}, bf16[512,512]{1,0:T(8,128)(2,1)S(1)}, u32[]{:S(2)}, u32[]{:S(2)}) collective-permute-start(bf16[512,512]{1,0:T(8,128)(2,1)S(1)} %get-tuple-element.27.mine_ref.mine_hbm), channel_id=1, source_target_pairs={{1,2},{3,4},{5,6},{7,8},{9,10},{11,12},{13,14},{2,1},{4,3},{6,5},{... | collective-permute-start | bytes 1572872 | tf_op jit(solution)/shard_map/ppermute | solution.py:301
  48.5 2.1 %copy-start.5 = (bf16[512,512]{1,0:T(8,128)(2,1)}, bf16[512,512]{1,0:T(8,128)(2,1)S(1)}, u32[]{:S(2)}) copy-start(bf16[512,512]{1,0:T(8,128)(2,1)S(1)} %collective-permute-done.4.other_ref.other_hbm) | copy-start | bytes 1572868
  49.3 1.4 %copy-start.7 = (bf16[512,512]{1,0:T(8,128)(2,1)}, bf16[512,512]{1,0:T(8,128)(2,1)S(1)}, u32[]{:S(2)}) copy-start(bf16[512,512]{1,0:T(8,128)(2,1)S(1)} %collective-permute-done.5.back_other_ref.back_other_hbm) | copy-start | bytes 1572868
  50.7 13.9 %all-to-all-start.2 = ((bf16[8,32,512]{2,1,0:T(8,128)(2,1)}), bf16[8,32,512]{2,1,0:T(8,128)(2,1)S(1)}, u32[]{:S(2)}, u32[]{:S(2)}) async-start(bf16[8,32,512]{2,1,0:T(8,128)(2,1)} %bitcast.3), calls=%async_computation.2 | async-start | bytes 524288 | tf_op jit(solution)/shard_map/all_to_all | solution.py:277
  54.4 15.8 %copy-start.9 = (bf16[512,512]{1,0:T(8,128)(2,1)}, bf16[512,512]{1,0:T(8,128)(2,1)S(1)}, u32[]{:S(2)}) copy-start(bf16[512,512]{1,0:T(8,128)(2,1)S(1)} %collective-permute-done.6.outer_ref.outer_hbm) | copy-start | bytes 1572868
  66.0 13.3 %all-to-all-start.3 = ((bf16[8,32,512]{2,1,0:T(8,128)(2,1)}), bf16[8,32,512]{2,1,0:T(8,128)(2,1)S(1)}, u32[]{:S(2)}, u32[]{:S(2)}) async-start(bf16[8,32,512]{2,1,0:T(8,128)(2,1)} %merge.3), calls=%async_computation.3 | async-start | bytes 524288 | tf_op jit(solution)/shard_map/all_to_all | solution.py:277
  70.1 10.7 %copy-start.18 = (s32[4]{0:T(128)S(1)}, s32[4]{0:T(128)}, u32[]{:S(2)}) copy-start(s32[4]{0:T(128)} %blocks_ref.15) | copy-start | bytes 52
  79.3 1.5 %collective-permute-start.7 = (bf16[256,512]{1,0:T(8,128)(2,1)S(1)}, bf16[256,512]{1,0:T(8,128)(2,1)S(1)}, u32[]{:S(2)}, u32[]{:S(2)}) collective-permute-start(bf16[256,512]{1,0:T(8,128)(2,1)S(1)} %bitcast.7), channel_id=1, source_target_pairs={{0,1},{1,0},{2,3},{3,2},{4,5},{5,4},{6,7},{7,6},{8,9},{9,8},{10,11... | collective-permute-start | bytes 786440 | tf_op jit(solution)/shard_map/ppermute | solution.py:273
  80.8 1.2 %copy-start.13 = (f32[512,512]{1,0:T(8,128)S(1)}, f32[512,512]{1,0:T(8,128)}, u32[]{:S(2)}) copy-start(f32[512,512]{1,0:T(8,128)} %get-tuple-element.32.partial_ref) | copy-start | bytes 3145732
  82.0 1.0 %copy-start.15 = (bf16[512,512]{1,0:T(8,128)(2,1)S(1)}, bf16[512,512]{1,0:T(8,128)(2,1)}, u32[]{:S(2)}) copy-start(bf16[512,512]{1,0:T(8,128)(2,1)} %get-tuple-element.33.own_state_ref) | copy-start | bytes 1572868

commit v3 on v2

v3 whole, which is shorter than its diff:
```python
import functools

import jax
import jax.numpy as jnp
from jax import lax
from jax.experimental import pallas as pl
from jax.experimental.pallas import tpu as pltpu
from jax.sharding import PartitionSpec as P

ITERS = 2
STEP = 0.5
F32 = jnp.float32
BF16 = jnp.bfloat16
FIRST = pltpu.CompilerParams(vmem_limit_bytes=58 * 2**20)
MERGE = pltpu.CompilerParams(vmem_limit_bytes=12 * 2**20)
BAND = pltpu.CompilerParams(vmem_limit_bytes=58 * 2**20)
UPDATE = pltpu.CompilerParams(vmem_limit_bytes=53850 * 2**10)
VMEM = pl.BlockSpec(memory_space=pltpu.VMEM)
HBM = pl.BlockSpec(memory_space=pltpu.HBM)
ANY = pl.BlockSpec(memory_space=pl.ANY)
SMEM = pl.BlockSpec(memory_space=pltpu.SMEM)


def dot(a, b):
    return jnp.dot(a, b, preferred_element_type=F32)


def dot_t(a, b):
    return lax.dot_general(a, b, (((0,), (0,)), ((), ())), preferred_element_type=F32)


class Place:
    def __init__(self, block, blocks, cores):
        self.chip = block // (blocks * cores)
        self.core = (block // blocks) % cores
        self.blk = block % blocks


def back_terms(local_ref, hub_ref, lr_ref, panel_ref, term_ref, acc_ref, out_ref):
    count, tile, _ = lr_ref.shape
    for s in range(count):
        rows = pl.ds(pl.multiple_of(local_ref[s] * tile, tile), tile)
        term_ref[s] = dot_t(lr_ref[s], panel_ref[rows, :])
    acc_ref[...] = jnp.zeros_like(acc_ref)
    for s in range(count):
        acc_ref[pl.ds(pl.multiple_of(hub_ref[s] * tile, tile), tile), :] += term_ref[s]
    out_ref[...] = acc_ref[...].astype(BF16)


def fetch(pairs, sems):
    copies = [pltpu.make_async_copy(a, b, sems.at[n]) for n, (a, b) in enumerate(pairs)]
    for copy in copies:
        copy.start()
    return copies


def contributions(cores, blocks_ref, back_ref, panel_ref, keep_ref, send_ref):
    me, core = lax.axis_index("row"), lax.axis_index("col")
    hubs = blocks_ref.shape[0]
    tile = back_ref.shape[0] // hubs
    blocks = panel_ref.shape[0] // tile
    per_half = hubs // cores

    def write(ref, half):
        for j in range(per_half):
            hub = half * per_half + j
            place = Place(blocks_ref[hub], blocks, cores)
            out = pl.ds(j * tile, tile)
            row = pl.ds(pl.multiple_of(hub * tile, tile), tile)
            own = pl.ds(pl.multiple_of(place.blk * tile, tile), tile)
            here, near = place.chip == me, place.core == core

            @pl.when(jnp.logical_not(here))
            def _():
                ref[out, :] = back_ref[row, :]

            @pl.when(here & near)
            def _():
                ref[out, :] = panel_ref[own, :]

            @pl.when(here & jnp.logical_not(near))
            def _():
                ref[out, :] = jnp.zeros_like(ref[out, :])

    write(keep_ref, core)
    write(send_ref, 1 - core)


def first_kernel(cores, *refs):
    sources, (panel_ref, back_ref, keep_ref, send_ref, acc_ref) = refs[:5], refs[5:10]
    held, (sems, term_ref) = refs[10:15], refs[15:]
    for copy in fetch(list(zip(sources, held)), sems):
        copy.wait()
    blocks_ref, local_ref, hub_ref, effects_ref, lr_ref = held
    panel_ref[...] = effects_ref[...].astype(BF16)
    back_terms(local_ref, hub_ref, lr_ref, panel_ref, term_ref, acc_ref, back_ref)
    contributions(cores, blocks_ref, back_ref, panel_ref, keep_ref, send_ref)


def merge_kernel(cores, tile, per_chip, blocks_ref, in_ref, *rest):
    *_, out_ref = rest
    me, core = lax.axis_index("row"), lax.axis_index("col")
    chips, rows, _ = in_ref.shape
    hub = (core * (chips * rows) + me * rows) // tile
    owner = blocks_ref[hub] // per_chip

    def add(p, total):
        return total + jnp.where(p == owner, 0.0, in_ref[p].astype(F32))

    def put(p, carry):
        out_ref[p] = jnp.where(p == owner, total, state)
        return carry

    zero = jnp.zeros(in_ref.shape[1:], F32)
    total = lax.fori_loop(0, chips, add, zero, unroll=chips <= 16).astype(BF16)
    state = in_ref[owner]
    lax.fori_loop(0, chips, put, 0, unroll=chips <= 16)


def band_kernel(
    cores,
    blocks_ref,
    local_ref,
    hub_ref,
    current_hbm,
    zscores_hbm,
    ridge_hbm,
    band_hbm,
    mine_hbm,
    other_hbm,
    back_hbm,
    back_other_hbm,
    lr_hbm,
    next_ref,
    chip_ref,
    current_ref,
    zscores_ref,
    ridge_ref,
    band_ref,
    back_ref,
    back_other_ref,
    lr_ref,
    sems,
):
    me, core = lax.axis_index("row"), lax.axis_index("col")
    blocks, width, tile, _ = band_ref.shape
    rows = blocks * tile
    reach = width // 2
    mine = pl.ds(pl.multiple_of(core * rows, rows), rows)
    other = pl.ds(pl.multiple_of((1 - core) * rows, rows), rows)
    copies = fetch(
        [
            (mine_hbm, chip_ref.at[mine]),
            (other_hbm, chip_ref.at[other]),
            (band_hbm, band_ref),
            (current_hbm, current_ref),
            (zscores_hbm, zscores_ref),
            (ridge_hbm, ridge_ref),
            (back_hbm, back_ref),
            (back_other_hbm, back_other_ref),
            (lr_hbm, lr_ref),
        ],
        sems,
    )
    for copy in copies[:3]:
        copy.wait()

    def product(b, at):
        low, high = max(0, at - reach), min(cores * blocks, at + reach + 1)
        tiles = [band_ref[b, c - at + reach] for c in range(low, high)]
        return dot(jnp.concatenate(tiles, axis=1), chip_ref[low * tile : high * tile, :])

    for n in range(cores):

        @pl.when(core == n)
        def _():
            for b in range(blocks):
                next_ref[b * tile : (b + 1) * tile, :] = product(b, n * blocks + b)

    for copy in copies[3:]:
        copy.wait()
    for b in range(blocks):
        out = slice(b * tile, (b + 1) * tile)
        current = current_ref[out, :]
        gradient = next_ref[out, :] + (ridge_ref[...] * current - zscores_ref[out, :])
        next_ref[out, :] = current - STEP * gradient

    for hub in range(blocks_ref.shape[0]):
        place = Place(blocks_ref[hub], blocks, cores)
        row = pl.ds(hub * tile, tile)
        own = pl.ds(pl.multiple_of(place.blk * tile, tile), tile)

        @pl.when((place.chip == me) & (place.core == core))
        def _():
            both = back_ref[row, :].astype(F32) + back_other_ref[row, :].astype(F32)
            next_ref[own, :] -= STEP * both

    for s in range(lr_ref.shape[0]):
        block = blocks_ref[hub_ref[s]]
        row = pl.ds(pl.multiple_of(local_ref[s] * tile, tile), tile)

        @pl.when(Place(block, blocks, cores).chip == me)
        def _():
            at = pl.ds(pl.multiple_of((block - me * (cores * blocks)) * tile, tile), tile)
            next_ref[row, :] -= STEP * dot(lr_ref[s], chip_ref[at, :])


def edge_kernel(
    outer_hbm, band_hbm, partial_hbm, out_hbm, outer_ref, band_ref, partial_ref, out_ref, sems
):
    core = lax.axis_index("col")
    blocks, reach, tile, _ = band_ref.shape
    first = (band_hbm.shape[1] - reach) * core
    for copy in fetch(
        [
            (outer_hbm, outer_ref),
            (band_hbm.at[:, pl.ds(first, reach)], band_ref),
            (partial_hbm, partial_ref),
        ],
        sems,
    ):
        copy.wait()

    def write(b, skip, low, high):
        tiles = [band_ref[b, skip + n] for n in range(high - low)]
        out = pl.ds(b * tile, tile)
        gradient = dot(jnp.concatenate(tiles, axis=1), outer_ref[low * tile : high * tile, :])
        out_ref[out, :] = partial_ref[out, :] - STEP * gradient
        pltpu.make_async_copy(out_ref.at[out], out_hbm.at[out], sems.at[3 + b]).start()

    @pl.when(core == 0)
    def _():
        for b in range(blocks):
            write(b, 0, b, blocks)

    @pl.when(core != 0)
    def _():
        for b in range(blocks):
            write(b, blocks - 1 - b, 0, b + 1)

    for b in range(blocks):
        out = pl.ds(b * tile, tile)
        pltpu.make_async_copy(out_ref.at[out], out_hbm.at[out], sems.at[3 + b]).wait()


def step_kernel(
    cores,
    last,
    blocks_ref,
    local_ref,
    hub_ref,
    lr_ref,
    half_ref,
    half_other_ref,
    partial_hbm,
    *rest,
):
    if last:
        next_hbm, rest = rest[0], rest[1:]
    else:
        (next_hbm, panel_hbm, back_hbm, keep_ref, send_ref), rest = rest[:5], rest[5:]
    partial_ref, panel_ref, state_ref, grad_ref, term_ref, next_ref, sems = rest
    me, core = lax.axis_index("row"), lax.axis_index("col")
    count, tile, _ = lr_ref.shape
    rows = next_ref.shape[0]
    blocks = rows // tile
    hubs = blocks_ref.shape[0]
    half = half_ref.shape[0]
    copies = fetch([(partial_hbm, partial_ref)], sems)
    near = pl.ds(pl.multiple_of(core * half, half), half)
    away = pl.ds(pl.multiple_of((1 - core) * half, half), half)
    state_ref[near, :] = half_ref[...]
    state_ref[away, :] = half_other_ref[...]
    grad_ref[...] = jnp.zeros_like(grad_ref)

    for hub in range(hubs):
        place = Place(blocks_ref[hub], blocks, cores)
        own = pl.ds(pl.multiple_of(place.blk * tile, tile), tile)
        row = pl.ds(hub * tile, tile)

        @pl.when((place.chip == me) & (place.core == core))
        def _():
            grad_ref[own, :] += state_ref[row, :].astype(F32)

        @pl.when(place.chip == me)
        def _():
            state_ref[row, :] = jnp.zeros_like(state_ref[row, :])

    for s in range(count):
        col = pl.ds(pl.multiple_of(hub_ref[s] * tile, tile), tile)
        term_ref[s] = dot(lr_ref[s], state_ref[col, :])
    for s in range(count):
        grad_ref[pl.ds(pl.multiple_of(local_ref[s] * tile, tile), tile), :] += term_ref[s]

    for copy in copies:
        copy.wait()
    done = []
    for b in range(blocks):
        out = pl.ds(b * tile, tile)
        following = partial_ref[out, :] - STEP * grad_ref[out, :]
        next_ref[out, :] = following
        done += fetch([(next_ref.at[out], next_hbm.at[out])], sems.at[pl.ds(2 + b, 1)])
        if not last:
            panel_ref[out, :] = following.astype(BF16)
    if not last:
        back_ref, acc_ref = state_ref, grad_ref
        done += fetch([(panel_ref, panel_hbm)], sems.at[pl.ds(2 + blocks, 1)])
        back_terms(local_ref, hub_ref, lr_ref, panel_ref, term_ref, acc_ref, back_ref)
        done += fetch([(back_ref, back_hbm)], sems.at[pl.ds(3 + blocks, 1)])
        contributions(cores, blocks_ref, back_ref, panel_ref, keep_ref, send_ref)
    for copy in done:
        copy.wait()


def join_kernel(keep_ref, came_ref, out_ref):
    out_ref[...] = (keep_ref[...].astype(F32) + came_ref[...].astype(F32)).astype(BF16)


def shards(rows_dev, cores, effects, zscores, ridge, band, lr, lr_local, lr_hub, hub_blocks):
    blocks, _, tile, _ = band.shape
    rows, traits = effects.shape
    hubs = hub_blocks.shape[0]
    hub_rows = hubs * tile
    half = hub_rows // cores
    total = rows_dev * cores
    panel_type = jax.ShapeDtypeStruct((rows, traits), BF16)
    back_type = jax.ShapeDtypeStruct((hub_rows, traits), BF16)
    ridge = ridge[None, :]

    odd = [(i, i + 1) for i in range(cores - 1, total - 1, cores)]
    odd = odd + [(j, i) for i, j in odd]
    swap = [(0, 1), (1, 0)]

    def other_core(x):
        return lax.ppermute(x, "col", swap)

    def exchange(x):
        x = x.reshape(rows_dev, half // rows_dev, traits)
        return lax.all_to_all(x, "row", 0, 0)

    half_type = jax.ShapeDtypeStruct((half, traits), BF16)
    panels, back, keep, send = pl.pallas_call(
        functools.partial(first_kernel, cores),
        out_shape=(panel_type, back_type, half_type, half_type),
        in_specs=[HBM] * 5,
        out_specs=(VMEM,) * 4,
        scratch_shapes=[
            pltpu.VMEM((hub_rows, traits), F32),
            pltpu.SMEM(hub_blocks.shape, jnp.int32),
            pltpu.SMEM(lr_local.shape, jnp.int32),
            pltpu.SMEM(lr_hub.shape, jnp.int32),
            pltpu.VMEM(effects.shape, F32),
            pltpu.VMEM(lr.shape, BF16),
            pltpu.SemaphoreType.DMA((5,)),
            pltpu.VMEM((lr.shape[0], tile, traits), F32),
        ],
        compiler_params=FIRST,
        name="first",
    )(hub_blocks, lr_local, lr_hub, effects, lr)

    current = effects
    for sweep in range(ITERS):
        last = sweep == ITERS - 1
        outer = lax.ppermute(panels, ("row", "col"), odd)
        came = other_core(send)
        other = other_core(panels)
        back_other = other_core(back)
        chosen = pl.pallas_call(
            join_kernel,
            out_shape=half_type,
            in_specs=[VMEM] * 2,
            out_specs=VMEM,
            compiler_params=MERGE,
            name="join",
        )(keep, came)
        gathered = exchange(chosen)
        merged = pl.pallas_call(
            functools.partial(merge_kernel, cores, tile, blocks * cores),
            out_shape=jax.ShapeDtypeStruct(gathered.shape, BF16),
            in_specs=[SMEM, VMEM, ANY, ANY],
            out_specs=VMEM,
            compiler_params=MERGE,
            name="merge",
        )(hub_blocks, gathered, other, back_other)
        partial = pl.pallas_call(
            functools.partial(band_kernel, cores),
            out_shape=jax.ShapeDtypeStruct((rows, traits), F32),
            in_specs=[SMEM] * 3 + [HBM] * 9,
            out_specs=VMEM,
            scratch_shapes=[
                pltpu.VMEM((cores * rows, traits), BF16),
                pltpu.VMEM(current.shape, F32),
                pltpu.VMEM(zscores.shape, F32),
                pltpu.VMEM(ridge.shape, F32),
                pltpu.VMEM(band.shape, BF16),
                pltpu.VMEM(back.shape, BF16),
                pltpu.VMEM(back.shape, BF16),
                pltpu.VMEM(lr.shape, BF16),
                pltpu.SemaphoreType.DMA((9,)),
            ],
            compiler_params=BAND,
            cost_estimate=pl.CostEstimate(
                flops=10**6, bytes_accessed=2**20, transcendentals=0
            ),
            name="band",
        )(
            hub_blocks,
            lr_local,
            lr_hub,
            current,
            zscores,
            ridge,
            band,
            panels,
            other,
            back,
            back_other,
            lr,
        )
        partial = pl.pallas_call(
            edge_kernel,
            out_shape=jax.ShapeDtypeStruct((rows, traits), F32),
            in_specs=[HBM] * 3,
            out_specs=HBM,
            scratch_shapes=[
                pltpu.VMEM((rows, traits), BF16),
                pltpu.VMEM((blocks, band.shape[1] // 2, tile, tile), BF16),
                pltpu.VMEM((rows, traits), F32),
                pltpu.VMEM((rows, traits), F32),
                pltpu.SemaphoreType.DMA((blocks + 3,)),
            ],
            compiler_params=BAND,
            name="edge",
        )(outer, band, partial)
        mine = exchange(merged).reshape(half, traits)
        mine, partial = lax.optimization_barrier((mine, partial))
        theirs = other_core(mine)
        out_shape, out_specs = [jax.ShapeDtypeStruct((rows, traits), F32)], [HBM]
        if not last:
            out_shape += [panel_type, back_type, half_type, half_type]
            out_specs += [HBM, HBM, VMEM, VMEM]
        result = pl.pallas_call(
            functools.partial(step_kernel, cores, last),
            out_shape=tuple(out_shape),
            in_specs=[SMEM] * 3 + [VMEM] * 3 + [HBM],
            out_specs=tuple(out_specs),
            scratch_shapes=[
                pltpu.VMEM((rows, traits), F32),
                pltpu.VMEM((rows, traits), BF16),
                pltpu.VMEM((hub_rows, traits), BF16),
                pltpu.VMEM((max(rows, hub_rows), traits), F32),
                pltpu.VMEM((lr.shape[0], tile, traits), F32),
                pltpu.VMEM((rows, traits), F32),
                pltpu.SemaphoreType.DMA((blocks + 4,)),
            ],
            compiler_params=UPDATE,
            name="step",
        )(
            hub_blocks,
            lr_local,
            lr_hub,
            lr,
            mine,
            theirs,
            partial,
        )
        if last:
            return result[0]
        current, panels, back, keep, send = result


def solution(mesh):
    every = ("groups", "row", "col")
    placed = (
        P(every, None),
        P(every, None),
        P("groups"),
        P(every, None, None, None),
        P(every, None, None),
        P(every),
        P(every),
        P("groups"),
    )
    return jax.shard_map(
        functools.partial(shards, mesh.shape["row"], mesh.shape["col"]),
        mesh=mesh,
        in_specs=placed,
        out_specs=P(every, None),
        check_vma=False,
    )
```

time: 86.2 us -> 79 us (0.916)
  waiting for transfers between devices: 32.7 us -> 22 us
  Pallas kernels: 23.8 us -> 28.9 us
  local copies, waits for them, and re-layouts: 7.64 us -> 2.6 us
  starting transfers between devices: 21 us -> 24.5 us
    all_to_all x4, waiting for transfers between devices: 26.5 us -> 17.2 us  [exchange(): return lax.all_to_all(x, 'row', 0, 0)]
    unnamed x42 -> x36, local copies, waits for them, and re-layouts: 7.64 us -> 2.6 us
    pallas_call x5 -> x7, Pallas kernels: 16.9 us -> 19.7 us  [the longest x2 9.39 us: shards(): pl.pallas_call(functools.partial(band_kernel, cores), out_shape=jax.Shape...]
    all_to_all x4, starting transfers between devices: 18.6 us -> 21.2 us  [exchange(): return lax.all_to_all(x, 'row', 0, 0)]
    pallas_call x2, Pallas kernels: 4.22 us -> 6.51 us  [shards(): pl.pallas_call(functools.partial(step_kernel, cores, last), out_shape=tup...]
    ppermute x6 -> x8, waiting for transfers between devices: 6.25 us -> 4.81 us  [other_core(): return lax.ppermute(x, 'col', swap)]
    ppermute x6 -> x8, starting transfers between devices: 1.11 us -> 1.88 us  [other_core(): return lax.ppermute(x, 'col', swap)]
  transfers between devices with their start and end apart: 12 -> 14, of which waited for: 10 -> 6; matrix products, arithmetic and copies ran while one was open for 0% -> 0% of each run, Pallas kernels for 17% -> 25%
where the time goes in v3:
time: 79 us; the launch traced here: 78.2 us
  Pallas kernels  28.9 us (37%)
  starting transfers between devices  24.5 us (31%)
  waiting for transfers between devices  22 us (28%)
  local copies, waits for them, and re-layouts  2.6 us (3%)
    all_to_all x4, starting transfers between devices, exchange(): return lax.all_to_all(x, 'row', 0, 0)  21.2 us
    all_to_all x4, waiting for transfers between devices, exchange(): return lax.all_to_all(x, 'row', 0, 0)  17.2 us
    pallas_call x2, Pallas kernels, shards(): pl.pallas_call(functools.partial(band_kernel, cores), out_shape=jax.Shape...  9.39 us
    pallas_call x2, Pallas kernels, shards(): pl.pallas_call(functools.partial(step_kernel, cores, last), out_shape=tup...  6.51 us
    pallas_call x2, Pallas kernels, shards(): pl.pallas_call(edge_kernel, out_shape=jax.ShapeDtypeStruct((rows, traits)...  5.63 us
    ppermute x8, waiting for transfers between devices, other_core(): return lax.ppermute(x, 'col', swap)  4.81 us
    pallas_call x1, Pallas kernels, shards(): pl.pallas_call(functools.partial(first_kernel, cores), out_shape=(panel_t...  3.16 us
    pallas_call x2, Pallas kernels, shards(): pl.pallas_call(functools.partial(merge_kernel, cores, tile, blocks * core...  2.67 us
  transfers between devices with their start and end apart: 14, of which 6 were waited for; matrix products, arithmetic and copies ran while one was open for 0% of the time, Pallas kernels for 25%

profile of v3, /device:TPU:0, one launch (start us, length us, event | category | flops | bytes accessed | tf_op | source)
XLA Modules:
  0.0 78.2 jit_solution(15432874931621460255)
XLA Ops:
  0.0 3.2 %first.1 = (bf16[512,512]{1,0:T(8,128)(2,1)}, bf16[512,512]{1,0:T(8,128)(2,1)}, bf16[256,512]{1,0:T(8,128)(2,1)}, bf16[256,512]{1,0:T(8,128)(2,1)}) custom-call(s32[4]{0:T(128)} %blocks_ref.11, s32[8]{0:T(128)} %local_ref.7, s32[8]{0:T(128)} %hub_ref.7, f32[512,512]{1,0:T(8,128)} %current_hbm.1, bf16[8,128,128]{2,1,0:T(8,128)(2,1)} %lr_ref.3), custom_call_target="tpu_custom_call" | custom-call | tf_op jit(solution)/shard_map/first/pallas_call | solution.py:342
  3.2 0.5 collective-permute-start
  3.7 0.1 collective-permute-start.1
  3.8 0.4 collective-permute-start.2
  4.2 0.9 %collective-permute-done.came_ref = bf16[256,512]{1,0:T(8,128)(2,1)S(1)} collective-permute-done((bf16[256,512]{1,0:T(8,128)(2,1)}, bf16[256,512]{1,0:T(8,128)(2,1)S(1)}, u32[]{:S(2)}, u32[]{:S(2)}) %collective-permute-start) | collective-permute-done | bytes 262176 | tf_op jit(solution)/shard_map/ppermute | solution.py:335
  5.1 0.9 %copy-done.6 = bf16[256,512]{1,0:T(8,128)(2,1)S(1)} copy-done((bf16[256,512]{1,0:T(8,128)(2,1)S(1)}, bf16[256,512]{1,0:T(8,128)(2,1)}, u32[]{:S(2)}) %copy-start.6) | copy-done | bytes 262168
  6.0 0.8 join.2
  6.8 7.2 %all-to-all-start = ((bf16[8,32,512]{2,1,0:T(8,128)(2,1)}), bf16[8,32,512]{2,1,0:T(8,128)(2,1)S(1)}, u32[]{:S(2)}, u32[]{:S(2)}) async-start(bf16[8,32,512]{2,1,0:T(8,128)(2,1)} %bitcast), calls=%async_computation | async-start | bytes 524288 | tf_op jit(solution)/shard_map/all_to_all | solution.py:339
  14.0 0.0 copy-done.15
  14.0 0.7 collective-permute-start.3
  14.7 0.0 collective-permute-done.1.rest_0_.other_hbm
  14.7 0.0 copy-start.3
  14.7 0.0 collective-permute-done.2.rest_1_.back_other_hbm
  14.7 0.0 copy-start.5
  14.7 8.6 %all-to-all-done.in_ref = bf16[8,32,512]{2,1,0:T(8,128)(2,1)S(1)} async-done(((bf16[8,32,512]{2,1,0:T(8,128)(2,1)}), bf16[8,32,512]{2,1,0:T(8,128)(2,1)S(1)}, u32[]{:S(2)}, u32[]{:S(2)}) %all-to-all-start) | async-done | bytes 262176 | tf_op jit(solution)/shard_map/all_to_all | solution.py:339
  23.3 0.0 copy-done.7
  23.3 1.3 %merge.2 = bf16[8,32,512]{2,1,0:T(8,128)(2,1)} custom-call(s32[4]{0:T(128)S(1)} %copy-done.7, bf16[8,32,512]{2,1,0:T(8,128)(2,1)S(1)} %all-to-all-done.in_ref, bf16[512,512]{1,0:T(8,128)(2,1)S(1)} %collective-permute-done.1.rest_0_.other_hbm, bf16[512,512]{1,0:T(8,128)(2,1)S(1)} %collective-permute-done.2.rest_1_.back_other_hbm), custom_call_target="tpu_custom_call" | custom-call | tf_op jit(solution)/shard_map/merge/pallas_call | solution.py:377
  24.6 3.8 %all-to-all-start.1 = ((bf16[8,32,512]{2,1,0:T(8,128)(2,1)}), bf16[8,32,512]{2,1,0:T(8,128)(2,1)S(1)}, u32[]{:S(2)}, u32[]{:S(2)}) async-start(bf16[8,32,512]{2,1,0:T(8,128)(2,1)} %merge.2), calls=%async_computation.1 | async-start | bytes 524288 | tf_op jit(solution)/shard_map/all_to_all | solution.py:339
  28.5 0.0 copy-done.3
  28.5 0.0 copy-done.5
  28.5 4.7 %band.2.partial_hbm = f32[512,512]{1,0:T(8,128)} custom-call(s32[4]{0:T(128)} %blocks_ref.11, s32[8]{0:T(128)} %local_ref.7, s32[8]{0:T(128)} %hub_ref.7, f32[512,512]{1,0:T(8,128)} %current_hbm.1, f32[512,512]{1,0:T(8,128)} %zscores_hbm.3, f32[1,512]{1,0:T(1,128)} %bitcast.9, bf16[4,9,128,128]{3,2,1,0:T(8,128)(2,1)} %band_hbm.7, ...), custom_call_target="tpu_custom_call" | custom-call | flops 1000000 | bytes 1048576 | tf_op jit(solution)/shard_map/band/pallas_call | solution.py:385
  33.2 0.0 copy-start
  33.2 0.0 copy-start.8
  33.2 0.0 copy-start.10
  33.2 0.0 copy-start.12
  33.2 0.0 collective-permute-done.3.outer_hbm
  33.2 0.0 copy-start.17
  33.3 0.8 copy-done.17
  34.0 2.8 %edge.2.partial_hbm = f32[512,512]{1,0:T(8,128)} custom-call(bf16[512,512]{1,0:T(8,128)(2,1)} %copy-done.17, bf16[4,9,128,128]{3,2,1,0:T(8,128)(2,1)} %band_hbm.7, f32[512,512]{1,0:T(8,128)} %band.2.partial_hbm), custom_call_target="tpu_custom_call" | custom-call | tf_op jit(solution)/shard_map/edge/pallas_call | solution.py:420
  36.9 0.0 all-to-all-done.1
  36.9 0.1 collective-permute-start.4
  37.0 1.5 %collective-permute-done.4.half_other_ref = bf16[256,512]{1,0:T(8,128)(2,1)S(1)} collective-permute-done((bf16[256,512]{1,0:T(8,128)(2,1)S(1)}, bf16[256,512]{1,0:T(8,128)(2,1)S(1)}, u32[]{:S(2)}, u32[]{:S(2)}) %collective-permute-start.4) | collective-permute-done | bytes 262176 | tf_op jit(solution)/shard_map/ppermute | solution.py:335
  38.5 0.0 copy-done
  38.5 0.0 copy-done.8
  38.5 0.0 copy-done.10
  38.5 0.0 copy-done.12
  38.5 3.7 %step.2 = (f32[512,512]{1,0:T(8,128)}, bf16[512,512]{1,0:T(8,128)(2,1)}, bf16[512,512]{1,0:T(8,128)(2,1)}, bf16[256,512]{1,0:T(8,128)(2,1)S(1)}, bf16[256,512]{1,0:T(8,128)(2,1)S(1)}) custom-call(s32[4]{0:T(128)S(1)} %copy-done.8, s32[8]{0:T(128)S(1)} %copy-done.10, s32[8]{0:T(128)S(1)} %copy-done.12, bf16[8,128,128]{2,1,0:T(8,128)(2,1)S(1)} %copy-done, ...), custom_call_target="tpu_custom_call" | custom-call | tf_op jit(solution)/shard_map/step/pallas_call | solution.py:442
  42.2 0.0 copy-start.14
  42.2 0.2 collective-permute-start.5
  42.4 0.4 collective-permute-start.6
  42.8 0.1 collective-permute-start.7
  42.9 0.9 %collective-permute-done.5.came_ref = bf16[256,512]{1,0:T(8,128)(2,1)S(1)} collective-permute-done((bf16[256,512]{1,0:T(8,128)(2,1)S(1)}, bf16[256,512]{1,0:T(8,128)(2,1)S(1)}, u32[]{:S(2)}, u32[]{:S(2)}) %collective-permute-start.5) | collective-permute-done | bytes 262176 | tf_op jit(solution)/shard_map/ppermute | solution.py:335
  43.8 0.8 join.3
  44.5 6.3 %all-to-all-start.2 = ((bf16[8,32,512]{2,1,0:T(8,128)(2,1)}), bf16[8,32,512]{2,1,0:T(8,128)(2,1)S(1)}, u32[]{:S(2)}, u32[]{:S(2)}) async-start(bf16[8,32,512]{2,1,0:T(8,128)(2,1)} %bitcast.3), calls=%async_computation.2 | async-start | bytes 524288 | tf_op jit(solution)/shard_map/all_to_all | solution.py:339
  50.9 0.0 copy-done.14
  50.9 0.7 collective-permute-start.8
  51.6 0.0 collective-permute-done.6.rest_0_.other_hbm
  51.6 0.0 collective-permute-done.7.rest_1_.back_other_hbm
  51.6 8.6 %all-to-all-done.2.in_ref = bf16[8,32,512]{2,1,0:T(8,128)(2,1)S(1)} async-done(((bf16[8,32,512]{2,1,0:T(8,128)(2,1)}), bf16[8,32,512]{2,1,0:T(8,128)(2,1)S(1)}, u32[]{:S(2)}, u32[]{:S(2)}) %all-to-all-start.2) | async-done | bytes 262176 | tf_op jit(solution)/shard_map/all_to_all | solution.py:339
  60.2 1.3 %merge.3 = bf16[8,32,512]{2,1,0:T(8,128)(2,1)} custom-call(s32[4]{0:T(128)S(1)} %copy-done.8, bf16[8,32,512]{2,1,0:T(8,128)(2,1)S(1)} %all-to-all-done.2.in_ref, bf16[512,512]{1,0:T(8,128)(2,1)S(1)} %collective-permute-done.6.rest_0_.other_hbm, bf16[512,512]{1,0:T(8,128)(2,1)S(1)} %collective-permute-done.7.rest_1_.back_other_hbm), custom_call_target="tpu_custom_call" | custom-call | tf_op jit(solution)/shard_map/merge/pallas_call | solution.py:377
  61.5 3.8 %all-to-all-start.3 = ((bf16[8,32,512]{2,1,0:T(8,128)(2,1)}), bf16[8,32,512]{2,1,0:T(8,128)(2,1)S(1)}, u32[]{:S(2)}, u32[]{:S(2)}) async-start(bf16[8,32,512]{2,1,0:T(8,128)(2,1)} %merge.3), calls=%async_computation.3 | async-start | bytes 524288 | tf_op jit(solution)/shard_map/all_to_all | solution.py:339
  65.4 4.7 %band.3.partial_hbm = f32[512,512]{1,0:T(8,128)} custom-call(s32[4]{0:T(128)} %blocks_ref.11, s32[8]{0:T(128)} %local_ref.7, s32[8]{0:T(128)} %hub_ref.7, f32[512,512]{1,0:T(8,128)} %get-tuple-element.28.current_hbm, f32[512,512]{1,0:T(8,128)} %zscores_hbm.3, f32[1,512]{1,0:T(1,128)} %bitcast.10, bf16[4,9,128,128]{3,2,1,0:T(8,128)(2,1)} %band_hbm.7, ...), custom_call_target="tpu_custom_call" | custom-call | flops 1000000 | bytes 1048576 | tf_op jit(solution)/shard_map/band/pallas_call | solution.py:385
  70.1 0.0 copy-start.1
  70.1 0.0 copy-start.9
  70.1 0.0 copy-start.11
  70.1 0.0 copy-start.13
  70.1 0.0 collective-permute-done.8.outer_hbm
  70.2 0.0 copy-start.16
  70.2 0.8 %copy-done.16 = bf16[512,512]{1,0:T(8,128)(2,1)} copy-done((bf16[512,512]{1,0:T(8,128)(2,1)}, bf16[512,512]{1,0:T(8,128)(2,1)S(1)}, u32[]{:S(2)}) %copy-start.16) | copy-done | bytes 524312
  71.0 2.8 %edge.3.partial_hbm = f32[512,512]{1,0:T(8,128)} custom-call(bf16[512,512]{1,0:T(8,128)(2,1)} %copy-done.16, bf16[4,9,128,128]{3,2,1,0:T(8,128)(2,1)} %band_hbm.7, f32[512,512]{1,0:T(8,128)} %band.3.partial_hbm), custom_call_target="tpu_custom_call" | custom-call | tf_op jit(solution)/shard_map/edge/pallas_call | solution.py:420
  73.8 0.0 all-to-all-done.3
  73.8 0.1 collective-permute-start.9
  73.9 1.5 %collective-permute-done.9.half_other_ref = bf16[256,512]{1,0:T(8,128)(2,1)S(1)} collective-permute-done((bf16[256,512]{1,0:T(8,128)(2,1)S(1)}, bf16[256,512]{1,0:T(8,128)(2,1)S(1)}, u32[]{:S(2)}, u32[]{:S(2)}) %collective-permute-start.9) | collective-permute-done | bytes 262176 | tf_op jit(solution)/shard_map/ppermute | solution.py:335
  75.4 2.8 %step.3 = f32[512,512]{1,0:T(8,128)} custom-call(s32[4]{0:T(128)S(1)} %copy-done.9, s32[8]{0:T(128)S(1)} %copy-done.11, s32[8]{0:T(128)S(1)} %copy-done.13, bf16[8,128,128]{2,1,0:T(8,128)(2,1)S(1)} %copy-done.1, bf16[256,512]{1,0:T(8,128)(2,1)S(1)} %bitcast.6, bf16[256,512]{1,0:T(8,128)(2,1)S(1)} %collective-permute-done.9.half_other_ref, ...), custom_call_target="tpu_custom_call" | custom-call | tf_op jit(solution)/shard_map/step/pallas_call | solution.py:442
  (11 shorter events, 0.0 us)
Async XLA Ops:
  0.0 23.3 %copy-start.7 = (s32[4]{0:T(128)S(1)}, s32[4]{0:T(128)}, u32[]{:S(2)}) copy-start(s32[4]{0:T(128)} %blocks_ref.11) | copy-start | bytes 52
  3.2 1.9 %collective-permute-start = (bf16[256,512]{1,0:T(8,128)(2,1)}, bf16[256,512]{1,0:T(8,128)(2,1)S(1)}, u32[]{:S(2)}, u32[]{:S(2)}) collective-permute-start(bf16[256,512]{1,0:T(8,128)(2,1)} %get-tuple-element.19), channel_id=1, source_target_pairs={{0,1},{1,0},{2,3},{3,2},{4,5},{5,4},{6,7},{7,6},{8,9},{9,8},{10,11... | collective-permute-start | bytes 786440 | tf_op jit(solution)/shard_map/ppermute | solution.py:335
  3.7 11.0 %collective-permute-start.1 = (bf16[512,512]{1,0:T(8,128)(2,1)}, bf16[512,512]{1,0:T(8,128)(2,1)S(1)}, u32[]{:S(2)}, u32[]{:S(2)}) collective-permute-start(bf16[512,512]{1,0:T(8,128)(2,1)} %get-tuple-element.20.mine_hbm), channel_id=1, source_target_pairs={{0,1},{1,0},{2,3},{3,2},{4,5},{5,4},{6,7},{7,6},{8,9},{9,8},{10,11... | collective-permute-start | bytes 1572872 | tf_op jit(solution)/shard_map/ppermute | solution.py:335
  3.8 10.9 %collective-permute-start.2 = (bf16[512,512]{1,0:T(8,128)(2,1)}, bf16[512,512]{1,0:T(8,128)(2,1)S(1)}, u32[]{:S(2)}, u32[]{:S(2)}) collective-permute-start(bf16[512,512]{1,0:T(8,128)(2,1)} %get-tuple-element.21.back_hbm), channel_id=1, source_target_pairs={{0,1},{1,0},{2,3},{3,2},{4,5},{5,4},{6,7},{7,6},{8,9},{9,8},{10,11... | collective-permute-start | bytes 1572872 | tf_op jit(solution)/shard_map/ppermute | solution.py:335
  5.1 0.9 %copy-start.6 = (bf16[256,512]{1,0:T(8,128)(2,1)S(1)}, bf16[256,512]{1,0:T(8,128)(2,1)}, u32[]{:S(2)}) copy-start(bf16[256,512]{1,0:T(8,128)(2,1)} %get-tuple-element.18.keep_ref) | copy-start | bytes 786436
  6.0 7.9 %copy-start.15 = (bf16[512,512]{1,0:T(8,128)(2,1)S(1)}, bf16[512,512]{1,0:T(8,128)(2,1)}, u32[]{:S(2)}) copy-start(bf16[512,512]{1,0:T(8,128)(2,1)} %get-tuple-element.20.mine_hbm) | copy-start | bytes 1572868
  6.8 16.5 %all-to-all-start = ((bf16[8,32,512]{2,1,0:T(8,128)(2,1)}), bf16[8,32,512]{2,1,0:T(8,128)(2,1)S(1)}, u32[]{:S(2)}, u32[]{:S(2)}) async-start(bf16[8,32,512]{2,1,0:T(8,128)(2,1)} %bitcast), calls=%async_computation | async-start | bytes 524288 | tf_op jit(solution)/shard_map/all_to_all | solution.py:339
  14.0 19.3 %collective-permute-start.3 = (bf16[512,512]{1,0:T(8,128)(2,1)S(1)}, bf16[512,512]{1,0:T(8,128)(2,1)S(1)}, u32[]{:S(2)}, u32[]{:S(2)}) collective-permute-start(bf16[512,512]{1,0:T(8,128)(2,1)S(1)} %copy-done.15), channel_id=1, source_target_pairs={{1,2},{3,4},{5,6},{7,8},{9,10},{11,12},{13,14},{2,1},{4,3},{6,5},{... | collective-permute-start | bytes 1572872 | tf_op jit(solution)/shard_map/ppermute | solution.py:364
  14.7 13.8 %copy-start.3 = (bf16[512,512]{1,0:T(8,128)(2,1)}, bf16[512,512]{1,0:T(8,128)(2,1)S(1)}, u32[]{:S(2)}) copy-start(bf16[512,512]{1,0:T(8,128)(2,1)S(1)} %collective-permute-done.1.rest_0_.other_hbm) | copy-start | bytes 1572868
  14.7 13.8 %copy-start.5 = (bf16[512,512]{1,0:T(8,128)(2,1)}, bf16[512,512]{1,0:T(8,128)(2,1)S(1)}, u32[]{:S(2)}) copy-start(bf16[512,512]{1,0:T(8,128)(2,1)S(1)} %collective-permute-done.2.rest_1_.back_other_hbm) | copy-start | bytes 1572868
  24.6 12.2 %all-to-all-start.1 = ((bf16[8,32,512]{2,1,0:T(8,128)(2,1)}), bf16[8,32,512]{2,1,0:T(8,128)(2,1)S(1)}, u32[]{:S(2)}, u32[]{:S(2)}) async-start(bf16[8,32,512]{2,1,0:T(8,128)(2,1)} %merge.2), calls=%async_computation.1 | async-start | bytes 524288 | tf_op jit(solution)/shard_map/all_to_all | solution.py:339
  33.2 5.3 %copy-start = (bf16[8,128,128]{2,1,0:T(8,128)(2,1)S(1)}, bf16[8,128,128]{2,1,0:T(8,128)(2,1)}, u32[]{:S(2)}) copy-start(bf16[8,128,128]{2,1,0:T(8,128)(2,1)} %lr_ref.3) | copy-start | bytes 786436
  33.2 5.3 %copy-start.8 = (s32[4]{0:T(128)S(1)}, s32[4]{0:T(128)}, u32[]{:S(2)}) copy-start(s32[4]{0:T(128)} %blocks_ref.11) | copy-start | bytes 52
  33.2 5.3 %copy-start.10 = (s32[8]{0:T(128)S(1)}, s32[8]{0:T(128)}, u32[]{:S(2)}) copy-start(s32[8]{0:T(128)} %local_ref.7) | copy-start | bytes 100
  33.2 5.3 %copy-start.12 = (s32[8]{0:T(128)S(1)}, s32[8]{0:T(128)}, u32[]{:S(2)}) copy-start(s32[8]{0:T(128)} %hub_ref.7) | copy-start | bytes 100
  33.2 0.8 %copy-start.17 = (bf16[512,512]{1,0:T(8,128)(2,1)}, bf16[512,512]{1,0:T(8,128)(2,1)S(1)}, u32[]{:S(2)}) copy-start(bf16[512,512]{1,0:T(8,128)(2,1)S(1)} %collective-permute-done.3.outer_hbm) | copy-start | bytes 1572868
  36.9 1.6 %collective-permute-start.4 = (bf16[256,512]{1,0:T(8,128)(2,1)S(1)}, bf16[256,512]{1,0:T(8,128)(2,1)S(1)}, u32[]{:S(2)}, u32[]{:S(2)}) collective-permute-start(bf16[256,512]{1,0:T(8,128)(2,1)S(1)} %bitcast.7), channel_id=1, source_target_pairs={{0,1},{1,0},{2,3},{3,2},{4,5},{5,4},{6,7},{7,6},{8,9},{9,8},{10,11... | collective-permute-start | bytes 786440 | tf_op jit(solution)/shard_map/ppermute | solution.py:335
  42.2 8.7 %copy-start.14 = (bf16[512,512]{1,0:T(8,128)(2,1)S(1)}, bf16[512,512]{1,0:T(8,128)(2,1)}, u32[]{:S(2)}) copy-start(bf16[512,512]{1,0:T(8,128)(2,1)} %get-tuple-element.26.mine_hbm) | copy-start | bytes 1572868
  42.2 1.6 %collective-permute-start.5 = (bf16[256,512]{1,0:T(8,128)(2,1)S(1)}, bf16[256,512]{1,0:T(8,128)(2,1)S(1)}, u32[]{:S(2)}, u32[]{:S(2)}) collective-permute-start(bf16[256,512]{1,0:T(8,128)(2,1)S(1)} %get-tuple-element.25), channel_id=1, source_target_pairs={{0,1},{1,0},{2,3},{3,2},{4,5},{5,4},{6,7},{7,6},{8,9},{9,8},{10,11... | collective-permute-start | bytes 786440 | tf_op jit(solution)/shard_map/ppermute | solution.py:335
  42.4 9.2 %collective-permute-start.6 = (bf16[512,512]{1,0:T(8,128)(2,1)}, bf16[512,512]{1,0:T(8,128)(2,1)S(1)}, u32[]{:S(2)}, u32[]{:S(2)}) collective-permute-start(bf16[512,512]{1,0:T(8,128)(2,1)} %get-tuple-element.26.mine_hbm), channel_id=1, source_target_pairs={{0,1},{1,0},{2,3},{3,2},{4,5},{5,4},{6,7},{7,6},{8,9},{9,8},{10,11... | collective-permute-start | bytes 1572872 | tf_op jit(solution)/shard_map/ppermute | solution.py:335
  42.8 8.8 %collective-permute-start.7 = (bf16[512,512]{1,0:T(8,128)(2,1)}, bf16[512,512]{1,0:T(8,128)(2,1)S(1)}, u32[]{:S(2)}, u32[]{:S(2)}) collective-permute-start(bf16[512,512]{1,0:T(8,128)(2,1)} %get-tuple-element.27.back_hbm), channel_id=1, source_target_pairs={{0,1},{1,0},{2,3},{3,2},{4,5},{5,4},{6,7},{7,6},{8,9},{9,8},{10,11... | collective-permute-start | bytes 1572872 | tf_op jit(solution)/shard_map/ppermute | solution.py:335
  44.5 15.7 %all-to-all-start.2 = ((bf16[8,32,512]{2,1,0:T(8,128)(2,1)}), bf16[8,32,512]{2,1,0:T(8,128)(2,1)S(1)}, u32[]{:S(2)}, u32[]{:S(2)}) async-start(bf16[8,32,512]{2,1,0:T(8,128)(2,1)} %bitcast.3), calls=%async_computation.2 | async-start | bytes 524288 | tf_op jit(solution)/shard_map/all_to_all | solution.py:339
  50.9 19.3 %collective-permute-start.8 = (bf16[512,512]{1,0:T(8,128)(2,1)S(1)}, bf16[512,512]{1,0:T(8,128)(2,1)S(1)}, u32[]{:S(2)}, u32[]{:S(2)}) collective-permute-start(bf16[512,512]{1,0:T(8,128)(2,1)S(1)} %copy-done.14), channel_id=1, source_target_pairs={{1,2},{3,4},{5,6},{7,8},{9,10},{11,12},{13,14},{2,1},{4,3},{6,5},{... | collective-permute-start | bytes 1572872 | tf_op jit(solution)/shard_map/ppermute | solution.py:364
  51.6 13.8 %copy-start.2 = (bf16[512,512]{1,0:T(8,128)(2,1)}, bf16[512,512]{1,0:T(8,128)(2,1)S(1)}, u32[]{:S(2)}) copy-start(bf16[512,512]{1,0:T(8,128)(2,1)S(1)} %collective-permute-done.6.rest_0_.other_hbm) | copy-start | bytes 1572868
  51.6 13.8 %copy-start.4 = (bf16[512,512]{1,0:T(8,128)(2,1)}, bf16[512,512]{1,0:T(8,128)(2,1)S(1)}, u32[]{:S(2)}) copy-start(bf16[512,512]{1,0:T(8,128)(2,1)S(1)} %collective-permute-done.7.rest_1_.back_other_hbm) | copy-start | bytes 1572868
  61.5 12.2 %all-to-all-start.3 = ((bf16[8,32,512]{2,1,0:T(8,128)(2,1)}), bf16[8,32,512]{2,1,0:T(8,128)(2,1)S(1)}, u32[]{:S(2)}, u32[]{:S(2)}) async-start(bf16[8,32,512]{2,1,0:T(8,128)(2,1)} %merge.3), calls=%async_computation.3 | async-start | bytes 524288 | tf_op jit(solution)/shard_map/all_to_all | solution.py:339
  70.1 5.3 %copy-start.1 = (bf16[8,128,128]{2,1,0:T(8,128)(2,1)S(1)}, bf16[8,128,128]{2,1,0:T(8,128)(2,1)}, u32[]{:S(2)}) copy-start(bf16[8,128,128]{2,1,0:T(8,128)(2,1)} %lr_ref.3) | copy-start | bytes 786436
  70.1 5.3 %copy-start.9 = (s32[4]{0:T(128)S(1)}, s32[4]{0:T(128)}, u32[]{:S(2)}) copy-start(s32[4]{0:T(128)} %blocks_ref.11) | copy-start | bytes 52
  70.1 5.3 %copy-start.11 = (s32[8]{0:T(128)S(1)}, s32[8]{0:T(128)}, u32[]{:S(2)}) copy-start(s32[8]{0:T(128)} %local_ref.7) | copy-start | bytes 100
  70.1 5.3 %copy-start.13 = (s32[8]{0:T(128)S(1)}, s32[8]{0:T(128)}, u32[]{:S(2)}) copy-start(s32[8]{0:T(128)} %hub_ref.7) | copy-start | bytes 100
  70.2 0.8 %copy-start.16 = (bf16[512,512]{1,0:T(8,128)(2,1)}, bf16[512,512]{1,0:T(8,128)(2,1)S(1)}, u32[]{:S(2)}) copy-start(bf16[512,512]{1,0:T(8,128)(2,1)S(1)} %collective-permute-done.8.outer_hbm) | copy-start | bytes 1572868
  73.8 1.6 %collective-permute-start.9 = (bf16[256,512]{1,0:T(8,128)(2,1)S(1)}, bf16[256,512]{1,0:T(8,128)(2,1)S(1)}, u32[]{:S(2)}, u32[]{:S(2)}) collective-permute-start(bf16[256,512]{1,0:T(8,128)(2,1)S(1)} %bitcast.5), channel_id=1, source_target_pairs={{0,1},{1,0},{2,3},{3,2},{4,5},{5,4},{6,7},{7,6},{8,9},{9,8},{10,11... | collective-permute-start | bytes 786440 | tf_op jit(solution)/shard_map/ppermute | solution.py:335

commit v4 on v3

--- a/solution.py
+++ b/solution.py
@@ -14,6 +14,7 @@
 FIRST = pltpu.CompilerParams(vmem_limit_bytes=58 * 2**20)
 MERGE = pltpu.CompilerParams(vmem_limit_bytes=12 * 2**20)
 BAND = pltpu.CompilerParams(vmem_limit_bytes=58 * 2**20)
+EDGE = pltpu.CompilerParams(vmem_limit_bytes=54500 * 2**10)
 UPDATE = pltpu.CompilerParams(vmem_limit_bytes=53850 * 2**10)
 VMEM = pl.BlockSpec(memory_space=pltpu.VMEM)
 HBM = pl.BlockSpec(memory_space=pltpu.HBM)
@@ -27,6 +28,16 @@
 
 def dot_t(a, b):
     return lax.dot_general(a, b, (((0,), (0,)), ((), ())), preferred_element_type=F32)
+
+
+ORDERS = {8: (1, 6, 0, 2, 5, 4, 3, 7)}
+
+
+def position(chip, chips):
+    order = ORDERS.get(chips)
+    if order is None:
+        return chip
+    return sum(jnp.where(chip == c, p, 0) for p, c in enumerate(order))
 
 
 class Place:
@@ -101,8 +112,8 @@
     *_, out_ref = rest
     me, core = lax.axis_index("row"), lax.axis_index("col")
     chips, rows, _ = in_ref.shape
-    hub = (core * (chips * rows) + me * rows) // tile
-    owner = blocks_ref[hub] // per_chip
+    hub = (core * (chips * rows) + position(me, chips) * rows) // tile
+    owner = position(blocks_ref[hub] // per_chip, chips)
 
     def add(p, total):
         return total + jnp.where(p == owner, 0.0, in_ref[p].astype(F32))
@@ -131,7 +142,7 @@
     back_hbm,
     back_other_hbm,
     lr_hbm,
-    next_ref,
+    next_hbm,
     chip_ref,
     current_ref,
     zscores_ref,
@@ -140,29 +151,52 @@
     back_ref,
     back_other_ref,
     lr_ref,
+    next_ref,
     sems,
 ):
     me, core = lax.axis_index("row"), lax.axis_index("col")
     blocks, width, tile, _ = band_ref.shape
     rows = blocks * tile
     reach = width // 2
+    hubs = blocks_ref.shape[0]
     mine = pl.ds(pl.multiple_of(core * rows, rows), rows)
     other = pl.ds(pl.multiple_of((1 - core) * rows, rows), rows)
-    copies = fetch(
-        [
-            (mine_hbm, chip_ref.at[mine]),
-            (other_hbm, chip_ref.at[other]),
-            (band_hbm, band_ref),
-            (current_hbm, current_ref),
-            (zscores_hbm, zscores_ref),
-            (ridge_hbm, ridge_ref),
-            (back_hbm, back_ref),
-            (back_other_hbm, back_other_ref),
-            (lr_hbm, lr_ref),
-        ],
-        sems,
-    )
-    for copy in copies[:3]:
+    ahead = [
+        (mine_hbm, chip_ref.at[mine]),
+        (other_hbm, chip_ref.at[other]),
+        (band_hbm, band_ref),
+    ]
+    behind = [
+        (current_hbm, current_ref),
+        (zscores_hbm, zscores_ref),
+        (ridge_hbm, ridge_ref),
+        (lr_hbm, lr_ref),
+    ]
+    extra, store = len(ahead) + len(behind), len(ahead) + len(behind) + 2 * hubs
+    early = fetch(ahead, sems)
+    late = fetch(behind, sems.at[pl.ds(len(ahead), len(behind))])
+
+    def owned(hub):
+        place = Place(blocks_ref[hub], blocks, cores)
+        return (place.chip == me) & (place.core == core), place.blk
+
+    def sums(hub):
+        row = pl.ds(hub * tile, tile)
+        return [
+            pltpu.make_async_copy(back_hbm.at[row], back_ref.at[row], sems.at[extra + 2 * hub]),
+            pltpu.make_async_copy(
+                back_other_hbm.at[row], back_other_ref.at[row], sems.at[extra + 2 * hub + 1]
+            ),
+        ]
+
+    for hub in range(hubs):
+
+        @pl.when(owned(hub)[0])
+        def _():
+            for copy in sums(hub):
+                copy.start()
+
+    for copy in early:
         copy.wait()
 
     def product(b, at):
@@ -177,7 +211,7 @@
             for b in range(blocks):
                 next_ref[b * tile : (b + 1) * tile, :] = product(b, n * blocks + b)
 
-    for copy in copies[3:]:
+    for copy in late:
         copy.wait()
     for b in range(blocks):
         out = slice(b * tile, (b + 1) * tile)
@@ -185,13 +219,15 @@
         gradient = next_ref[out, :] + (ridge_ref[...] * current - zscores_ref[out, :])
         next_ref[out, :] = current - STEP * gradient
 
-    for hub in range(blocks_ref.shape[0]):
-        place = Place(blocks_ref[hub], blocks, cores)
+    for hub in range(hubs):
+        here, blk = owned(hub)
         row = pl.ds(hub * tile, tile)
-        own = pl.ds(pl.multiple_of(place.blk * tile, tile), tile)
-
-        @pl.when((place.chip == me) & (place.core == core))
+        own = pl.ds(pl.multiple_of(blk * tile, tile), tile)
+
+        @pl.when(here)
         def _():
+            for copy in sums(hub):
+                copy.wait()
             both = back_ref[row, :].astype(F32) + back_other_ref[row, :].astype(F32)
             next_ref[own, :] -= STEP * both
 
@@ -204,16 +240,19 @@
             at = pl.ds(pl.multiple_of((block - me * (cores * blocks)) * tile, tile), tile)
             next_ref[row, :] -= STEP * dot(lr_ref[s], chip_ref[at, :])
 
+    done = pltpu.make_async_copy(next_ref, next_hbm, sems.at[store])
+    done.start()
+    done.wait()
+
 
 def edge_kernel(
-    outer_hbm, band_hbm, partial_hbm, out_hbm, outer_ref, band_ref, partial_ref, out_ref, sems
+    outer_ref, band_hbm, partial_hbm, out_hbm, band_ref, partial_ref, out_ref, sems
 ):
     core = lax.axis_index("col")
     blocks, reach, tile, _ = band_ref.shape
     first = (band_hbm.shape[1] - reach) * core
     for copy in fetch(
         [
-            (outer_hbm, outer_ref),
             (band_hbm.at[:, pl.ds(first, reach)], band_ref),
             (partial_hbm, partial_ref),
         ],
@@ -336,7 +375,8 @@
 
     def exchange(x):
         x = x.reshape(rows_dev, half // rows_dev, traits)
-        return lax.all_to_all(x, "row", 0, 0)
+        order = ORDERS.get(rows_dev)
+        return lax.all_to_all(x, "row", 0, 0, axis_index_groups=order and [list(order)])
 
     half_type = jax.ShapeDtypeStruct((half, traits), BF16)
     panels, back, keep, send = pl.pallas_call(
@@ -386,7 +426,7 @@
             functools.partial(band_kernel, cores),
             out_shape=jax.ShapeDtypeStruct((rows, traits), F32),
             in_specs=[SMEM] * 3 + [HBM] * 9,
-            out_specs=VMEM,
+            out_specs=HBM,
             scratch_shapes=[
                 pltpu.VMEM((cores * rows, traits), BF16),
                 pltpu.VMEM(current.shape, F32),
@@ -396,7 +436,8 @@
                 pltpu.VMEM(back.shape, BF16),
                 pltpu.VMEM(back.shape, BF16),
                 pltpu.VMEM(lr.shape, BF16),
-                pltpu.SemaphoreType.DMA((9,)),
+                pltpu.VMEM((rows, traits), F32),
+                pltpu.SemaphoreType.DMA((8 + 2 * hubs,)),
             ],
             compiler_params=BAND,
             cost_estimate=pl.CostEstimate(
@@ -420,16 +461,15 @@
         partial = pl.pallas_call(
             edge_kernel,
             out_shape=jax.ShapeDtypeStruct((rows, traits), F32),
-            in_specs=[HBM] * 3,
+            in_specs=[VMEM, HBM, HBM],
             out_specs=HBM,
             scratch_shapes=[
-                pltpu.VMEM((rows, traits), BF16),
                 pltpu.VMEM((blocks, band.shape[1] // 2, tile, tile), BF16),
                 pltpu.VMEM((rows, traits), F32),
                 pltpu.VMEM((rows, traits), F32),
                 pltpu.SemaphoreType.DMA((blocks + 3,)),
             ],
-            compiler_params=BAND,
+            compiler_params=EDGE,
             name="edge",
         )(outer, band, partial)
         mine = exchange(merged).reshape(half, traits)

time: 79 us -> 77.7 us (0.984)
  local copies, waits for them, and re-layouts: 2.6 us -> 1.03 us
  starting transfers between devices: 24.5 us -> 25.9 us
    all_to_all x4, starting transfers between devices: 21.2 us -> 22.8 us  [exchange(): lax.all_to_all(x, 'row', 0, 0, axis_index_groups=order and [list(order)])]
    unnamed x36 -> x32, local copies, waits for them, and re-layouts: 2.6 us -> 1.03 us
  transfers between devices with their start and end apart: 14 -> 14, of which waited for: 6 -> 8; matrix products, arithmetic and copies ran while one was open for 0% -> 0% of each run, Pallas kernels for 25% -> 24%
where the time goes in v4:
time: 77.7 us; the launch traced here: 76.9 us
  Pallas kernels  28.3 us (36%)
  starting transfers between devices  25.9 us (33%)
  waiting for transfers between devices  21.4 us (28%)
  local copies, waits for them, and re-layouts  1.03 us (1%)
    all_to_all x4, starting transfers between devices, exchange(): lax.all_to_all(x, 'row', 0, 0, axis_index_groups=order and [list(order)])  22.8 us
    all_to_all x4, waiting for transfers between devices, exchange(): lax.all_to_all(x, 'row', 0, 0, axis_index_groups=order and [list(order)])  16.6 us
    pallas_call x2, Pallas kernels, shards(): pl.pallas_call(functools.partial(band_kernel, cores), out_shape=jax.Shape...  8.9 us
    pallas_call x2, Pallas kernels, shards(): pl.pallas_call(functools.partial(step_kernel, cores, last), out_shape=tup...  6.51 us
    pallas_call x2, Pallas kernels, shards(): pl.pallas_call(edge_kernel, out_shape=jax.ShapeDtypeStruct((rows, traits)...  5.45 us
    ppermute x8, waiting for transfers between devices, other_core(): return lax.ppermute(x, 'col', swap)  4.83 us
    pallas_call x1, Pallas kernels, shards(): pl.pallas_call(functools.partial(first_kernel, cores), out_shape=(panel_t...  3.17 us
    pallas_call x2, Pallas kernels, shards(): pl.pallas_call(functools.partial(merge_kernel, cores, tile, blocks * core...  2.7 us
  transfers between devices with their start and end apart: 14, of which 8 were waited for; matrix products, arithmetic and copies ran while one was open for 0% of the time, Pallas kernels for 24%

profile of v4, /device:TPU:0, one launch (start us, length us, event | category | flops | bytes accessed | tf_op | source)
XLA Modules:
  0.0 76.9 jit_solution(10787892113149016110)
XLA Ops:
  0.0 3.2 %first.1 = (bf16[512,512]{1,0:T(8,128)(2,1)}, bf16[512,512]{1,0:T(8,128)(2,1)}, bf16[256,512]{1,0:T(8,128)(2,1)}, bf16[256,512]{1,0:T(8,128)(2,1)}) custom-call(s32[4]{0:T(128)} %blocks_ref.11, s32[8]{0:T(128)} %local_ref.7, s32[8]{0:T(128)} %hub_ref.7, f32[512,512]{1,0:T(8,128)} %current_hbm.1, bf16[8,128,128]{2,1,0:T(8,128)(2,1)} %lr_ref.3), custom_call_target="tpu_custom_call" | custom-call | tf_op jit(solution)/shard_map/first/pallas_call | solution.py:382
  3.2 0.5 collective-permute-start
  3.7 0.1 collective-permute-start.1
  3.8 0.4 collective-permute-start.2
  4.2 0.9 %collective-permute-done.came_ref = bf16[256,512]{1,0:T(8,128)(2,1)S(1)} collective-permute-done((bf16[256,512]{1,0:T(8,128)(2,1)}, bf16[256,512]{1,0:T(8,128)(2,1)S(1)}, u32[]{:S(2)}, u32[]{:S(2)}) %collective-permute-start) | collective-permute-done | bytes 262176 | tf_op jit(solution)/shard_map/ppermute | solution.py:374
  5.1 0.9 %copy-done.6 = bf16[256,512]{1,0:T(8,128)(2,1)S(1)} copy-done((bf16[256,512]{1,0:T(8,128)(2,1)S(1)}, bf16[256,512]{1,0:T(8,128)(2,1)}, u32[]{:S(2)}) %copy-start.6) | copy-done | bytes 262168
  6.0 0.8 join.2
  6.8 7.7 %all-to-all-start = ((bf16[8,32,512]{2,1,0:T(8,128)(2,1)}), bf16[8,32,512]{2,1,0:T(8,128)(2,1)S(1)}, u32[]{:S(2)}, u32[]{:S(2)}) async-start(bf16[8,32,512]{2,1,0:T(8,128)(2,1)} %bitcast), calls=%async_computation | async-start | bytes 524288 | tf_op jit(solution)/shard_map/all_to_all | solution.py:379
  14.5 0.0 copy-done.15
  14.5 0.7 collective-permute-start.3
  15.2 0.0 collective-permute-done.1.rest_0_.other_hbm
  15.2 0.0 copy-start.3
  15.2 0.0 collective-permute-done.2.rest_1_.back_other_hbm
  15.2 0.0 copy-start.5
  15.3 7.5 %all-to-all-done.in_ref = bf16[8,32,512]{2,1,0:T(8,128)(2,1)S(1)} async-done(((bf16[8,32,512]{2,1,0:T(8,128)(2,1)}), bf16[8,32,512]{2,1,0:T(8,128)(2,1)S(1)}, u32[]{:S(2)}, u32[]{:S(2)}) %all-to-all-start) | async-done | bytes 262176 | tf_op jit(solution)/shard_map/all_to_all | solution.py:379
  22.8 0.0 copy-done.7
  22.8 1.4 %merge.2 = bf16[8,32,512]{2,1,0:T(8,128)(2,1)} custom-call(s32[4]{0:T(128)S(1)} %copy-done.7, bf16[8,32,512]{2,1,0:T(8,128)(2,1)S(1)} %all-to-all-done.in_ref, bf16[512,512]{1,0:T(8,128)(2,1)S(1)} %collective-permute-done.1.rest_0_.other_hbm, bf16[512,512]{1,0:T(8,128)(2,1)S(1)} %collective-permute-done.2.rest_1_.back_other_hbm), custom_call_target="tpu_custom_call" | custom-call | tf_op jit(solution)/shard_map/merge/pallas_call | solution.py:417
  24.1 4.6 %all-to-all-start.1 = ((bf16[8,32,512]{2,1,0:T(8,128)(2,1)}), bf16[8,32,512]{2,1,0:T(8,128)(2,1)S(1)}, u32[]{:S(2)}, u32[]{:S(2)}) async-start(bf16[8,32,512]{2,1,0:T(8,128)(2,1)} %merge.2), calls=%async_computation.1 | async-start | bytes 524288 | tf_op jit(solution)/shard_map/all_to_all | solution.py:379
  28.8 0.0 copy-done.3
  28.8 0.0 copy-done.5
  28.8 4.4 %band.2.partial_hbm = f32[512,512]{1,0:T(8,128)} custom-call(s32[4]{0:T(128)} %blocks_ref.11, s32[8]{0:T(128)} %local_ref.7, s32[8]{0:T(128)} %hub_ref.7, f32[512,512]{1,0:T(8,128)} %current_hbm.1, f32[512,512]{1,0:T(8,128)} %zscores_hbm.3, f32[1,512]{1,0:T(1,128)} %bitcast.9, bf16[4,9,128,128]{3,2,1,0:T(8,128)(2,1)} %band_hbm.7, ...), custom_call_target="tpu_custom_call" | custom-call | flops 1000000 | bytes 1048576 | tf_op jit(solution)/shard_map/band/pallas_call | solution.py:425
  33.3 0.0 copy-start
  33.3 0.0 copy-start.8
  33.3 0.0 copy-start.10
  33.3 0.0 copy-start.12
  33.3 0.0 collective-permute-done.3.outer_ref
  33.3 2.7 %edge.2.partial_hbm = f32[512,512]{1,0:T(8,128)} custom-call(bf16[512,512]{1,0:T(8,128)(2,1)S(1)} %collective-permute-done.3.outer_ref, bf16[4,9,128,128]{3,2,1,0:T(8,128)(2,1)} %band_hbm.7, f32[512,512]{1,0:T(8,128)} %band.2.partial_hbm), custom_call_target="tpu_custom_call" | custom-call | tf_op jit(solution)/shard_map/edge/pallas_call | solution.py:461
  36.1 0.8 %all-to-all-done.1 = bf16[8,32,512]{2,1,0:T(8,128)(2,1)S(1)} async-done(((bf16[8,32,512]{2,1,0:T(8,128)(2,1)}), bf16[8,32,512]{2,1,0:T(8,128)(2,1)S(1)}, u32[]{:S(2)}, u32[]{:S(2)}) %all-to-all-start.1) | async-done | bytes 262176 | tf_op jit(solution)/shard_map/all_to_all | solution.py:379
  36.8 0.0 collective-permute-start.4
  36.8 1.5 %collective-permute-done.4.half_other_ref = bf16[256,512]{1,0:T(8,128)(2,1)S(1)} collective-permute-done((bf16[256,512]{1,0:T(8,128)(2,1)S(1)}, bf16[256,512]{1,0:T(8,128)(2,1)S(1)}, u32[]{:S(2)}, u32[]{:S(2)}) %collective-permute-start.4) | collective-permute-done | bytes 262176 | tf_op jit(solution)/shard_map/ppermute | solution.py:374
  38.4 0.0 copy-done
  38.4 0.0 copy-done.8
  38.4 0.0 copy-done.10
  38.4 0.0 copy-done.12
  38.4 3.7 %step.2 = (f32[512,512]{1,0:T(8,128)}, bf16[512,512]{1,0:T(8,128)(2,1)}, bf16[512,512]{1,0:T(8,128)(2,1)}, bf16[256,512]{1,0:T(8,128)(2,1)S(1)}, bf16[256,512]{1,0:T(8,128)(2,1)S(1)}) custom-call(s32[4]{0:T(128)S(1)} %copy-done.8, s32[8]{0:T(128)S(1)} %copy-done.10, s32[8]{0:T(128)S(1)} %copy-done.12, bf16[8,128,128]{2,1,0:T(8,128)(2,1)S(1)} %copy-done, ...), custom_call_target="tpu_custom_call" | custom-call | tf_op jit(solution)/shard_map/step/pallas_call | solution.py:482
  42.1 0.0 copy-start.14
  42.1 0.2 collective-permute-start.5
  42.3 0.4 collective-permute-start.6
  42.7 0.1 collective-permute-start.7
  42.8 0.9 %collective-permute-done.5.came_ref = bf16[256,512]{1,0:T(8,128)(2,1)S(1)} collective-permute-done((bf16[256,512]{1,0:T(8,128)(2,1)S(1)}, bf16[256,512]{1,0:T(8,128)(2,1)S(1)}, u32[]{:S(2)}, u32[]{:S(2)}) %collective-permute-start.5) | collective-permute-done | bytes 262176 | tf_op jit(solution)/shard_map/ppermute | solution.py:374
  43.7 0.8 join.3
  44.4 5.8 %all-to-all-start.2 = ((bf16[8,32,512]{2,1,0:T(8,128)(2,1)}), bf16[8,32,512]{2,1,0:T(8,128)(2,1)S(1)}, u32[]{:S(2)}, u32[]{:S(2)}) async-start(bf16[8,32,512]{2,1,0:T(8,128)(2,1)} %bitcast.3), calls=%async_computation.2 | async-start | bytes 524288 | tf_op jit(solution)/shard_map/all_to_all | solution.py:379
  50.2 0.0 copy-done.14
  50.2 0.7 collective-permute-start.8
  50.9 0.0 collective-permute-done.6.rest_0_.other_hbm
  50.9 0.0 copy-start.2
  51.0 0.0 collective-permute-done.7.rest_1_.back_other_hbm
  51.0 0.0 copy-start.4
  51.0 7.5 %all-to-all-done.2.in_ref = bf16[8,32,512]{2,1,0:T(8,128)(2,1)S(1)} async-done(((bf16[8,32,512]{2,1,0:T(8,128)(2,1)}), bf16[8,32,512]{2,1,0:T(8,128)(2,1)S(1)}, u32[]{:S(2)}, u32[]{:S(2)}) %all-to-all-start.2) | async-done | bytes 262176 | tf_op jit(solution)/shard_map/all_to_all | solution.py:379
  58.5 1.4 %merge.3 = bf16[8,32,512]{2,1,0:T(8,128)(2,1)} custom-call(s32[4]{0:T(128)S(1)} %copy-done.8, bf16[8,32,512]{2,1,0:T(8,128)(2,1)S(1)} %all-to-all-done.2.in_ref, bf16[512,512]{1,0:T(8,128)(2,1)S(1)} %collective-permute-done.6.rest_0_.other_hbm, bf16[512,512]{1,0:T(8,128)(2,1)S(1)} %collective-permute-done.7.rest_1_.back_other_hbm), custom_call_target="tpu_custom_call" | custom-call | tf_op jit(solution)/shard_map/merge/pallas_call | solution.py:417
  59.9 4.6 %all-to-all-start.3 = ((bf16[8,32,512]{2,1,0:T(8,128)(2,1)}), bf16[8,32,512]{2,1,0:T(8,128)(2,1)S(1)}, u32[]{:S(2)}, u32[]{:S(2)}) async-start(bf16[8,32,512]{2,1,0:T(8,128)(2,1)} %merge.3), calls=%async_computation.3 | async-start | bytes 524288 | tf_op jit(solution)/shard_map/all_to_all | solution.py:379
  64.5 4.5 %band.3.partial_hbm = f32[512,512]{1,0:T(8,128)} custom-call(s32[4]{0:T(128)} %blocks_ref.11, s32[8]{0:T(128)} %local_ref.7, s32[8]{0:T(128)} %hub_ref.7, f32[512,512]{1,0:T(8,128)} %get-tuple-element.28.current_hbm, f32[512,512]{1,0:T(8,128)} %zscores_hbm.3, f32[1,512]{1,0:T(1,128)} %bitcast.10, bf16[4,9,128,128]{3,2,1,0:T(8,128)(2,1)} %band_hbm.7, ...), custom_call_target="tpu_custom_call" | custom-call | flops 1000000 | bytes 1048576 | tf_op jit(solution)/shard_map/band/pallas_call | solution.py:425
  69.0 0.0 copy-start.1
  69.0 0.0 copy-start.9
  69.0 0.0 copy-start.11
  69.0 0.0 copy-start.13
  69.0 0.0 collective-permute-done.8.outer_ref
  69.0 2.7 %edge.3.partial_hbm = f32[512,512]{1,0:T(8,128)} custom-call(bf16[512,512]{1,0:T(8,128)(2,1)S(1)} %collective-permute-done.8.outer_ref, bf16[4,9,128,128]{3,2,1,0:T(8,128)(2,1)} %band_hbm.7, f32[512,512]{1,0:T(8,128)} %band.3.partial_hbm), custom_call_target="tpu_custom_call" | custom-call | tf_op jit(solution)/shard_map/edge/pallas_call | solution.py:461
  71.8 0.8 %all-to-all-done.3 = bf16[8,32,512]{2,1,0:T(8,128)(2,1)S(1)} async-done(((bf16[8,32,512]{2,1,0:T(8,128)(2,1)}), bf16[8,32,512]{2,1,0:T(8,128)(2,1)S(1)}, u32[]{:S(2)}, u32[]{:S(2)}) %all-to-all-start.3) | async-done | bytes 262176 | tf_op jit(solution)/shard_map/all_to_all | solution.py:379
  72.5 0.0 collective-permute-start.9
  72.5 1.5 %collective-permute-done.9.half_other_ref = bf16[256,512]{1,0:T(8,128)(2,1)S(1)} collective-permute-done((bf16[256,512]{1,0:T(8,128)(2,1)S(1)}, bf16[256,512]{1,0:T(8,128)(2,1)S(1)}, u32[]{:S(2)}, u32[]{:S(2)}) %collective-permute-start.9) | collective-permute-done | bytes 262176 | tf_op jit(solution)/shard_map/ppermute | solution.py:374
  74.1 0.0 copy-done.1
  74.1 0.0 copy-done.11
  74.1 2.8 %step.3 = f32[512,512]{1,0:T(8,128)} custom-call(s32[4]{0:T(128)S(1)} %copy-done.9, s32[8]{0:T(128)S(1)} %copy-done.11, s32[8]{0:T(128)S(1)} %copy-done.13, bf16[8,128,128]{2,1,0:T(8,128)(2,1)S(1)} %copy-done.1, bf16[256,512]{1,0:T(8,128)(2,1)S(1)} %bitcast.6, bf16[256,512]{1,0:T(8,128)(2,1)S(1)} %collective-permute-done.9.half_other_ref, ...), custom_call_target="tpu_custom_call" | custom-call | tf_op jit(solution)/shard_map/step/pallas_call | solution.py:482
  (7 shorter events, 0.0 us)
Async XLA Ops:
  0.0 22.8 %copy-start.7 = (s32[4]{0:T(128)S(1)}, s32[4]{0:T(128)}, u32[]{:S(2)}) copy-start(s32[4]{0:T(128)} %blocks_ref.11) | copy-start | bytes 52
  3.2 1.9 %collective-permute-start = (bf16[256,512]{1,0:T(8,128)(2,1)}, bf16[256,512]{1,0:T(8,128)(2,1)S(1)}, u32[]{:S(2)}, u32[]{:S(2)}) collective-permute-start(bf16[256,512]{1,0:T(8,128)(2,1)} %get-tuple-element.19), channel_id=1, source_target_pairs={{0,1},{1,0},{2,3},{3,2},{4,5},{5,4},{6,7},{7,6},{8,9},{9,8},{10,11... | collective-permute-start | bytes 786440 | tf_op jit(solution)/shard_map/ppermute | solution.py:374
  3.7 11.5 %collective-permute-start.1 = (bf16[512,512]{1,0:T(8,128)(2,1)}, bf16[512,512]{1,0:T(8,128)(2,1)S(1)}, u32[]{:S(2)}, u32[]{:S(2)}) collective-permute-start(bf16[512,512]{1,0:T(8,128)(2,1)} %get-tuple-element.20.mine_hbm), channel_id=1, source_target_pairs={{0,1},{1,0},{2,3},{3,2},{4,5},{5,4},{6,7},{7,6},{8,9},{9,8},{10,11... | collective-permute-start | bytes 1572872 | tf_op jit(solution)/shard_map/ppermute | solution.py:374
  3.8 11.5 %collective-permute-start.2 = (bf16[512,512]{1,0:T(8,128)(2,1)}, bf16[512,512]{1,0:T(8,128)(2,1)S(1)}, u32[]{:S(2)}, u32[]{:S(2)}) collective-permute-start(bf16[512,512]{1,0:T(8,128)(2,1)} %get-tuple-element.21.back_hbm), channel_id=1, source_target_pairs={{0,1},{1,0},{2,3},{3,2},{4,5},{5,4},{6,7},{7,6},{8,9},{9,8},{10,11... | collective-permute-start | bytes 1572872 | tf_op jit(solution)/shard_map/ppermute | solution.py:374
  5.1 0.9 %copy-start.6 = (bf16[256,512]{1,0:T(8,128)(2,1)S(1)}, bf16[256,512]{1,0:T(8,128)(2,1)}, u32[]{:S(2)}) copy-start(bf16[256,512]{1,0:T(8,128)(2,1)} %get-tuple-element.18.keep_ref) | copy-start | bytes 786436
  6.0 8.5 %copy-start.15 = (bf16[512,512]{1,0:T(8,128)(2,1)S(1)}, bf16[512,512]{1,0:T(8,128)(2,1)}, u32[]{:S(2)}) copy-start(bf16[512,512]{1,0:T(8,128)(2,1)} %get-tuple-element.20.mine_hbm) | copy-start | bytes 1572868
  6.8 16.0 %all-to-all-start = ((bf16[8,32,512]{2,1,0:T(8,128)(2,1)}), bf16[8,32,512]{2,1,0:T(8,128)(2,1)S(1)}, u32[]{:S(2)}, u32[]{:S(2)}) async-start(bf16[8,32,512]{2,1,0:T(8,128)(2,1)} %bitcast), calls=%async_computation | async-start | bytes 524288 | tf_op jit(solution)/shard_map/all_to_all | solution.py:379
  14.5 18.8 %collective-permute-start.3 = (bf16[512,512]{1,0:T(8,128)(2,1)S(1)}, bf16[512,512]{1,0:T(8,128)(2,1)S(1)}, u32[]{:S(2)}, u32[]{:S(2)}) collective-permute-start(bf16[512,512]{1,0:T(8,128)(2,1)S(1)} %copy-done.15), channel_id=1, source_target_pairs={{1,2},{3,4},{5,6},{7,8},{9,10},{11,12},{13,14},{2,1},{4,3},{6,5},{... | collective-permute-start | bytes 1572872 | tf_op jit(solution)/shard_map/ppermute | solution.py:404
  15.2 13.6 %copy-start.3 = (bf16[512,512]{1,0:T(8,128)(2,1)}, bf16[512,512]{1,0:T(8,128)(2,1)S(1)}, u32[]{:S(2)}) copy-start(bf16[512,512]{1,0:T(8,128)(2,1)S(1)} %collective-permute-done.1.rest_0_.other_hbm) | copy-start | bytes 1572868
  15.2 13.6 %copy-start.5 = (bf16[512,512]{1,0:T(8,128)(2,1)}, bf16[512,512]{1,0:T(8,128)(2,1)S(1)}, u32[]{:S(2)}) copy-start(bf16[512,512]{1,0:T(8,128)(2,1)S(1)} %collective-permute-done.2.rest_1_.back_other_hbm) | copy-start | bytes 1572868
  24.1 12.7 %all-to-all-start.1 = ((bf16[8,32,512]{2,1,0:T(8,128)(2,1)}), bf16[8,32,512]{2,1,0:T(8,128)(2,1)S(1)}, u32[]{:S(2)}, u32[]{:S(2)}) async-start(bf16[8,32,512]{2,1,0:T(8,128)(2,1)} %merge.2), calls=%async_computation.1 | async-start | bytes 524288 | tf_op jit(solution)/shard_map/all_to_all | solution.py:379
  33.3 5.1 %copy-start = (bf16[8,128,128]{2,1,0:T(8,128)(2,1)S(1)}, bf16[8,128,128]{2,1,0:T(8,128)(2,1)}, u32[]{:S(2)}) copy-start(bf16[8,128,128]{2,1,0:T(8,128)(2,1)} %lr_ref.3) | copy-start | bytes 786436
  33.3 5.1 %copy-start.8 = (s32[4]{0:T(128)S(1)}, s32[4]{0:T(128)}, u32[]{:S(2)}) copy-start(s32[4]{0:T(128)} %blocks_ref.11) | copy-start | bytes 52
  33.3 5.1 %copy-start.10 = (s32[8]{0:T(128)S(1)}, s32[8]{0:T(128)}, u32[]{:S(2)}) copy-start(s32[8]{0:T(128)} %local_ref.7) | copy-start | bytes 100
  33.3 5.1 %copy-start.12 = (s32[8]{0:T(128)S(1)}, s32[8]{0:T(128)}, u32[]{:S(2)}) copy-start(s32[8]{0:T(128)} %hub_ref.7) | copy-start | bytes 100
  36.8 1.5 %collective-permute-start.4 = (bf16[256,512]{1,0:T(8,128)(2,1)S(1)}, bf16[256,512]{1,0:T(8,128)(2,1)S(1)}, u32[]{:S(2)}, u32[]{:S(2)}) collective-permute-start(bf16[256,512]{1,0:T(8,128)(2,1)S(1)} %bitcast.7), channel_id=1, source_target_pairs={{0,1},{1,0},{2,3},{3,2},{4,5},{5,4},{6,7},{7,6},{8,9},{9,8},{10,11... | collective-permute-start | bytes 786440 | tf_op jit(solution)/shard_map/ppermute | solution.py:374
  42.1 8.2 %copy-start.14 = (bf16[512,512]{1,0:T(8,128)(2,1)S(1)}, bf16[512,512]{1,0:T(8,128)(2,1)}, u32[]{:S(2)}) copy-start(bf16[512,512]{1,0:T(8,128)(2,1)} %get-tuple-element.26.mine_hbm) | copy-start | bytes 1572868
  42.1 1.6 %collective-permute-start.5 = (bf16[256,512]{1,0:T(8,128)(2,1)S(1)}, bf16[256,512]{1,0:T(8,128)(2,1)S(1)}, u32[]{:S(2)}, u32[]{:S(2)}) collective-permute-start(bf16[256,512]{1,0:T(8,128)(2,1)S(1)} %get-tuple-element.25), channel_id=1, source_target_pairs={{0,1},{1,0},{2,3},{3,2},{4,5},{5,4},{6,7},{7,6},{8,9},{9,8},{10,11... | collective-permute-start | bytes 786440 | tf_op jit(solution)/shard_map/ppermute | solution.py:374
  42.3 8.7 %collective-permute-start.6 = (bf16[512,512]{1,0:T(8,128)(2,1)}, bf16[512,512]{1,0:T(8,128)(2,1)S(1)}, u32[]{:S(2)}, u32[]{:S(2)}) collective-permute-start(bf16[512,512]{1,0:T(8,128)(2,1)} %get-tuple-element.26.mine_hbm), channel_id=1, source_target_pairs={{0,1},{1,0},{2,3},{3,2},{4,5},{5,4},{6,7},{7,6},{8,9},{9,8},{10,11... | collective-permute-start | bytes 1572872 | tf_op jit(solution)/shard_map/ppermute | solution.py:374
  42.7 8.3 %collective-permute-start.7 = (bf16[512,512]{1,0:T(8,128)(2,1)}, bf16[512,512]{1,0:T(8,128)(2,1)S(1)}, u32[]{:S(2)}, u32[]{:S(2)}) collective-permute-start(bf16[512,512]{1,0:T(8,128)(2,1)} %get-tuple-element.27.back_hbm), channel_id=1, source_target_pairs={{0,1},{1,0},{2,3},{3,2},{4,5},{5,4},{6,7},{7,6},{8,9},{9,8},{10,11... | collective-permute-start | bytes 1572872 | tf_op jit(solution)/shard_map/ppermute | solution.py:374
  44.4 14.1 %all-to-all-start.2 = ((bf16[8,32,512]{2,1,0:T(8,128)(2,1)}), bf16[8,32,512]{2,1,0:T(8,128)(2,1)S(1)}, u32[]{:S(2)}, u32[]{:S(2)}) async-start(bf16[8,32,512]{2,1,0:T(8,128)(2,1)} %bitcast.3), calls=%async_computation.2 | async-start | bytes 524288 | tf_op jit(solution)/shard_map/all_to_all | solution.py:379
  50.2 18.8 %collective-permute-start.8 = (bf16[512,512]{1,0:T(8,128)(2,1)S(1)}, bf16[512,512]{1,0:T(8,128)(2,1)S(1)}, u32[]{:S(2)}, u32[]{:S(2)}) collective-permute-start(bf16[512,512]{1,0:T(8,128)(2,1)S(1)} %copy-done.14), channel_id=1, source_target_pairs={{1,2},{3,4},{5,6},{7,8},{9,10},{11,12},{13,14},{2,1},{4,3},{6,5},{... | collective-permute-start | bytes 1572872 | tf_op jit(solution)/shard_map/ppermute | solution.py:404
  50.9 13.6 %copy-start.2 = (bf16[512,512]{1,0:T(8,128)(2,1)}, bf16[512,512]{1,0:T(8,128)(2,1)S(1)}, u32[]{:S(2)}) copy-start(bf16[512,512]{1,0:T(8,128)(2,1)S(1)} %collective-permute-done.6.rest_0_.other_hbm) | copy-start | bytes 1572868
  51.0 13.5 %copy-start.4 = (bf16[512,512]{1,0:T(8,128)(2,1)}, bf16[512,512]{1,0:T(8,128)(2,1)S(1)}, u32[]{:S(2)}) copy-start(bf16[512,512]{1,0:T(8,128)(2,1)S(1)} %collective-permute-done.7.rest_1_.back_other_hbm) | copy-start | bytes 1572868
  59.9 12.7 %all-to-all-start.3 = ((bf16[8,32,512]{2,1,0:T(8,128)(2,1)}), bf16[8,32,512]{2,1,0:T(8,128)(2,1)S(1)}, u32[]{:S(2)}, u32[]{:S(2)}) async-start(bf16[8,32,512]{2,1,0:T(8,128)(2,1)} %merge.3), calls=%async_computation.3 | async-start | bytes 524288 | tf_op jit(solution)/shard_map/all_to_all | solution.py:379
  69.0 5.1 %copy-start.1 = (bf16[8,128,128]{2,1,0:T(8,128)(2,1)S(1)}, bf16[8,128,128]{2,1,0:T(8,128)(2,1)}, u32[]{:S(2)}) copy-start(bf16[8,128,128]{2,1,0:T(8,128)(2,1)} %lr_ref.3) | copy-start | bytes 786436
  69.0 5.1 %copy-start.9 = (s32[4]{0:T(128)S(1)}, s32[4]{0:T(128)}, u32[]{:S(2)}) copy-start(s32[4]{0:T(128)} %blocks_ref.11) | copy-start | bytes 52
  69.0 5.1 %copy-start.11 = (s32[8]{0:T(128)S(1)}, s32[8]{0:T(128)}, u32[]{:S(2)}) copy-start(s32[8]{0:T(128)} %local_ref.7) | copy-start | bytes 100
  69.0 5.1 %copy-start.13 = (s32[8]{0:T(128)S(1)}, s32[8]{0:T(128)}, u32[]{:S(2)}) copy-start(s32[8]{0:T(128)} %hub_ref.7) | copy-start | bytes 100
  72.5 1.5 %collective-permute-start.9 = (bf16[256,512]{1,0:T(8,128)(2,1)S(1)}, bf16[256,512]{1,0:T(8,128)(2,1)S(1)}, u32[]{:S(2)}, u32[]{:S(2)}) collective-permute-start(bf16[256,512]{1,0:T(8,128)(2,1)S(1)} %bitcast.5), channel_id=1, source_target_pairs={{0,1},{1,0},{2,3},{3,2},{4,5},{5,4},{6,7},{7,6},{8,9},{9,8},{10,11... | collective-permute-start | bytes 786440 | tf_op jit(solution)/shard_map/ppermute | solution.py:374

commit v5 on v4

--- a/solution.py
+++ b/solution.py
@@ -30,7 +30,7 @@
     return lax.dot_general(a, b, (((0,), (0,)), ((), ())), preferred_element_type=F32)
 
 
-ORDERS = {8: (1, 6, 0, 2, 5, 4, 3, 7)}
+ORDERS = {8: (4, 6, 1, 5, 0, 2, 7, 3)}
 
 
 def position(chip, chips):
@@ -245,43 +245,6 @@
     done.wait()
 
 
-def edge_kernel(
-    outer_ref, band_hbm, partial_hbm, out_hbm, band_ref, partial_ref, out_ref, sems
-):
-    core = lax.axis_index("col")
-    blocks, reach, tile, _ = band_ref.shape
-    first = (band_hbm.shape[1] - reach) * core
-    for copy in fetch(
-        [
-            (band_hbm.at[:, pl.ds(first, reach)], band_ref),
-            (partial_hbm, partial_ref),
-        ],
-        sems,
-    ):
-        copy.wait()
-
-    def write(b, skip, low, high):
-        tiles = [band_ref[b, skip + n] for n in range(high - low)]
-        out = pl.ds(b * tile, tile)
-        gradient = dot(jnp.concatenate(tiles, axis=1), outer_ref[low * tile : high * tile, :])
-        out_ref[out, :] = partial_ref[out, :] - STEP * gradient
-        pltpu.make_async_copy(out_ref.at[out], out_hbm.at[out], sems.at[3 + b]).start()
-
-    @pl.when(core == 0)
-    def _():
-        for b in range(blocks):
-            write(b, 0, b, blocks)
-
-    @pl.when(core != 0)
-    def _():
-        for b in range(blocks):
-            write(b, blocks - 1 - b, 0, b + 1)
-
-    for b in range(blocks):
-        out = pl.ds(b * tile, tile)
-        pltpu.make_async_copy(out_ref.at[out], out_hbm.at[out], sems.at[3 + b]).wait()
-
-
 def step_kernel(
     cores,
     last,
@@ -292,25 +255,52 @@
     half_ref,
     half_other_ref,
     partial_hbm,
+    outer_hbm,
+    band_hbm,
     *rest,
 ):
     if last:
         next_hbm, rest = rest[0], rest[1:]
     else:
         (next_hbm, panel_hbm, back_hbm, keep_ref, send_ref), rest = rest[:5], rest[5:]
-    partial_ref, panel_ref, state_ref, grad_ref, term_ref, next_ref, sems = rest
+    partial_ref, panel_ref, state_ref, grad_ref, term_ref, next_ref, edge_ref, sems = rest
     me, core = lax.axis_index("row"), lax.axis_index("col")
     count, tile, _ = lr_ref.shape
     rows = next_ref.shape[0]
     blocks = rows // tile
     hubs = blocks_ref.shape[0]
     half = half_ref.shape[0]
-    copies = fetch([(partial_hbm, partial_ref)], sems)
+    reach = edge_ref.shape[1]
+    first_edge = (band_hbm.shape[1] - reach) * core
+    copies = fetch(
+        [
+            (outer_hbm, panel_ref),
+            (band_hbm.at[:, pl.ds(first_edge, reach)], edge_ref),
+            (partial_hbm, partial_ref),
+        ],
+        sems,
+    )
     near = pl.ds(pl.multiple_of(core * half, half), half)
     away = pl.ds(pl.multiple_of((1 - core) * half, half), half)
     state_ref[near, :] = half_ref[...]
     state_ref[away, :] = half_other_ref[...]
-    grad_ref[...] = jnp.zeros_like(grad_ref)
+
+    def edge(b, skip, low, high):
+        tiles = [edge_ref[b, skip + n] for n in range(high - low)]
+        return dot(jnp.concatenate(tiles, axis=1), panel_ref[low * tile : high * tile, :])
+
+    copies[0].wait()
+    copies[1].wait()
+
+    @pl.when(core == 0)
+    def _():
+        for b in range(blocks):
+            grad_ref[b * tile : (b + 1) * tile, :] = edge(b, 0, b, blocks)
+
+    @pl.when(core != 0)
+    def _():
+        for b in range(blocks):
+            grad_ref[b * tile : (b + 1) * tile, :] = edge(b, blocks - 1 - b, 0, b + 1)
 
     for hub in range(hubs):
         place = Place(blocks_ref[hub], blocks, cores)
@@ -331,21 +321,20 @@
     for s in range(count):
         grad_ref[pl.ds(pl.multiple_of(local_ref[s] * tile, tile), tile), :] += term_ref[s]
 
-    for copy in copies:
-        copy.wait()
+    copies[2].wait()
     done = []
     for b in range(blocks):
         out = pl.ds(b * tile, tile)
         following = partial_ref[out, :] - STEP * grad_ref[out, :]
         next_ref[out, :] = following
-        done += fetch([(next_ref.at[out], next_hbm.at[out])], sems.at[pl.ds(2 + b, 1)])
+        done += fetch([(next_ref.at[out], next_hbm.at[out])], sems.at[pl.ds(3 + b, 1)])
         if not last:
             panel_ref[out, :] = following.astype(BF16)
     if not last:
         back_ref, acc_ref = state_ref, grad_ref
-        done += fetch([(panel_ref, panel_hbm)], sems.at[pl.ds(2 + blocks, 1)])
+        done += fetch([(panel_ref, panel_hbm)], sems.at[pl.ds(3 + blocks, 1)])
         back_terms(local_ref, hub_ref, lr_ref, panel_ref, term_ref, acc_ref, back_ref)
-        done += fetch([(back_ref, back_hbm)], sems.at[pl.ds(3 + blocks, 1)])
+        done += fetch([(back_ref, back_hbm)], sems.at[pl.ds(4 + blocks, 1)])
         contributions(cores, blocks_ref, back_ref, panel_ref, keep_ref, send_ref)
     for copy in done:
         copy.wait()
@@ -458,22 +447,8 @@
             back_other,
             lr,
         )
-        partial = pl.pallas_call(
-            edge_kernel,
-            out_shape=jax.ShapeDtypeStruct((rows, traits), F32),
-            in_specs=[VMEM, HBM, HBM],
-            out_specs=HBM,
-            scratch_shapes=[
-                pltpu.VMEM((blocks, band.shape[1] // 2, tile, tile), BF16),
-                pltpu.VMEM((rows, traits), F32),
-                pltpu.VMEM((rows, traits), F32),
-                pltpu.SemaphoreType.DMA((blocks + 3,)),
-            ],
-            compiler_params=EDGE,
-            name="edge",
-        )(outer, band, partial)
         mine = exchange(merged).reshape(half, traits)
-        mine, partial = lax.optimization_barrier((mine, partial))
+        mine, partial, outer = lax.optimization_barrier((mine, partial, outer))
         theirs = other_core(mine)
         out_shape, out_specs = [jax.ShapeDtypeStruct((rows, traits), F32)], [HBM]
         if not last:
@@ -482,7 +457,7 @@
         result = pl.pallas_call(
             functools.partial(step_kernel, cores, last),
             out_shape=tuple(out_shape),
-            in_specs=[SMEM] * 3 + [VMEM] * 3 + [HBM],
+            in_specs=[SMEM] * 3 + [VMEM] * 3 + [HBM] * 3,
             out_specs=tuple(out_specs),
             scratch_shapes=[
                 pltpu.VMEM((rows, traits), F32),
@@ -491,7 +466,8 @@
                 pltpu.VMEM((max(rows, hub_rows), traits), F32),
                 pltpu.VMEM((lr.shape[0], tile, traits), F32),
                 pltpu.VMEM((rows, traits), F32),
-                pltpu.SemaphoreType.DMA((blocks + 4,)),
+                pltpu.VMEM((blocks, band.shape[1] // 2, tile, tile), BF16),
+                pltpu.SemaphoreType.DMA((blocks + 5,)),
             ],
             compiler_params=UPDATE,
             name="step",
@@ -503,6 +479,8 @@
             mine,
             theirs,
             partial,
+            outer,
+            band,
         )
         if last:
             return result[0]

time: 77.7 us -> 72.3 us (0.931)
  waiting for transfers between devices: 21.4 us -> 18.3 us
  Pallas kernels: 28.3 us -> 25.9 us
    pallas_call x2 -> x0, Pallas kernels: 5.45 us -> none  [shards(): pl.pallas_call(edge_kernel, out_shape=jax.ShapeDtypeStruct((rows, traits)...]
    all_to_all x4, waiting for transfers between devices: 16.6 us -> 13.5 us  [exchange(): lax.all_to_all(x, 'row', 0, 0, axis_index_groups=order and [list(order)])]
    pallas_call x2, Pallas kernels: 6.51 us -> 8.27 us  [shards(): pl.pallas_call(functools.partial(step_kernel, cores, last), out_shape=tup...]
    pallas_call x2, Pallas kernels: 8.9 us -> 10.2 us  [shards(): pl.pallas_call(functools.partial(band_kernel, cores), out_shape=jax.Shape...]
  transfers between devices with their start and end apart: 14 -> 14, of which waited for: 8 -> 6; matrix products, arithmetic and copies ran while one was open for 0% -> 0% of each run, Pallas kernels for 24% -> 20%
where the time goes in v5:
time: 72.3 us; the launch traced here: 71.8 us
  starting transfers between devices  26.2 us (36%)
  Pallas kernels  25.9 us (36%)
  waiting for transfers between devices  18.3 us (25%)
  local copies, waits for them, and re-layouts  1.04 us (1%)
    all_to_all x4, starting transfers between devices, exchange(): lax.all_to_all(x, 'row', 0, 0, axis_index_groups=order and [list(order)])  23 us
    all_to_all x4, waiting for transfers between devices, exchange(): lax.all_to_all(x, 'row', 0, 0, axis_index_groups=order and [list(order)])  13.5 us
    pallas_call x2, Pallas kernels, shards(): pl.pallas_call(functools.partial(band_kernel, cores), out_shape=jax.Shape...  10.2 us
    pallas_call x2, Pallas kernels, shards(): pl.pallas_call(functools.partial(step_kernel, cores, last), out_shape=tup...  8.27 us
    ppermute x8, waiting for transfers between devices, other_core(): return lax.ppermute(x, 'col', swap)  4.85 us
    pallas_call x1, Pallas kernels, shards(): pl.pallas_call(functools.partial(first_kernel, cores), out_shape=(panel_t...  3.16 us
    pallas_call x2, Pallas kernels, shards(): pl.pallas_call(functools.partial(merge_kernel, cores, tile, blocks * core...  2.71 us
    ppermute x8, starting transfers between devices, other_core(): return lax.ppermute(x, 'col', swap)  1.84 us
  transfers between devices with their start and end apart: 14, of which 6 were waited for; matrix products, arithmetic and copies ran while one was open for 0% of the time, Pallas kernels for 20%

profile of v5, /device:TPU:0, one launch (start us, length us, event | category | flops | bytes accessed | tf_op | source)
XLA Modules:
  0.0 71.8 jit_solution(16470130137521762186)
XLA Ops:
  0.0 3.2 %first.1 = (bf16[512,512]{1,0:T(8,128)(2,1)}, bf16[512,512]{1,0:T(8,128)(2,1)}, bf16[256,512]{1,0:T(8,128)(2,1)}, bf16[256,512]{1,0:T(8,128)(2,1)}) custom-call(s32[4]{0:T(128)} %blocks_ref.11, s32[8]{0:T(128)} %local_ref.7, s32[8]{0:T(128)} %hub_ref.7, f32[512,512]{1,0:T(8,128)} %current_hbm.1, bf16[8,128,128]{2,1,0:T(8,128)(2,1)} %lr_ref.3), custom_call_target="tpu_custom_call" | custom-call | tf_op jit(solution)/shard_map/first/pallas_call | solution.py:371
  3.2 0.5 collective-permute-start
  3.7 0.1 collective-permute-start.1
  3.8 0.4 collective-permute-start.2
  4.2 0.9 %collective-permute-done.came_ref = bf16[256,512]{1,0:T(8,128)(2,1)S(1)} collective-permute-done((bf16[256,512]{1,0:T(8,128)(2,1)}, bf16[256,512]{1,0:T(8,128)(2,1)S(1)}, u32[]{:S(2)}, u32[]{:S(2)}) %collective-permute-start) | collective-permute-done | bytes 262176 | tf_op jit(solution)/shard_map/ppermute | solution.py:363
  5.1 0.9 %copy-done.6 = bf16[256,512]{1,0:T(8,128)(2,1)S(1)} copy-done((bf16[256,512]{1,0:T(8,128)(2,1)S(1)}, bf16[256,512]{1,0:T(8,128)(2,1)}, u32[]{:S(2)}) %copy-start.6) | copy-done | bytes 262168
  6.0 0.8 %join.2 = bf16[256,512]{1,0:T(8,128)(2,1)} custom-call(bf16[256,512]{1,0:T(8,128)(2,1)S(1)} %copy-done.6, bf16[256,512]{1,0:T(8,128)(2,1)S(1)} %collective-permute-done.came_ref), custom_call_target="tpu_custom_call" | custom-call | tf_op jit(solution)/shard_map/join/pallas_call | solution.py:397
  6.8 7.7 %all-to-all-start = ((bf16[8,32,512]{2,1,0:T(8,128)(2,1)}), bf16[8,32,512]{2,1,0:T(8,128)(2,1)S(1)}, u32[]{:S(2)}, u32[]{:S(2)}) async-start(bf16[8,32,512]{2,1,0:T(8,128)(2,1)} %bitcast), calls=%async_computation | async-start | bytes 524288 | tf_op jit(solution)/shard_map/all_to_all | solution.py:368
  14.5 0.0 copy-done.16
  14.5 0.7 collective-permute-start.3
  15.2 0.0 collective-permute-done.1.rest_0_.other_hbm
  15.2 0.0 copy-start.3
  15.2 0.0 collective-permute-done.2.rest_1_.back_other_hbm
  15.2 0.0 copy-start.5
  15.3 6.7 %all-to-all-done.in_ref = bf16[8,32,512]{2,1,0:T(8,128)(2,1)S(1)} async-done(((bf16[8,32,512]{2,1,0:T(8,128)(2,1)}), bf16[8,32,512]{2,1,0:T(8,128)(2,1)S(1)}, u32[]{:S(2)}, u32[]{:S(2)}) %all-to-all-start) | async-done | bytes 262176 | tf_op jit(solution)/shard_map/all_to_all | solution.py:368
  22.0 0.0 copy-done.7
  22.0 1.4 %merge.2 = bf16[8,32,512]{2,1,0:T(8,128)(2,1)} custom-call(s32[4]{0:T(128)S(1)} %copy-done.7, bf16[8,32,512]{2,1,0:T(8,128)(2,1)S(1)} %all-to-all-done.in_ref, bf16[512,512]{1,0:T(8,128)(2,1)S(1)} %collective-permute-done.1.rest_0_.other_hbm, bf16[512,512]{1,0:T(8,128)(2,1)S(1)} %collective-permute-done.2.rest_1_.back_other_hbm), custom_call_target="tpu_custom_call" | custom-call | tf_op jit(solution)/shard_map/merge/pallas_call | solution.py:406
  23.3 5.1 %all-to-all-start.1 = ((bf16[8,32,512]{2,1,0:T(8,128)(2,1)}), bf16[8,32,512]{2,1,0:T(8,128)(2,1)S(1)}, u32[]{:S(2)}, u32[]{:S(2)}) async-start(bf16[8,32,512]{2,1,0:T(8,128)(2,1)} %merge.2), calls=%async_computation.1 | async-start | bytes 524288 | tf_op jit(solution)/shard_map/all_to_all | solution.py:368
  28.4 0.0 copy-done.3
  28.4 0.0 copy-done.5
  28.4 0.0 copy-start
  28.4 0.0 copy-start.8
  28.4 0.0 copy-start.10
  28.5 0.0 copy-start.12
  28.5 5.1 %band.2.partial_hbm = f32[512,512]{1,0:T(8,128)} custom-call(s32[4]{0:T(128)} %blocks_ref.11, s32[8]{0:T(128)} %local_ref.7, s32[8]{0:T(128)} %hub_ref.7, f32[512,512]{1,0:T(8,128)} %current_hbm.1, f32[512,512]{1,0:T(8,128)} %zscores_hbm.3, f32[1,512]{1,0:T(1,128)} %bitcast.9, bf16[4,9,128,128]{3,2,1,0:T(8,128)(2,1)} %band_hbm.7, ...), custom_call_target="tpu_custom_call" | custom-call | flops 1000000 | bytes 1048576 | tf_op jit(solution)/shard_map/band/pallas_call | solution.py:414
  33.6 0.0 collective-permute-done.3.outer_hbm
  33.6 0.0 copy-start.14
  33.6 0.0 all-to-all-done.1
  33.6 0.1 collective-permute-start.4
  33.7 1.5 %collective-permute-done.4.half_other_ref = bf16[256,512]{1,0:T(8,128)(2,1)S(1)} collective-permute-done((bf16[256,512]{1,0:T(8,128)(2,1)S(1)}, bf16[256,512]{1,0:T(8,128)(2,1)S(1)}, u32[]{:S(2)}, u32[]{:S(2)}) %collective-permute-start.4) | collective-permute-done | bytes 262176 | tf_op jit(solution)/shard_map/ppermute | solution.py:363
  35.2 0.0 copy-done.14
  35.2 0.0 copy-done
  35.2 0.0 copy-done.8
  35.2 0.0 copy-done.10
  35.3 0.0 copy-done.12
  35.3 4.6 %step.2 = (f32[512,512]{1,0:T(8,128)}, bf16[512,512]{1,0:T(8,128)(2,1)}, bf16[512,512]{1,0:T(8,128)(2,1)}, bf16[256,512]{1,0:T(8,128)(2,1)S(1)}, bf16[256,512]{1,0:T(8,128)(2,1)S(1)}) custom-call(s32[4]{0:T(128)S(1)} %copy-done.8, s32[8]{0:T(128)S(1)} %copy-done.10, s32[8]{0:T(128)S(1)} %copy-done.12, bf16[8,128,128]{2,1,0:T(8,128)(2,1)S(1)} %copy-done, ...), custom_call_target="tpu_custom_call" | custom-call | tf_op jit(solution)/shard_map/step/pallas_call | solution.py:457
  39.9 0.0 copy-start.15
  39.9 0.2 collective-permute-start.5
  40.1 0.4 collective-permute-start.6
  40.5 0.1 collective-permute-start.7
  40.6 0.9 %collective-permute-done.5.came_ref = bf16[256,512]{1,0:T(8,128)(2,1)S(1)} collective-permute-done((bf16[256,512]{1,0:T(8,128)(2,1)S(1)}, bf16[256,512]{1,0:T(8,128)(2,1)S(1)}, u32[]{:S(2)}, u32[]{:S(2)}) %collective-permute-start.5) | collective-permute-done | bytes 262176 | tf_op jit(solution)/shard_map/ppermute | solution.py:363
  41.5 0.8 %join.3 = bf16[256,512]{1,0:T(8,128)(2,1)} custom-call(bf16[256,512]{1,0:T(8,128)(2,1)S(1)} %get-tuple-element.27.keep_ref, bf16[256,512]{1,0:T(8,128)(2,1)S(1)} %collective-permute-done.5.came_ref), custom_call_target="tpu_custom_call" | custom-call | tf_op jit(solution)/shard_map/join/pallas_call | solution.py:397
  42.3 5.1 %all-to-all-start.2 = ((bf16[8,32,512]{2,1,0:T(8,128)(2,1)}), bf16[8,32,512]{2,1,0:T(8,128)(2,1)S(1)}, u32[]{:S(2)}, u32[]{:S(2)}) async-start(bf16[8,32,512]{2,1,0:T(8,128)(2,1)} %bitcast.3), calls=%async_computation.2 | async-start | bytes 524288 | tf_op jit(solution)/shard_map/all_to_all | solution.py:368
  47.4 0.0 copy-done.15
  47.4 0.7 collective-permute-start.8
  48.1 0.0 collective-permute-done.6.rest_0_.other_hbm
  48.1 0.0 copy-start.2
  48.1 0.0 collective-permute-done.7.rest_1_.back_other_hbm
  48.1 0.0 copy-start.4
  48.1 6.7 %all-to-all-done.2.in_ref = bf16[8,32,512]{2,1,0:T(8,128)(2,1)S(1)} async-done(((bf16[8,32,512]{2,1,0:T(8,128)(2,1)}), bf16[8,32,512]{2,1,0:T(8,128)(2,1)S(1)}, u32[]{:S(2)}, u32[]{:S(2)}) %all-to-all-start.2) | async-done | bytes 262176 | tf_op jit(solution)/shard_map/all_to_all | solution.py:368
  54.9 1.4 %merge.3 = bf16[8,32,512]{2,1,0:T(8,128)(2,1)} custom-call(s32[4]{0:T(128)S(1)} %copy-done.8, bf16[8,32,512]{2,1,0:T(8,128)(2,1)S(1)} %all-to-all-done.2.in_ref, bf16[512,512]{1,0:T(8,128)(2,1)S(1)} %collective-permute-done.6.rest_0_.other_hbm, bf16[512,512]{1,0:T(8,128)(2,1)S(1)} %collective-permute-done.7.rest_1_.back_other_hbm), custom_call_target="tpu_custom_call" | custom-call | tf_op jit(solution)/shard_map/merge/pallas_call | solution.py:406
  56.2 5.1 %all-to-all-start.3 = ((bf16[8,32,512]{2,1,0:T(8,128)(2,1)}), bf16[8,32,512]{2,1,0:T(8,128)(2,1)S(1)}, u32[]{:S(2)}, u32[]{:S(2)}) async-start(bf16[8,32,512]{2,1,0:T(8,128)(2,1)} %merge.3), calls=%async_computation.3 | async-start | bytes 524288 | tf_op jit(solution)/shard_map/all_to_all | solution.py:368
  61.3 0.0 copy-done.4
  61.3 0.0 copy-start.1
  61.3 0.0 copy-start.9
  61.3 0.0 copy-start.11
  61.3 0.0 copy-start.13
  61.3 5.1 %band.3.partial_hbm = f32[512,512]{1,0:T(8,128)} custom-call(s32[4]{0:T(128)} %blocks_ref.11, s32[8]{0:T(128)} %local_ref.7, s32[8]{0:T(128)} %hub_ref.7, f32[512,512]{1,0:T(8,128)} %get-tuple-element.31.current_hbm, f32[512,512]{1,0:T(8,128)} %zscores_hbm.3, f32[1,512]{1,0:T(1,128)} %bitcast.10, bf16[4,9,128,128]{3,2,1,0:T(8,128)(2,1)} %band_hbm.7, ...), custom_call_target="tpu_custom_call" | custom-call | flops 1000000 | bytes 1048576 | tf_op jit(solution)/shard_map/band/pallas_call | solution.py:414
  66.5 0.0 collective-permute-done.8.outer_hbm
  66.5 0.0 all-to-all-done.3
  66.5 0.1 collective-permute-start.9
  66.6 1.5 %collective-permute-done.9.half_other_ref = bf16[256,512]{1,0:T(8,128)(2,1)S(1)} collective-permute-done((bf16[256,512]{1,0:T(8,128)(2,1)S(1)}, bf16[256,512]{1,0:T(8,128)(2,1)S(1)}, u32[]{:S(2)}, u32[]{:S(2)}) %collective-permute-start.9) | collective-permute-done | bytes 262176 | tf_op jit(solution)/shard_map/ppermute | solution.py:363
  68.1 0.0 copy-done.1
  68.1 3.6 %step.3 = f32[512,512]{1,0:T(8,128)} custom-call(s32[4]{0:T(128)S(1)} %copy-done.9, s32[8]{0:T(128)S(1)} %copy-done.11, s32[8]{0:T(128)S(1)} %copy-done.13, bf16[8,128,128]{2,1,0:T(8,128)(2,1)S(1)} %copy-done.1, bf16[256,512]{1,0:T(8,128)(2,1)S(1)} %bitcast.8, bf16[256,512]{1,0:T(8,128)(2,1)S(1)} %collective-permute-done.9.half_other_ref, ...), custom_call_target="tpu_custom_call" | custom-call | tf_op jit(solution)/shard_map/step/pallas_call | solution.py:457
  (7 shorter events, 0.0 us)
Async XLA Ops:
  0.0 22.0 %copy-start.7 = (s32[4]{0:T(128)S(1)}, s32[4]{0:T(128)}, u32[]{:S(2)}) copy-start(s32[4]{0:T(128)} %blocks_ref.11) | copy-start | bytes 52
  3.2 1.9 %collective-permute-start = (bf16[256,512]{1,0:T(8,128)(2,1)}, bf16[256,512]{1,0:T(8,128)(2,1)S(1)}, u32[]{:S(2)}, u32[]{:S(2)}) collective-permute-start(bf16[256,512]{1,0:T(8,128)(2,1)} %get-tuple-element.21), channel_id=1, source_target_pairs={{0,1},{1,0},{2,3},{3,2},{4,5},{5,4},{6,7},{7,6},{8,9},{9,8},{10,11... | collective-permute-start | bytes 786440 | tf_op jit(solution)/shard_map/ppermute | solution.py:363
  3.7 11.5 %collective-permute-start.1 = (bf16[512,512]{1,0:T(8,128)(2,1)}, bf16[512,512]{1,0:T(8,128)(2,1)S(1)}, u32[]{:S(2)}, u32[]{:S(2)}) collective-permute-start(bf16[512,512]{1,0:T(8,128)(2,1)} %get-tuple-element.22.mine_hbm), channel_id=1, source_target_pairs={{0,1},{1,0},{2,3},{3,2},{4,5},{5,4},{6,7},{7,6},{8,9},{9,8},{10,11... | collective-permute-start | bytes 1572872 | tf_op jit(solution)/shard_map/ppermute | solution.py:363
  3.8 11.5 %collective-permute-start.2 = (bf16[512,512]{1,0:T(8,128)(2,1)}, bf16[512,512]{1,0:T(8,128)(2,1)S(1)}, u32[]{:S(2)}, u32[]{:S(2)}) collective-permute-start(bf16[512,512]{1,0:T(8,128)(2,1)} %get-tuple-element.23.back_hbm), channel_id=1, source_target_pairs={{0,1},{1,0},{2,3},{3,2},{4,5},{5,4},{6,7},{7,6},{8,9},{9,8},{10,11... | collective-permute-start | bytes 1572872 | tf_op jit(solution)/shard_map/ppermute | solution.py:363
  5.1 0.9 %copy-start.6 = (bf16[256,512]{1,0:T(8,128)(2,1)S(1)}, bf16[256,512]{1,0:T(8,128)(2,1)}, u32[]{:S(2)}) copy-start(bf16[256,512]{1,0:T(8,128)(2,1)} %get-tuple-element.20.keep_ref) | copy-start | bytes 786436
  6.0 8.5 %copy-start.16 = (bf16[512,512]{1,0:T(8,128)(2,1)S(1)}, bf16[512,512]{1,0:T(8,128)(2,1)}, u32[]{:S(2)}) copy-start(bf16[512,512]{1,0:T(8,128)(2,1)} %get-tuple-element.22.mine_hbm) | copy-start | bytes 1572868
  6.8 15.2 %all-to-all-start = ((bf16[8,32,512]{2,1,0:T(8,128)(2,1)}), bf16[8,32,512]{2,1,0:T(8,128)(2,1)S(1)}, u32[]{:S(2)}, u32[]{:S(2)}) async-start(bf16[8,32,512]{2,1,0:T(8,128)(2,1)} %bitcast), calls=%async_computation | async-start | bytes 524288 | tf_op jit(solution)/shard_map/all_to_all | solution.py:368
  14.5 19.1 %collective-permute-start.3 = (bf16[512,512]{1,0:T(8,128)(2,1)S(1)}, bf16[512,512]{1,0:T(8,128)(2,1)S(1)}, u32[]{:S(2)}, u32[]{:S(2)}) collective-permute-start(bf16[512,512]{1,0:T(8,128)(2,1)S(1)} %copy-done.16), channel_id=1, source_target_pairs={{1,2},{3,4},{5,6},{7,8},{9,10},{11,12},{13,14},{2,1},{4,3},{6,5},{... | collective-permute-start | bytes 1572872 | tf_op jit(solution)/shard_map/ppermute | solution.py:393
  15.2 13.2 %copy-start.3 = (bf16[512,512]{1,0:T(8,128)(2,1)}, bf16[512,512]{1,0:T(8,128)(2,1)S(1)}, u32[]{:S(2)}) copy-start(bf16[512,512]{1,0:T(8,128)(2,1)S(1)} %collective-permute-done.1.rest_0_.other_hbm) | copy-start | bytes 1572868
  15.2 13.2 %copy-start.5 = (bf16[512,512]{1,0:T(8,128)(2,1)}, bf16[512,512]{1,0:T(8,128)(2,1)S(1)}, u32[]{:S(2)}) copy-start(bf16[512,512]{1,0:T(8,128)(2,1)S(1)} %collective-permute-done.2.rest_1_.back_other_hbm) | copy-start | bytes 1572868
  23.3 10.3 %all-to-all-start.1 = ((bf16[8,32,512]{2,1,0:T(8,128)(2,1)}), bf16[8,32,512]{2,1,0:T(8,128)(2,1)S(1)}, u32[]{:S(2)}, u32[]{:S(2)}) async-start(bf16[8,32,512]{2,1,0:T(8,128)(2,1)} %merge.2), calls=%async_computation.1 | async-start | bytes 524288 | tf_op jit(solution)/shard_map/all_to_all | solution.py:368
  28.4 6.8 %copy-start = (bf16[8,128,128]{2,1,0:T(8,128)(2,1)S(1)}, bf16[8,128,128]{2,1,0:T(8,128)(2,1)}, u32[]{:S(2)}) copy-start(bf16[8,128,128]{2,1,0:T(8,128)(2,1)} %lr_ref.3) | copy-start | bytes 786436
  28.4 6.8 %copy-start.8 = (s32[4]{0:T(128)S(1)}, s32[4]{0:T(128)}, u32[]{:S(2)}) copy-start(s32[4]{0:T(128)} %blocks_ref.11) | copy-start | bytes 52
  28.4 6.8 %copy-start.10 = (s32[8]{0:T(128)S(1)}, s32[8]{0:T(128)}, u32[]{:S(2)}) copy-start(s32[8]{0:T(128)} %local_ref.7) | copy-start | bytes 100
  28.5 6.8 %copy-start.12 = (s32[8]{0:T(128)S(1)}, s32[8]{0:T(128)}, u32[]{:S(2)}) copy-start(s32[8]{0:T(128)} %hub_ref.7) | copy-start | bytes 100
  33.6 1.6 %copy-start.14 = (bf16[512,512]{1,0:T(8,128)(2,1)}, bf16[512,512]{1,0:T(8,128)(2,1)S(1)}, u32[]{:S(2)}) copy-start(bf16[512,512]{1,0:T(8,128)(2,1)S(1)} %collective-permute-done.3.outer_hbm) | copy-start | bytes 1572868
  33.6 1.6 %collective-permute-start.4 = (bf16[256,512]{1,0:T(8,128)(2,1)S(1)}, bf16[256,512]{1,0:T(8,128)(2,1)S(1)}, u32[]{:S(2)}, u32[]{:S(2)}) collective-permute-start(bf16[256,512]{1,0:T(8,128)(2,1)S(1)} %bitcast.5), channel_id=1, source_target_pairs={{0,1},{1,0},{2,3},{3,2},{4,5},{5,4},{6,7},{7,6},{8,9},{9,8},{10,11... | collective-permute-start | bytes 786440 | tf_op jit(solution)/shard_map/ppermute | solution.py:363
  39.9 7.5 %copy-start.15 = (bf16[512,512]{1,0:T(8,128)(2,1)S(1)}, bf16[512,512]{1,0:T(8,128)(2,1)}, u32[]{:S(2)}) copy-start(bf16[512,512]{1,0:T(8,128)(2,1)} %get-tuple-element.29.mine_hbm) | copy-start | bytes 1572868
  39.9 1.6 %collective-permute-start.5 = (bf16[256,512]{1,0:T(8,128)(2,1)S(1)}, bf16[256,512]{1,0:T(8,128)(2,1)S(1)}, u32[]{:S(2)}, u32[]{:S(2)}) collective-permute-start(bf16[256,512]{1,0:T(8,128)(2,1)S(1)} %get-tuple-element.28), channel_id=1, source_target_pairs={{0,1},{1,0},{2,3},{3,2},{4,5},{5,4},{6,7},{7,6},{8,9},{9,8},{10,11... | collective-permute-start | bytes 786440 | tf_op jit(solution)/shard_map/ppermute | solution.py:363
  40.1 8.0 %collective-permute-start.6 = (bf16[512,512]{1,0:T(8,128)(2,1)}, bf16[512,512]{1,0:T(8,128)(2,1)S(1)}, u32[]{:S(2)}, u32[]{:S(2)}) collective-permute-start(bf16[512,512]{1,0:T(8,128)(2,1)} %get-tuple-element.29.mine_hbm), channel_id=1, source_target_pairs={{0,1},{1,0},{2,3},{3,2},{4,5},{5,4},{6,7},{7,6},{8,9},{9,8},{10,11... | collective-permute-start | bytes 1572872 | tf_op jit(solution)/shard_map/ppermute | solution.py:363
  40.5 7.6 %collective-permute-start.7 = (bf16[512,512]{1,0:T(8,128)(2,1)}, bf16[512,512]{1,0:T(8,128)(2,1)S(1)}, u32[]{:S(2)}, u32[]{:S(2)}) collective-permute-start(bf16[512,512]{1,0:T(8,128)(2,1)} %get-tuple-element.30.back_hbm), channel_id=1, source_target_pairs={{0,1},{1,0},{2,3},{3,2},{4,5},{5,4},{6,7},{7,6},{8,9},{9,8},{10,11... | collective-permute-start | bytes 1572872 | tf_op jit(solution)/shard_map/ppermute | solution.py:363
  42.3 12.6 %all-to-all-start.2 = ((bf16[8,32,512]{2,1,0:T(8,128)(2,1)}), bf16[8,32,512]{2,1,0:T(8,128)(2,1)S(1)}, u32[]{:S(2)}, u32[]{:S(2)}) async-start(bf16[8,32,512]{2,1,0:T(8,128)(2,1)} %bitcast.3), calls=%async_computation.2 | async-start | bytes 524288 | tf_op jit(solution)/shard_map/all_to_all | solution.py:368
  47.4 19.1 %collective-permute-start.8 = (bf16[512,512]{1,0:T(8,128)(2,1)S(1)}, bf16[512,512]{1,0:T(8,128)(2,1)S(1)}, u32[]{:S(2)}, u32[]{:S(2)}) collective-permute-start(bf16[512,512]{1,0:T(8,128)(2,1)S(1)} %copy-done.15), channel_id=1, source_target_pairs={{1,2},{3,4},{5,6},{7,8},{9,10},{11,12},{13,14},{2,1},{4,3},{6,5},{... | collective-permute-start | bytes 1572872 | tf_op jit(solution)/shard_map/ppermute | solution.py:393
  48.1 13.2 %copy-start.2 = (bf16[512,512]{1,0:T(8,128)(2,1)}, bf16[512,512]{1,0:T(8,128)(2,1)S(1)}, u32[]{:S(2)}) copy-start(bf16[512,512]{1,0:T(8,128)(2,1)S(1)} %collective-permute-done.6.rest_0_.other_hbm) | copy-start | bytes 1572868
  48.1 13.2 %copy-start.4 = (bf16[512,512]{1,0:T(8,128)(2,1)}, bf16[512,512]{1,0:T(8,128)(2,1)S(1)}, u32[]{:S(2)}) copy-start(bf16[512,512]{1,0:T(8,128)(2,1)S(1)} %collective-permute-done.7.rest_1_.back_other_hbm) | copy-start | bytes 1572868
  56.2 10.3 %all-to-all-start.3 = ((bf16[8,32,512]{2,1,0:T(8,128)(2,1)}), bf16[8,32,512]{2,1,0:T(8,128)(2,1)S(1)}, u32[]{:S(2)}, u32[]{:S(2)}) async-start(bf16[8,32,512]{2,1,0:T(8,128)(2,1)} %merge.3), calls=%async_computation.3 | async-start | bytes 524288 | tf_op jit(solution)/shard_map/all_to_all | solution.py:368
  61.3 6.8 %copy-start.1 = (bf16[8,128,128]{2,1,0:T(8,128)(2,1)S(1)}, bf16[8,128,128]{2,1,0:T(8,128)(2,1)}, u32[]{:S(2)}) copy-start(bf16[8,128,128]{2,1,0:T(8,128)(2,1)} %lr_ref.3) | copy-start | bytes 786436
  61.3 6.8 %copy-start.9 = (s32[4]{0:T(128)S(1)}, s32[4]{0:T(128)}, u32[]{:S(2)}) copy-start(s32[4]{0:T(128)} %blocks_ref.11) | copy-start | bytes 52
  61.3 6.8 %copy-start.11 = (s32[8]{0:T(128)S(1)}, s32[8]{0:T(128)}, u32[]{:S(2)}) copy-start(s32[8]{0:T(128)} %local_ref.7) | copy-start | bytes 100
  61.3 6.8 %copy-start.13 = (s32[8]{0:T(128)S(1)}, s32[8]{0:T(128)}, u32[]{:S(2)}) copy-start(s32[8]{0:T(128)} %hub_ref.7) | copy-start | bytes 100
  66.5 1.6 %collective-permute-start.9 = (bf16[256,512]{1,0:T(8,128)(2,1)S(1)}, bf16[256,512]{1,0:T(8,128)(2,1)S(1)}, u32[]{:S(2)}, u32[]{:S(2)}) collective-permute-start(bf16[256,512]{1,0:T(8,128)(2,1)S(1)} %bitcast.7), channel_id=1, source_target_pairs={{0,1},{1,0},{2,3},{3,2},{4,5},{5,4},{6,7},{7,6},{8,9},{9,8},{10,11... | collective-permute-start | bytes 786440 | tf_op jit(solution)/shard_map/ppermute | solution.py:363

commit v6 on v5

--- a/solution.py
+++ b/solution.py
@@ -30,7 +30,7 @@
     return lax.dot_general(a, b, (((0,), (0,)), ((), ())), preferred_element_type=F32)
 
 
-ORDERS = {8: (4, 6, 1, 5, 0, 2, 7, 3)}
+ORDERS = {8: (3, 6, 1, 0, 7, 5, 4, 2)}
 
 
 def position(chip, chips):
@@ -98,18 +98,25 @@
 
 
 def first_kernel(cores, *refs):
-    sources, (panel_ref, back_ref, keep_ref, send_ref, acc_ref) = refs[:5], refs[5:10]
-    held, (sems, term_ref) = refs[10:15], refs[15:]
+    sources, outs, acc_ref = refs[:5], refs[5:9], refs[9]
+    held, (sems, term_ref) = refs[10:15], refs[15:17]
+    panel_ref, back_ref, keep_ref, send_ref = refs[17:21]
     for copy in fetch(list(zip(sources, held)), sems):
         copy.wait()
     blocks_ref, local_ref, hub_ref, effects_ref, lr_ref = held
     panel_ref[...] = effects_ref[...].astype(BF16)
+    done = fetch([(panel_ref, outs[0])], sems.at[pl.ds(5, 1)])
     back_terms(local_ref, hub_ref, lr_ref, panel_ref, term_ref, acc_ref, back_ref)
     contributions(cores, blocks_ref, back_ref, panel_ref, keep_ref, send_ref)
+    done += fetch(
+        [(send_ref, outs[3]), (keep_ref, outs[2]), (back_ref, outs[1])], sems.at[pl.ds(6, 3)]
+    )
+    for copy in done:
+        copy.wait()
 
 
 def merge_kernel(cores, tile, per_chip, blocks_ref, in_ref, *rest):
-    *_, out_ref = rest
+    *_, out_hbm, out_ref, sems = rest
     me, core = lax.axis_index("row"), lax.axis_index("col")
     chips, rows, _ = in_ref.shape
     hub = (core * (chips * rows) + position(me, chips) * rows) // tile
@@ -120,12 +127,18 @@
 
     def put(p, carry):
         out_ref[p] = jnp.where(p == owner, total, state)
+        pltpu.make_async_copy(out_ref.at[p], out_hbm.at[p], sems.at[p]).start()
+        return carry
+
+    def finish(p, carry):
+        pltpu.make_async_copy(out_ref.at[p], out_hbm.at[p], sems.at[p]).wait()
         return carry
 
     zero = jnp.zeros(in_ref.shape[1:], F32)
     total = lax.fori_loop(0, chips, add, zero, unroll=chips <= 16).astype(BF16)
     state = in_ref[owner]
     lax.fori_loop(0, chips, put, 0, unroll=chips <= 16)
+    lax.fori_loop(0, chips, finish, 0, unroll=chips <= 16)
 
 
 def band_kernel(
@@ -372,7 +385,7 @@
         functools.partial(first_kernel, cores),
         out_shape=(panel_type, back_type, half_type, half_type),
         in_specs=[HBM] * 5,
-        out_specs=(VMEM,) * 4,
+        out_specs=(HBM,) * 4,
         scratch_shapes=[
             pltpu.VMEM((hub_rows, traits), F32),
             pltpu.SMEM(hub_blocks.shape, jnp.int32),
@@ -380,8 +393,12 @@
             pltpu.SMEM(lr_hub.shape, jnp.int32),
             pltpu.VMEM(effects.shape, F32),
             pltpu.VMEM(lr.shape, BF16),
-            pltpu.SemaphoreType.DMA((5,)),
+            pltpu.SemaphoreType.DMA((9,)),
             pltpu.VMEM((lr.shape[0], tile, traits), F32),
+            pltpu.VMEM((rows, traits), BF16),
+            pltpu.VMEM((hub_rows, traits), BF16),
+            pltpu.VMEM((half, traits), BF16),
+            pltpu.VMEM((half, traits), BF16),
         ],
         compiler_params=FIRST,
         name="first",
@@ -407,7 +424,11 @@
             functools.partial(merge_kernel, cores, tile, blocks * cores),
             out_shape=jax.ShapeDtypeStruct(gathered.shape, BF16),
             in_specs=[SMEM, VMEM, ANY, ANY],
-            out_specs=VMEM,
+            out_specs=HBM,
+            scratch_shapes=[
+                pltpu.VMEM(gathered.shape, BF16),
+                pltpu.SemaphoreType.DMA((rows_dev,)),
+            ],
             compiler_params=MERGE,
             name="merge",
         )(hub_blocks, gathered, other, back_other)

time: 72.3 us -> 71.6 us (level)
  Pallas kernels: 25.9 us -> 24.8 us
    pallas_call x2, Pallas kernels: 10.2 us -> 9.14 us  [shards(): pl.pallas_call(functools.partial(band_kernel, cores), out_shape=jax.Shape...]
  transfers between devices with their start and end apart: 14 -> 14, of which waited for: 6 -> 8; matrix products, arithmetic and copies ran while one was open for 0% -> 0% of each run, Pallas kernels for 20% -> 19%
where the time goes in v6:
time: 71.6 us; the launch traced here: 70.9 us
  starting transfers between devices  26.2 us (37%)
  Pallas kernels  24.8 us (35%)
  waiting for transfers between devices  18.7 us (26%)
  local copies, waits for them, and re-layouts  1.04 us (1%)
    all_to_all x4, starting transfers between devices, exchange(): lax.all_to_all(x, 'row', 0, 0, axis_index_groups=order and [list(order)])  23.1 us
    all_to_all x4, waiting for transfers between devices, exchange(): lax.all_to_all(x, 'row', 0, 0, axis_index_groups=order and [list(order)])  13.8 us
    pallas_call x2, Pallas kernels, shards(): pl.pallas_call(functools.partial(band_kernel, cores), out_shape=jax.Shape...  9.14 us
    pallas_call x2, Pallas kernels, shards(): pl.pallas_call(functools.partial(step_kernel, cores, last), out_shape=tup...  8.23 us
    ppermute x8, waiting for transfers between devices, other_core(): return lax.ppermute(x, 'col', swap)  4.86 us
    pallas_call x1, Pallas kernels, shards(): pl.pallas_call(functools.partial(first_kernel, cores), out_shape=(panel_t...  3.05 us
    pallas_call x2, Pallas kernels, shards(): pl.pallas_call(functools.partial(merge_kernel, cores, tile, blocks * core...  2.82 us
    ppermute x8, starting transfers between devices, other_core(): return lax.ppermute(x, 'col', swap)  1.72 us
  transfers between devices with their start and end apart: 14, of which 8 were waited for; matrix products, arithmetic and copies ran while one was open for 0% of the time, Pallas kernels for 19%

profile of v6, /device:TPU:0, one launch (start us, length us, event | category | flops | bytes accessed | tf_op | source)
XLA Modules:
  0.0 70.9 jit_solution(10135870486232127992)
XLA Ops:
  0.0 3.0 %first.1 = (bf16[512,512]{1,0:T(8,128)(2,1)}, bf16[512,512]{1,0:T(8,128)(2,1)}, bf16[256,512]{1,0:T(8,128)(2,1)}, bf16[256,512]{1,0:T(8,128)(2,1)}) custom-call(s32[4]{0:T(128)} %blocks_ref.11, s32[8]{0:T(128)} %local_ref.7, s32[8]{0:T(128)} %hub_ref.7, f32[512,512]{1,0:T(8,128)} %current_hbm.1, bf16[8,128,128]{2,1,0:T(8,128)(2,1)} %lr_ref.3), custom_call_target="tpu_custom_call" | custom-call | tf_op jit(solution)/shard_map/first/pallas_call | solution.py:384
  3.1 0.5 collective-permute-start
  3.6 0.1 collective-permute-start.1
  3.7 0.4 collective-permute-start.2
  4.1 0.9 %collective-permute-done.came_ref = bf16[256,512]{1,0:T(8,128)(2,1)S(1)} collective-permute-done((bf16[256,512]{1,0:T(8,128)(2,1)}, bf16[256,512]{1,0:T(8,128)(2,1)S(1)}, u32[]{:S(2)}, u32[]{:S(2)}) %collective-permute-start) | collective-permute-done | bytes 262176 | tf_op jit(solution)/shard_map/ppermute | solution.py:376
  5.0 0.9 %copy-done.6 = bf16[256,512]{1,0:T(8,128)(2,1)S(1)} copy-done((bf16[256,512]{1,0:T(8,128)(2,1)S(1)}, bf16[256,512]{1,0:T(8,128)(2,1)}, u32[]{:S(2)}) %copy-start.6) | copy-done | bytes 262168
  5.9 0.8 %join.2 = bf16[256,512]{1,0:T(8,128)(2,1)} custom-call(bf16[256,512]{1,0:T(8,128)(2,1)S(1)} %copy-done.6, bf16[256,512]{1,0:T(8,128)(2,1)S(1)} %collective-permute-done.came_ref), custom_call_target="tpu_custom_call" | custom-call | tf_op jit(solution)/shard_map/join/pallas_call | solution.py:414
  6.7 7.7 %all-to-all-start = ((bf16[8,32,512]{2,1,0:T(8,128)(2,1)}), bf16[8,32,512]{2,1,0:T(8,128)(2,1)S(1)}, u32[]{:S(2)}, u32[]{:S(2)}) async-start(bf16[8,32,512]{2,1,0:T(8,128)(2,1)} %bitcast), calls=%async_computation | async-start | bytes 524288 | tf_op jit(solution)/shard_map/all_to_all | solution.py:381
  14.4 0.0 copy-done.16
  14.4 0.7 collective-permute-start.3
  15.1 0.0 collective-permute-done.1.rest_0_.other_hbm
  15.1 0.0 copy-start.3
  15.1 0.0 collective-permute-done.2.rest_1_.back_other_hbm
  15.1 0.0 copy-start.5
  15.1 6.3 %all-to-all-done.in_ref = bf16[8,32,512]{2,1,0:T(8,128)(2,1)S(1)} async-done(((bf16[8,32,512]{2,1,0:T(8,128)(2,1)}), bf16[8,32,512]{2,1,0:T(8,128)(2,1)S(1)}, u32[]{:S(2)}, u32[]{:S(2)}) %all-to-all-start) | async-done | bytes 262176 | tf_op jit(solution)/shard_map/all_to_all | solution.py:381
  21.4 0.0 copy-done.7
  21.4 1.4 %merge.2 = bf16[8,32,512]{2,1,0:T(8,128)(2,1)} custom-call(s32[4]{0:T(128)S(1)} %copy-done.7, bf16[8,32,512]{2,1,0:T(8,128)(2,1)S(1)} %all-to-all-done.in_ref, bf16[512,512]{1,0:T(8,128)(2,1)S(1)} %collective-permute-done.1.rest_0_.other_hbm, bf16[512,512]{1,0:T(8,128)(2,1)S(1)} %collective-permute-done.2.rest_1_.back_other_hbm), custom_call_target="tpu_custom_call" | custom-call | tf_op jit(solution)/shard_map/merge/pallas_call | solution.py:423
  22.8 5.0 %all-to-all-start.1 = ((bf16[8,32,512]{2,1,0:T(8,128)(2,1)}), bf16[8,32,512]{2,1,0:T(8,128)(2,1)S(1)}, u32[]{:S(2)}, u32[]{:S(2)}) async-start(bf16[8,32,512]{2,1,0:T(8,128)(2,1)} %merge.2), calls=%async_computation.1 | async-start | bytes 524288 | tf_op jit(solution)/shard_map/all_to_all | solution.py:381
  27.8 0.0 copy-done.3
  27.8 0.0 copy-done.5
  27.8 0.0 copy-start
  27.8 0.0 copy-start.8
  27.8 0.0 copy-start.10
  27.8 0.0 copy-start.12
  27.9 4.6 %band.2.partial_hbm = f32[512,512]{1,0:T(8,128)} custom-call(s32[4]{0:T(128)} %blocks_ref.11, s32[8]{0:T(128)} %local_ref.7, s32[8]{0:T(128)} %hub_ref.7, f32[512,512]{1,0:T(8,128)} %current_hbm.1, f32[512,512]{1,0:T(8,128)} %zscores_hbm.3, f32[1,512]{1,0:T(1,128)} %bitcast.9, bf16[4,9,128,128]{3,2,1,0:T(8,128)(2,1)} %band_hbm.7, ...), custom_call_target="tpu_custom_call" | custom-call | flops 1000000 | bytes 1048576 | tf_op jit(solution)/shard_map/band/pallas_call | solution.py:435
  32.4 0.0 collective-permute-done.3.outer_hbm
  32.4 0.0 copy-start.14
  32.5 0.6 all-to-all-done.1
  33.1 0.0 collective-permute-start.4
  33.1 1.5 %collective-permute-done.4.half_other_ref = bf16[256,512]{1,0:T(8,128)(2,1)S(1)} collective-permute-done((bf16[256,512]{1,0:T(8,128)(2,1)S(1)}, bf16[256,512]{1,0:T(8,128)(2,1)S(1)}, u32[]{:S(2)}, u32[]{:S(2)}) %collective-permute-start.4) | collective-permute-done | bytes 262176 | tf_op jit(solution)/shard_map/ppermute | solution.py:376
  34.6 0.0 copy-done.14
  34.6 0.0 copy-done
  34.6 0.0 copy-done.8
  34.6 0.0 copy-done.10
  34.6 0.0 copy-done.12
  34.6 4.6 %step.2 = (f32[512,512]{1,0:T(8,128)}, bf16[512,512]{1,0:T(8,128)(2,1)}, bf16[512,512]{1,0:T(8,128)(2,1)}, bf16[256,512]{1,0:T(8,128)(2,1)S(1)}, bf16[256,512]{1,0:T(8,128)(2,1)S(1)}) custom-call(s32[4]{0:T(128)S(1)} %copy-done.8, s32[8]{0:T(128)S(1)} %copy-done.10, s32[8]{0:T(128)S(1)} %copy-done.12, bf16[8,128,128]{2,1,0:T(8,128)(2,1)S(1)} %copy-done, ...), custom_call_target="tpu_custom_call" | custom-call | tf_op jit(solution)/shard_map/step/pallas_call | solution.py:478
  39.2 0.0 copy-start.15
  39.3 0.2 collective-permute-start.5
  39.4 0.4 collective-permute-start.6
  39.8 0.1 collective-permute-start.7
  39.9 0.9 %collective-permute-done.5.came_ref = bf16[256,512]{1,0:T(8,128)(2,1)S(1)} collective-permute-done((bf16[256,512]{1,0:T(8,128)(2,1)S(1)}, bf16[256,512]{1,0:T(8,128)(2,1)S(1)}, u32[]{:S(2)}, u32[]{:S(2)}) %collective-permute-start.5) | collective-permute-done | bytes 262176 | tf_op jit(solution)/shard_map/ppermute | solution.py:376
  40.9 0.8 %join.3 = bf16[256,512]{1,0:T(8,128)(2,1)} custom-call(bf16[256,512]{1,0:T(8,128)(2,1)S(1)} %get-tuple-element.27.keep_ref, bf16[256,512]{1,0:T(8,128)(2,1)S(1)} %collective-permute-done.5.came_ref), custom_call_target="tpu_custom_call" | custom-call | tf_op jit(solution)/shard_map/join/pallas_call | solution.py:414
  41.6 5.5 %all-to-all-start.2 = ((bf16[8,32,512]{2,1,0:T(8,128)(2,1)}), bf16[8,32,512]{2,1,0:T(8,128)(2,1)S(1)}, u32[]{:S(2)}, u32[]{:S(2)}) async-start(bf16[8,32,512]{2,1,0:T(8,128)(2,1)} %bitcast.3), calls=%async_computation.2 | async-start | bytes 524288 | tf_op jit(solution)/shard_map/all_to_all | solution.py:381
  47.1 0.0 copy-done.15
  47.1 0.7 collective-permute-start.8
  47.8 0.0 collective-permute-done.6.rest_0_.other_hbm
  47.8 0.0 copy-start.2
  47.8 0.0 collective-permute-done.7.rest_1_.back_other_hbm
  47.8 0.0 copy-start.4
  47.8 6.3 %all-to-all-done.2.in_ref = bf16[8,32,512]{2,1,0:T(8,128)(2,1)S(1)} async-done(((bf16[8,32,512]{2,1,0:T(8,128)(2,1)}), bf16[8,32,512]{2,1,0:T(8,128)(2,1)S(1)}, u32[]{:S(2)}, u32[]{:S(2)}) %all-to-all-start.2) | async-done | bytes 262176 | tf_op jit(solution)/shard_map/all_to_all | solution.py:381
  54.1 1.4 %merge.3 = bf16[8,32,512]{2,1,0:T(8,128)(2,1)} custom-call(s32[4]{0:T(128)S(1)} %copy-done.8, bf16[8,32,512]{2,1,0:T(8,128)(2,1)S(1)} %all-to-all-done.2.in_ref, bf16[512,512]{1,0:T(8,128)(2,1)S(1)} %collective-permute-done.6.rest_0_.other_hbm, bf16[512,512]{1,0:T(8,128)(2,1)S(1)} %collective-permute-done.7.rest_1_.back_other_hbm), custom_call_target="tpu_custom_call" | custom-call | tf_op jit(solution)/shard_map/merge/pallas_call | solution.py:423
  55.5 5.0 %all-to-all-start.3 = ((bf16[8,32,512]{2,1,0:T(8,128)(2,1)}), bf16[8,32,512]{2,1,0:T(8,128)(2,1)S(1)}, u32[]{:S(2)}, u32[]{:S(2)}) async-start(bf16[8,32,512]{2,1,0:T(8,128)(2,1)} %merge.3), calls=%async_computation.3 | async-start | bytes 524288 | tf_op jit(solution)/shard_map/all_to_all | solution.py:381
  60.5 0.0 copy-done.2
  60.5 0.0 copy-start.1
  60.5 0.0 copy-start.9
  60.5 0.0 copy-start.11
  60.5 0.0 copy-start.13
  60.5 4.6 %band.3.partial_hbm = f32[512,512]{1,0:T(8,128)} custom-call(s32[4]{0:T(128)} %blocks_ref.11, s32[8]{0:T(128)} %local_ref.7, s32[8]{0:T(128)} %hub_ref.7, f32[512,512]{1,0:T(8,128)} %get-tuple-element.31.current_hbm, f32[512,512]{1,0:T(8,128)} %zscores_hbm.3, f32[1,512]{1,0:T(1,128)} %bitcast.10, bf16[4,9,128,128]{3,2,1,0:T(8,128)(2,1)} %band_hbm.7, ...), custom_call_target="tpu_custom_call" | custom-call | flops 1000000 | bytes 1048576 | tf_op jit(solution)/shard_map/band/pallas_call | solution.py:435
  65.1 0.0 collective-permute-done.8.outer_hbm
  65.1 0.6 all-to-all-done.3
  65.7 0.0 collective-permute-start.9
  65.8 1.5 %collective-permute-done.9.half_other_ref = bf16[256,512]{1,0:T(8,128)(2,1)S(1)} collective-permute-done((bf16[256,512]{1,0:T(8,128)(2,1)S(1)}, bf16[256,512]{1,0:T(8,128)(2,1)S(1)}, u32[]{:S(2)}, u32[]{:S(2)}) %collective-permute-start.9) | collective-permute-done | bytes 262176 | tf_op jit(solution)/shard_map/ppermute | solution.py:376
  67.3 0.0 copy-done.9
  67.3 3.6 %step.3 = f32[512,512]{1,0:T(8,128)} custom-call(s32[4]{0:T(128)S(1)} %copy-done.9, s32[8]{0:T(128)S(1)} %copy-done.11, s32[8]{0:T(128)S(1)} %copy-done.13, bf16[8,128,128]{2,1,0:T(8,128)(2,1)S(1)} %copy-done.1, bf16[256,512]{1,0:T(8,128)(2,1)S(1)} %bitcast.8, bf16[256,512]{1,0:T(8,128)(2,1)S(1)} %collective-permute-done.9.half_other_ref, ...), custom_call_target="tpu_custom_call" | custom-call | tf_op jit(solution)/shard_map/step/pallas_call | solution.py:478
  (7 shorter events, 0.0 us)
Async XLA Ops:
  0.0 21.4 %copy-start.7 = (s32[4]{0:T(128)S(1)}, s32[4]{0:T(128)}, u32[]{:S(2)}) copy-start(s32[4]{0:T(128)} %blocks_ref.11) | copy-start | bytes 52
  3.1 1.9 %collective-permute-start = (bf16[256,512]{1,0:T(8,128)(2,1)}, bf16[256,512]{1,0:T(8,128)(2,1)S(1)}, u32[]{:S(2)}, u32[]{:S(2)}) collective-permute-start(bf16[256,512]{1,0:T(8,128)(2,1)} %get-tuple-element.21), channel_id=1, source_target_pairs={{0,1},{1,0},{2,3},{3,2},{4,5},{5,4},{6,7},{7,6},{8,9},{9,8},{10,11... | collective-permute-start | bytes 786440 | tf_op jit(solution)/shard_map/ppermute | solution.py:376
  3.6 11.5 %collective-permute-start.1 = (bf16[512,512]{1,0:T(8,128)(2,1)}, bf16[512,512]{1,0:T(8,128)(2,1)S(1)}, u32[]{:S(2)}, u32[]{:S(2)}) collective-permute-start(bf16[512,512]{1,0:T(8,128)(2,1)} %get-tuple-element.22.mine_hbm), channel_id=1, source_target_pairs={{0,1},{1,0},{2,3},{3,2},{4,5},{5,4},{6,7},{7,6},{8,9},{9,8},{10,11... | collective-permute-start | bytes 1572872 | tf_op jit(solution)/shard_map/ppermute | solution.py:376
  3.7 11.5 %collective-permute-start.2 = (bf16[512,512]{1,0:T(8,128)(2,1)}, bf16[512,512]{1,0:T(8,128)(2,1)S(1)}, u32[]{:S(2)}, u32[]{:S(2)}) collective-permute-start(bf16[512,512]{1,0:T(8,128)(2,1)} %get-tuple-element.23.back_hbm), channel_id=1, source_target_pairs={{0,1},{1,0},{2,3},{3,2},{4,5},{5,4},{6,7},{7,6},{8,9},{9,8},{10,11... | collective-permute-start | bytes 1572872 | tf_op jit(solution)/shard_map/ppermute | solution.py:376
  5.0 0.9 %copy-start.6 = (bf16[256,512]{1,0:T(8,128)(2,1)S(1)}, bf16[256,512]{1,0:T(8,128)(2,1)}, u32[]{:S(2)}) copy-start(bf16[256,512]{1,0:T(8,128)(2,1)} %get-tuple-element.20.keep_ref) | copy-start | bytes 786436
  5.9 8.5 %copy-start.16 = (bf16[512,512]{1,0:T(8,128)(2,1)S(1)}, bf16[512,512]{1,0:T(8,128)(2,1)}, u32[]{:S(2)}) copy-start(bf16[512,512]{1,0:T(8,128)(2,1)} %get-tuple-element.22.mine_hbm) | copy-start | bytes 1572868
  6.7 14.7 %all-to-all-start = ((bf16[8,32,512]{2,1,0:T(8,128)(2,1)}), bf16[8,32,512]{2,1,0:T(8,128)(2,1)S(1)}, u32[]{:S(2)}, u32[]{:S(2)}) async-start(bf16[8,32,512]{2,1,0:T(8,128)(2,1)} %bitcast), calls=%async_computation | async-start | bytes 524288 | tf_op jit(solution)/shard_map/all_to_all | solution.py:381
  14.4 18.0 %collective-permute-start.3 = (bf16[512,512]{1,0:T(8,128)(2,1)S(1)}, bf16[512,512]{1,0:T(8,128)(2,1)S(1)}, u32[]{:S(2)}, u32[]{:S(2)}) collective-permute-start(bf16[512,512]{1,0:T(8,128)(2,1)S(1)} %copy-done.16), channel_id=1, source_target_pairs={{1,2},{3,4},{5,6},{7,8},{9,10},{11,12},{13,14},{2,1},{4,3},{6,5},{... | collective-permute-start | bytes 1572872 | tf_op jit(solution)/shard_map/ppermute | solution.py:410
  15.1 12.7 %copy-start.3 = (bf16[512,512]{1,0:T(8,128)(2,1)}, bf16[512,512]{1,0:T(8,128)(2,1)S(1)}, u32[]{:S(2)}) copy-start(bf16[512,512]{1,0:T(8,128)(2,1)S(1)} %collective-permute-done.1.rest_0_.other_hbm) | copy-start | bytes 1572868
  15.1 12.7 %copy-start.5 = (bf16[512,512]{1,0:T(8,128)(2,1)}, bf16[512,512]{1,0:T(8,128)(2,1)S(1)}, u32[]{:S(2)}) copy-start(bf16[512,512]{1,0:T(8,128)(2,1)S(1)} %collective-permute-done.2.rest_1_.back_other_hbm) | copy-start | bytes 1572868
  22.8 10.2 %all-to-all-start.1 = ((bf16[8,32,512]{2,1,0:T(8,128)(2,1)}), bf16[8,32,512]{2,1,0:T(8,128)(2,1)S(1)}, u32[]{:S(2)}, u32[]{:S(2)}) async-start(bf16[8,32,512]{2,1,0:T(8,128)(2,1)} %merge.2), calls=%async_computation.1 | async-start | bytes 524288 | tf_op jit(solution)/shard_map/all_to_all | solution.py:381
  27.8 6.8 %copy-start = (bf16[8,128,128]{2,1,0:T(8,128)(2,1)S(1)}, bf16[8,128,128]{2,1,0:T(8,128)(2,1)}, u32[]{:S(2)}) copy-start(bf16[8,128,128]{2,1,0:T(8,128)(2,1)} %lr_ref.3) | copy-start | bytes 786436
  27.8 6.8 %copy-start.8 = (s32[4]{0:T(128)S(1)}, s32[4]{0:T(128)}, u32[]{:S(2)}) copy-start(s32[4]{0:T(128)} %blocks_ref.11) | copy-start | bytes 52
  27.8 6.8 %copy-start.10 = (s32[8]{0:T(128)S(1)}, s32[8]{0:T(128)}, u32[]{:S(2)}) copy-start(s32[8]{0:T(128)} %local_ref.7) | copy-start | bytes 100
  27.8 6.8 %copy-start.12 = (s32[8]{0:T(128)S(1)}, s32[8]{0:T(128)}, u32[]{:S(2)}) copy-start(s32[8]{0:T(128)} %hub_ref.7) | copy-start | bytes 100
  32.4 2.2 %copy-start.14 = (bf16[512,512]{1,0:T(8,128)(2,1)}, bf16[512,512]{1,0:T(8,128)(2,1)S(1)}, u32[]{:S(2)}) copy-start(bf16[512,512]{1,0:T(8,128)(2,1)S(1)} %collective-permute-done.3.outer_hbm) | copy-start | bytes 1572868
  33.1 1.5 %collective-permute-start.4 = (bf16[256,512]{1,0:T(8,128)(2,1)S(1)}, bf16[256,512]{1,0:T(8,128)(2,1)S(1)}, u32[]{:S(2)}, u32[]{:S(2)}) collective-permute-start(bf16[256,512]{1,0:T(8,128)(2,1)S(1)} %bitcast.5), channel_id=1, source_target_pairs={{0,1},{1,0},{2,3},{3,2},{4,5},{5,4},{6,7},{7,6},{8,9},{9,8},{10,11... | collective-permute-start | bytes 786440 | tf_op jit(solution)/shard_map/ppermute | solution.py:376
  39.2 7.8 %copy-start.15 = (bf16[512,512]{1,0:T(8,128)(2,1)S(1)}, bf16[512,512]{1,0:T(8,128)(2,1)}, u32[]{:S(2)}) copy-start(bf16[512,512]{1,0:T(8,128)(2,1)} %get-tuple-element.29.mine_hbm) | copy-start | bytes 1572868
  39.3 1.6 %collective-permute-start.5 = (bf16[256,512]{1,0:T(8,128)(2,1)S(1)}, bf16[256,512]{1,0:T(8,128)(2,1)S(1)}, u32[]{:S(2)}, u32[]{:S(2)}) collective-permute-start(bf16[256,512]{1,0:T(8,128)(2,1)S(1)} %get-tuple-element.28), channel_id=1, source_target_pairs={{0,1},{1,0},{2,3},{3,2},{4,5},{5,4},{6,7},{7,6},{8,9},{9,8},{10,11... | collective-permute-start | bytes 786440 | tf_op jit(solution)/shard_map/ppermute | solution.py:376
  39.4 8.4 %collective-permute-start.6 = (bf16[512,512]{1,0:T(8,128)(2,1)}, bf16[512,512]{1,0:T(8,128)(2,1)S(1)}, u32[]{:S(2)}, u32[]{:S(2)}) collective-permute-start(bf16[512,512]{1,0:T(8,128)(2,1)} %get-tuple-element.29.mine_hbm), channel_id=1, source_target_pairs={{0,1},{1,0},{2,3},{3,2},{4,5},{5,4},{6,7},{7,6},{8,9},{9,8},{10,11... | collective-permute-start | bytes 1572872 | tf_op jit(solution)/shard_map/ppermute | solution.py:376
  39.8 8.0 %collective-permute-start.7 = (bf16[512,512]{1,0:T(8,128)(2,1)}, bf16[512,512]{1,0:T(8,128)(2,1)S(1)}, u32[]{:S(2)}, u32[]{:S(2)}) collective-permute-start(bf16[512,512]{1,0:T(8,128)(2,1)} %get-tuple-element.30.back_hbm), channel_id=1, source_target_pairs={{0,1},{1,0},{2,3},{3,2},{4,5},{5,4},{6,7},{7,6},{8,9},{9,8},{10,11... | collective-permute-start | bytes 1572872 | tf_op jit(solution)/shard_map/ppermute | solution.py:376
  41.6 12.5 %all-to-all-start.2 = ((bf16[8,32,512]{2,1,0:T(8,128)(2,1)}), bf16[8,32,512]{2,1,0:T(8,128)(2,1)S(1)}, u32[]{:S(2)}, u32[]{:S(2)}) async-start(bf16[8,32,512]{2,1,0:T(8,128)(2,1)} %bitcast.3), calls=%async_computation.2 | async-start | bytes 524288 | tf_op jit(solution)/shard_map/all_to_all | solution.py:381
  47.1 18.0 %collective-permute-start.8 = (bf16[512,512]{1,0:T(8,128)(2,1)S(1)}, bf16[512,512]{1,0:T(8,128)(2,1)S(1)}, u32[]{:S(2)}, u32[]{:S(2)}) collective-permute-start(bf16[512,512]{1,0:T(8,128)(2,1)S(1)} %copy-done.15), channel_id=1, source_target_pairs={{1,2},{3,4},{5,6},{7,8},{9,10},{11,12},{13,14},{2,1},{4,3},{6,5},{... | collective-permute-start | bytes 1572872 | tf_op jit(solution)/shard_map/ppermute | solution.py:410
  47.8 12.7 %copy-start.2 = (bf16[512,512]{1,0:T(8,128)(2,1)}, bf16[512,512]{1,0:T(8,128)(2,1)S(1)}, u32[]{:S(2)}) copy-start(bf16[512,512]{1,0:T(8,128)(2,1)S(1)} %collective-permute-done.6.rest_0_.other_hbm) | copy-start | bytes 1572868
  47.8 12.7 %copy-start.4 = (bf16[512,512]{1,0:T(8,128)(2,1)}, bf16[512,512]{1,0:T(8,128)(2,1)S(1)}, u32[]{:S(2)}) copy-start(bf16[512,512]{1,0:T(8,128)(2,1)S(1)} %collective-permute-done.7.rest_1_.back_other_hbm) | copy-start | bytes 1572868
  55.5 10.2 %all-to-all-start.3 = ((bf16[8,32,512]{2,1,0:T(8,128)(2,1)}), bf16[8,32,512]{2,1,0:T(8,128)(2,1)S(1)}, u32[]{:S(2)}, u32[]{:S(2)}) async-start(bf16[8,32,512]{2,1,0:T(8,128)(2,1)} %merge.3), calls=%async_computation.3 | async-start | bytes 524288 | tf_op jit(solution)/shard_map/all_to_all | solution.py:381
  60.5 6.8 %copy-start.1 = (bf16[8,128,128]{2,1,0:T(8,128)(2,1)S(1)}, bf16[8,128,128]{2,1,0:T(8,128)(2,1)}, u32[]{:S(2)}) copy-start(bf16[8,128,128]{2,1,0:T(8,128)(2,1)} %lr_ref.3) | copy-start | bytes 786436
  60.5 6.8 %copy-start.9 = (s32[4]{0:T(128)S(1)}, s32[4]{0:T(128)}, u32[]{:S(2)}) copy-start(s32[4]{0:T(128)} %blocks_ref.11) | copy-start | bytes 52
  60.5 6.8 %copy-start.11 = (s32[8]{0:T(128)S(1)}, s32[8]{0:T(128)}, u32[]{:S(2)}) copy-start(s32[8]{0:T(128)} %local_ref.7) | copy-start | bytes 100
  60.5 6.8 %copy-start.13 = (s32[8]{0:T(128)S(1)}, s32[8]{0:T(128)}, u32[]{:S(2)}) copy-start(s32[8]{0:T(128)} %hub_ref.7) | copy-start | bytes 100
  65.7 1.5 %collective-permute-start.9 = (bf16[256,512]{1,0:T(8,128)(2,1)S(1)}, bf16[256,512]{1,0:T(8,128)(2,1)S(1)}, u32[]{:S(2)}, u32[]{:S(2)}) collective-permute-start(bf16[256,512]{1,0:T(8,128)(2,1)S(1)} %bitcast.7), channel_id=1, source_target_pairs={{0,1},{1,0},{2,3},{3,2},{4,5},{5,4},{6,7},{7,6},{8,9},{9,8},{10,11... | collective-permute-start | bytes 786440 | tf_op jit(solution)/shard_map/ppermute | solution.py:376
